TPU v7x, 32 devices: a whole 2x2x4 slice. The times are simulated.
32 devices in a mesh: dp: 8 (over z, x), tensor: 4 (over y, core).
Axes of the slice: x: 2, y: 2, z: 4, core: 2. Of those that a mesh axis runs over, the one named last changes fastest.
Arguments:
- tokens: bfloat16 [12608, 768], P(('dp', 'tensor')), may hold values from -6 to 6
- teacher: bfloat16 [12608, 768], P(('dp', 'tensor')), may hold values from -6 to 6
- valid_mask: int32 [64, 197], P('dp'), may hold values from 0 to 1, as said below
- expert_ids: int32 [12608, 2], P(('dp', 'tensor')), may hold values from 0 to 7, all different within a row; in each aligned block of 394 rows (0 to 393, 394 to 787, ...) at most 123 rows name the same one
- attn_gain: bfloat16 [768], P('dp'), may hold values from 0.5 to 1.5
- attn_shift: bfloat16 [768], P('dp'), may hold values from -1.5 to 1.5
- qkv_weight: bfloat16 [768, 3, 768], P('dp', None, 'tensor'), may hold values from -0.21875 to 0.21875
- proj_weight: bfloat16 [768, 768], P('dp', 'tensor'), may hold values from -1.5 to 1.5
- moe_gain: bfloat16 [768], P('dp'), may hold values from 0.5 to 1.5
- moe_shift: bfloat16 [768], P('dp'), may hold values from -1.5 to 1.5
- router_weight: bfloat16 [768, 8], P('dp'), may hold values from -0.15625 to 0.15625
- up_weight: bfloat16 [8, 768, 3072], P('dp', None, 'tensor'), may hold values from -0.21875 to 0.21875
- down_weight: bfloat16 [8, 768, 3072], P('dp', None, 'tensor'), may hold values from -0.625 to 0.625
Outputs:
- loss_value: float32 [], replicated
- output: bfloat16 [12608, 768], P(('dp', 'tensor'))
- grad_tokens: float32 [12608, 768], P(('dp', 'tensor'))
- grad_attn_gain: float32 [768], P('dp')
- grad_attn_shift: float32 [768], P('dp')
- grad_qkv_weight: float32 [768, 3, 768], P('dp', None, 'tensor')
- grad_proj_weight: float32 [768, 768], P('dp', 'tensor')
- grad_moe_gain: float32 [768], P('dp')
- grad_moe_shift: float32 [768], P('dp')
- grad_router_weight: float32 [768, 8], P('dp')
- grad_up_weight: float32 [8, 768, 3072], P('dp', None, 'tensor')
- grad_down_weight: float32 [8, 768, 3072], P('dp', None, 'tensor')
Inputs may be any that keep to these rules, and one draw needn't show every extreme that they name: `valid_mask`: position 0 of every image is 1. `expert_ids`: each row names 2 different experts; among the 394 rows of one device (aligned blocks) no expert is named more than 123 times, a bound that some block reaches.
All inputs are finite; a program needn't handle non-finite values.
Results may differ from a plain program's by a relative error of at most 0.0085.
Values may be sent and summed in bfloat16 or wider, within the bound.
No kernel may reach another device: no remote copies, remote signals or barrier semaphores. Data moves between devices by JAX's collectives and lax.ppermute only.
A program may use at most 192 MiB of HBM per device.

v0:
```python
import jax
import jax.numpy as jnp
from jax import lax
from jax.sharding import PartitionSpec as P

HD = 64


EPSILON = 1e-06
MASKED = -1000000000.0


def layer_norm(values, norm_gain, norm_shift):
    center = values - jnp.mean(values, axis=-1, keepdims=True)
    spread = jnp.mean(center * center, axis=-1, keepdims=True)
    return center * lax.rsqrt(spread + EPSILON) * norm_gain + norm_shift


def gelu_exact(values):
    return jax.nn.gelu(values, approximate=False)


def contract_last(operand, weights):
    return lax.dot_general(
        operand, weights, (((1,), (1,)), ((), ())), preferred_element_type=jnp.float32
    )


def contract_first(operand, weights):
    return lax.dot_general(
        operand, weights, (((0,), (0,)), ((), ())), preferred_element_type=jnp.float32
    )


def group_rows(values):
    return lax.all_gather(values, "tensor", axis=0, tiled=True)


def row_sums(operand, weights):
    return lax.psum_scatter(
        contract_last(operand, weights), "tensor", scatter_dimension=0, tiled=True
    )


def slot_gather(values):
    return lax.all_gather(values, "tensor", axis=0, tiled=True)


def slot_sums(operand, weights):
    return lax.psum_scatter(
        contract_last(operand, weights), "tensor", scatter_dimension=0, tiled=True
    )


def to_experts(buffer):
    return lax.all_to_all(buffer, "dp", split_axis=0, concat_axis=0, tiled=True)


def from_experts(buffer):
    return lax.all_to_all(buffer, "dp", split_axis=0, concat_axis=0, tiled=True)


def slot_table(expert_ids, experts):
    flat_ids = expert_ids.reshape(-1)
    onehot = (flat_ids[:, None] == lax.iota(jnp.int32, experts)[None, :]).astype(jnp.int32)
    earlier = jnp.cumsum(onehot, axis=0) - onehot
    return (flat_ids, jnp.sum(earlier * onehot, axis=1))


def local(
    tokens,
    teacher,
    valid_mask,
    expert_ids,
    attn_gain,
    attn_shift,
    qkv_weight,
    proj_weight,
    moe_gain,
    moe_shift,
    router_weight,
    up_weight,
    down_weight,
):
    local_rows, model_width = tokens.shape
    images, image_len = valid_mask.shape
    experts = router_weight.shape[1]
    top_count = expert_ids.shape[1]
    capacity = max(2, (top_count * local_rows + experts - 1) // experts * 5 // 4)
    tensor_count = lax.axis_size("tensor")
    gathered = (
        lax.all_gather(attn_gain, "dp", axis=0, tiled=True),
        lax.all_gather(attn_shift, "dp", axis=0, tiled=True),
        lax.all_gather(moe_gain, "dp", axis=0, tiled=True),
        lax.all_gather(moe_shift, "dp", axis=0, tiled=True),
        lax.all_gather(qkv_weight, "dp", axis=0, tiled=True),
        lax.all_gather(proj_weight, "dp", axis=0, tiled=True),
        lax.all_gather(router_weight, "dp", axis=0, tiled=True),
    )
    gain_one = gathered[0].astype(jnp.float32)
    shift_one = gathered[1].astype(jnp.float32)
    gain_two = gathered[2].astype(jnp.float32)
    shift_two = gathered[3].astype(jnp.float32)
    qkv_full = gathered[4]
    proj_full = gathered[5]
    router_full = gathered[6]
    token_values = tokens.astype(jnp.float32)
    normed = layer_norm(token_values, gain_one, shift_one).astype(jnp.bfloat16)
    normed_all = group_rows(normed)
    qkv_flat = qkv_full.reshape(model_width, -1)
    qkv_act = jnp.dot(normed_all, qkv_flat, preferred_element_type=jnp.float32).astype(jnp.bfloat16)
    heads_local = qkv_flat.shape[1] // (3 * HD)
    qkv_parts = qkv_act.reshape(images, image_len, 3, heads_local, HD)
    queries = qkv_parts[:, :, 0]
    keys_all = qkv_parts[:, :, 1]
    values_all = qkv_parts[:, :, 2]
    score_scale = HD ** (-0.5)
    key_valid = (valid_mask > 0)[:, None, None, :]
    scores = (
        jnp.einsum("bqhe,bkhe->bhqk", queries, keys_all, preferred_element_type=jnp.float32)
        * score_scale
    )
    scores = jnp.where(key_valid, scores, MASKED)
    log_total = jax.nn.logsumexp(scores, axis=-1, keepdims=True)
    attn_probs = jnp.exp(scores - log_total)
    probs_low = attn_probs.astype(jnp.bfloat16)
    context = jnp.einsum(
        "bhqk,bkhe->bqhe", probs_low, values_all, preferred_element_type=jnp.float32
    )
    context_low = context.astype(jnp.bfloat16).reshape(images * image_len, heads_local * HD)
    attn_out = row_sums(context_low, proj_full)
    residual = token_values + attn_out
    hidden_in = layer_norm(residual, gain_two, shift_two).astype(jnp.bfloat16)
    logits = jnp.dot(hidden_in, router_full, preferred_element_type=jnp.float32)
    router_probs = jax.nn.softmax(logits, axis=-1)
    choose = (expert_ids[:, :, None] == lax.iota(jnp.int32, experts)[None, None, :]).astype(
        jnp.float32
    )
    gate_values = jnp.sum(choose * router_probs[:, None, :], axis=-1)
    flat_ids, slot_index = slot_table(expert_ids, experts)
    copies = jnp.repeat(hidden_in, top_count, axis=0)
    empty_slots = jnp.zeros((experts, capacity, model_width), jnp.bfloat16)
    arrived = to_experts(empty_slots.at[flat_ids, slot_index].set(copies))
    expert_rows = arrived.reshape(-1, model_width)
    rows_all = slot_gather(expert_rows)
    up_values = jnp.dot(rows_all, up_weight[0], preferred_element_type=jnp.float32)
    hidden_low = gelu_exact(up_values).astype(jnp.bfloat16)
    expert_out = slot_sums(hidden_low, down_weight[0])
    returned = from_experts(expert_out.astype(jnp.bfloat16).reshape(experts, capacity, model_width))
    picked = (
        returned[flat_ids, slot_index]
        .astype(jnp.float32)
        .reshape(local_rows, top_count, model_width)
    )
    moe_out = jnp.sum(gate_values[:, :, None] * picked, axis=1)
    result = residual + moe_out
    flat_mask = valid_mask.reshape(-1)
    own_mask = lax.dynamic_slice_in_dim(
        flat_mask, lax.axis_index("tensor") * local_rows, local_rows
    ).astype(jnp.float32)
    errors = result - teacher.astype(jnp.float32)
    row_loss = jnp.mean(errors * errors, axis=-1)
    loss_sum, valid_count = lax.psum(
        (jnp.sum(own_mask * row_loss), jnp.sum(own_mask)), ("dp", "tensor")
    )
    loss_value = loss_sum / valid_count
    token_total = local_rows * lax.axis_size("dp") * tensor_count
    grad_result = own_mask[:, None] * errors * (token_total / valid_count)
    grad_gates = jnp.sum(grad_result[:, None, :] * picked, axis=-1)
    grad_picked = (
        (gate_values[:, :, None] * grad_result[:, None, :])
        .astype(jnp.bfloat16)
        .reshape(-1, model_width)
    )
    grad_arrived = to_experts(empty_slots.at[flat_ids, slot_index].set(grad_picked))
    grad_expert = grad_arrived.reshape(-1, model_width)
    grad_all = slot_gather(grad_expert)
    grad_hidden = jnp.dot(grad_all, down_weight[0], preferred_element_type=jnp.float32)
    grad_down_part = contract_first(grad_all, hidden_low)[None]
    gelu_value, gelu_back = jax.vjp(gelu_exact, up_values)
    grad_up_values = gelu_back(grad_hidden)[0].astype(jnp.bfloat16)
    grad_up_part = contract_first(rows_all, grad_up_values)[None]
    grad_rows = slot_sums(grad_up_values, up_weight[0]).astype(jnp.bfloat16)
    grad_back = from_experts(grad_rows.reshape(experts, capacity, model_width))
    grad_copies = (
        grad_back[flat_ids, slot_index]
        .astype(jnp.float32)
        .reshape(local_rows, top_count, model_width)
    )
    grad_probs = jnp.sum(choose * grad_gates[:, :, None], axis=1)
    grad_logits = router_probs * (
        grad_probs - jnp.sum(router_probs * grad_probs, axis=-1, keepdims=True)
    )
    grad_logits_low = grad_logits.astype(jnp.bfloat16)
    grad_hidden_in = jnp.sum(grad_copies, axis=1) + contract_last(grad_logits_low, router_full)
    grad_router = contract_first(hidden_in, grad_logits_low)
    norm_value, norm_back = jax.vjp(layer_norm, residual, gain_two, shift_two)
    grad_mixed_norm, grad_gain_two, grad_shift_two = norm_back(grad_hidden_in)
    grad_residual = grad_result + grad_mixed_norm
    grad_attn_all = group_rows(grad_residual.astype(jnp.bfloat16))
    grad_context = jnp.dot(grad_attn_all, proj_full, preferred_element_type=jnp.float32).astype(
        jnp.bfloat16
    )
    grad_proj = contract_first(grad_attn_all, context_low)
    grad_context_heads = grad_context.reshape(images, image_len, heads_local, HD)
    grad_values = jnp.einsum(
        "bhqk,bqhe->bkhe", probs_low, grad_context_heads, preferred_element_type=jnp.float32
    )
    grad_pr = jnp.einsum(
        "bqhe,bkhe->bhqk", grad_context_heads, values_all, preferred_element_type=jnp.float32
    )
    row_delta = jnp.sum(attn_probs * grad_pr, axis=-1, keepdims=True)
    grad_scores = (attn_probs * (grad_pr - row_delta)).astype(jnp.bfloat16)
    grad_queries = (
        jnp.einsum("bhqk,bkhe->bqhe", grad_scores, keys_all, preferred_element_type=jnp.float32)
        * score_scale
    )
    grad_keys = (
        jnp.einsum("bhqk,bqhe->bkhe", grad_scores, queries, preferred_element_type=jnp.float32)
        * score_scale
    )
    grad_qkv = jnp.stack([grad_queries, grad_keys, grad_values], axis=2).astype(jnp.bfloat16)
    grad_qkv = grad_qkv.reshape(images * image_len, -1)
    grad_qkv_full = contract_first(normed_all, grad_qkv).reshape(qkv_full.shape)
    grad_normed = row_sums(grad_qkv, qkv_flat)
    first_value, first_back = jax.vjp(layer_norm, token_values, gain_one, shift_one)
    grad_tokens_norm, grad_gain_one, grad_shift_one = first_back(grad_normed)
    grad_tokens = grad_residual + grad_tokens_norm
    summed = (
        lax.psum_scatter(grad_gain_one, "dp", scatter_dimension=0, tiled=True),
        lax.psum_scatter(grad_shift_one, "dp", scatter_dimension=0, tiled=True),
        lax.psum_scatter(grad_gain_two, "dp", scatter_dimension=0, tiled=True),
        lax.psum_scatter(grad_shift_two, "dp", scatter_dimension=0, tiled=True),
        lax.psum_scatter(grad_router, "dp", scatter_dimension=0, tiled=True),
        lax.psum_scatter(grad_qkv_full, "dp", scatter_dimension=0, tiled=True),
        lax.psum_scatter(grad_proj, "dp", scatter_dimension=0, tiled=True),
    )
    shared = lax.psum((summed[0], summed[1], summed[2], summed[3], summed[4]), "tensor")
    return (
        loss_value,
        result.astype(jnp.bfloat16),
        grad_tokens,
        shared[0],
        shared[1],
        summed[5],
        summed[6],
        shared[2],
        shared[3],
        shared[4],
        grad_up_part,
        grad_down_part,
    )


def solution(mesh):
    in_specs = (
        P(("dp", "tensor"), None),
        P(("dp", "tensor"), None),
        P("dp", None),
        P(("dp", "tensor"), None),
        P("dp"),
        P("dp"),
        P("dp", None, "tensor"),
        P("dp", "tensor"),
        P("dp"),
        P("dp"),
        P("dp", None),
        P("dp", None, "tensor"),
        P("dp", None, "tensor"),
    )
    out_specs = (
        P(),
        P(("dp", "tensor"), None),
        P(("dp", "tensor"), None),
        P("dp"),
        P("dp"),
        P("dp", None, "tensor"),
        P("dp", "tensor"),
        P("dp"),
        P("dp"),
        P("dp", None),
        P("dp", None, "tensor"),
        P("dp", None, "tensor"),
    )
    return jax.shard_map(local, mesh=mesh, in_specs=in_specs, out_specs=out_specs, check_vma=False)
```

profile of v0, /device:TPU:0, one launch (start us, length us, event | category | flops | bytes accessed | tf_op | source)
XLA Modules:
  0.0 1235.8 jit_solution(4999663334242218778)
XLA Ops:
  12.6 23.9 %all-reduce.15 = (bf16[768]{0:T(1024)(128)(2,1)S(1)}, bf16[768]{0:T(1024)(128)(2,1)S(1)}, bf16[768]{0:T(1024)(128)(2,1)}, bf16[768]{0:T(1024)(128)(2,1)}) all-reduce(bf16[768]{0:T(1024)(128)(2,1)S(1)} %dynamic-update-slice.1, bf16[768]{0:T(1024)(128)(2,1)S(1)} %dynamic-update-slice, ...), channel_id=1, replica_groups=mesh['dp'=8,'tensor'=4] {'dp'}, use_global_device_ids=true, to_apply=%add.2 | all-reduce | flops 3072 | bytes 12288
  43.3 35.6 %all_gather.36 = bf16[768,3,192]{2,1,0:T(4,128)(2,1)S(1)} all-gather(bf16[96,3,192]{2,1,0:T(4,128)(2,1)S(1)} %copy.111), channel_id=1, replica_groups=mesh['dp'=8,'tensor'=4] {'dp'}, dimensions={0}, use_global_device_ids=true | all-gather | bytes 995328 | tf_op jit(solution)/shard_map/all_gather | solution.py:96
  84.1 33.1 %all_gather.37 = bf16[768,192]{1,0:T(8,128)(2,1)} all-gather(bf16[96,192]{1,0:T(8,128)(2,1)S(1)} %copy-done.43), channel_id=1, replica_groups=mesh['dp'=8,'tensor'=4] {'dp'}, dimensions={0}, use_global_device_ids=true | all-gather | bytes 331776 | tf_op jit(solution)/shard_map/all_gather | solution.py:97
  117.2 3.8 reshape.288
  121.1 4.7 convolution_convert_fusion
  125.8 4.8 reshape.237
  138.6 3.0 fusion.60
  141.7 45.9 %fusion = f32[400,768]{1,0:T(8,128)S(1)} fusion(f32[1576,768]{1,0:T(8,128)} %fusion.60), kind=kCustom, calls=%all-reduce-scatter | all-reduce-scatter fusion | flops 1228801 | bytes 6070784
  190.6 4.3 concatenate.15
  200.0 74.9 %scatter_fusion = bf16[8,123,768]{2,0,1:T(8,128)(2,1)S(1)} fusion(bf16[8,123,768]{2,0,1:T(8,128)(2,1)S(1)} %broadcast_in_dim.33.clone, s32[788]{0:T(1024)S(1)} %get-tuple-element.20, bf16[788,768]{1,0:T(8,128)(2,1)} %reshape.265), kind=kCustom, calls=%fused_computation.2 | custom fusion | bytes 3637408 | tf_op jit(solution)/shard_map/scatter | solution.py:143
  275.2 41.0 %all_to_all.20 = bf16[8,123,768]{2,1,0:T(8,128)(2,1)} all-to-all(bf16[8,123,768]{2,1,0:T(8,128)(2,1)S(1)} %copy.124), channel_id=1, replica_groups=mesh['dp'=8,'tensor'=4] {'dp'}, dimensions={0} | all-to-all | bytes 3022848 | tf_op jit(solution)/shard_map/all_to_all | solution.py:56
  316.2 3.0 reshape.243
  319.3 44.3 %all-gather.8.cloned.1.call-done = bf16[3936,768]{1,0:T(8,128)(2,1)} async-done(((bf16[984,768]{1,0:T(8,128)(2,1)}), bf16[3936,768]{1,0:T(8,128)(2,1)}) %all-gather.8.cloned.1.call-update) | async-done | bytes 6045712 | tf_op jit(solution)/shard_map/all_gather | solution.py:46
  363.6 32.7 %multiply_convert_fusion = (bf16[3936,768]{1,0:T(8,128)(2,1)S(1)}, f32[3936,768]{1,0:T(8,128)}, f32[3936,768]{1,0:T(8,128)}) fusion(bf16[3936,768]{1,0:T(8,128)(2,1)} %all-gather.8.cloned.1.call-done, bf16[1,768,768]{2,1,0:T(8,128)(2,1)S(1)} %copy-done), kind=kOutput, calls=%fused_computation.7 | convolution fusion | flops 4839579648 | bytes 37453824 | tf_op jit(solution)/shard_map/dot_general | solution.py:146
  396.3 2.6 copy-done.70
  399.0 7.8 fusion.24
  406.8 96.0 %reduce-scatter.12.cloned.1.call-done = f32[984,768]{1,0:T(8,128)} async-done(((f32[3936,768]{1,0:T(8,128)}), f32[984,768]{1,0:T(8,128)}) %reduce-scatter.12.cloned.1.call-update) | async-done | bytes 3022864 | tf_op jit(solution)/shard_map/reduce_scatter | solution.py:50
  506.4 5.5 all-to-all-start.1
  513.3 55.6 %psum.50 = f32[]{:T(128)} all-reduce(f32[]{:T(128)} %get-tuple-element.38), channel_id=1, replica_groups=mesh['dp'=8,'tensor'=4] {'dp','tensor'}, use_global_device_ids=true, to_apply=%region_20.21 | all-reduce | flops 1 | bytes 8 | tf_op jit(solution)/shard_map/psum | solution.py:163
  568.9 26.4 %all-gather.1 = bf16[8,96,8]{1,2,0:T(8,128)(2,1)S(1)} all-gather(bf16[1,96,8]{1,2,0:T(8,128)(2,1)S(1)} %bitcast.124), channel_id=1, replica_groups=mesh['dp'=8,'tensor'=4] {'dp'}, dimensions={0}, use_global_device_ids=true | all-gather | bytes 13824 | tf_op jit(solution)/shard_map/all_gather | solution.py:98
  597.8 2.2 copy.125
  600.1 14.2 %gather_fusion = bf16[788,768]{1,0:T(8,128)(2,1)} fusion(bf16[8,123,768]{2,0,1:T(8,128)(2,1)S(1)} %copy.125, s32[788]{0:T(1024)S(1)} %get-tuple-element.19), kind=kCustom, calls=%fused_computation | custom fusion | bytes 2427040 | tf_op jit(solution)/shard_map/gather | solution.py:151
  614.2 3.8 reshape.249
  618.0 4.8 multiply_reduce_fusion.2
  625.0 2.2 mul.285
  627.2 4.2 mul.286
  631.4 2.9 multiply_convert_fusion.2
  634.4 74.9 %scatter_fusion.1 = bf16[8,123,768]{2,0,1:T(8,128)(2,1)S(1)} fusion(bf16[8,123,768]{2,0,1:T(8,128)(2,1)S(1)} %broadcast_in_dim.33, s32[788]{0:T(1024)S(1)} %get-tuple-element.20, bf16[788,768]{1,0:T(8,128)(2,1)} %multiply_convert_fusion.2), kind=kCustom, calls=%fused_computation.3 | custom fusion | bytes 3637408 | tf_op jit(solution)/shard_map/scatter | solution.py:175
  709.6 35.4 %all_to_all.21 = bf16[8,123,768]{2,1,0:T(8,128)(2,1)} all-to-all(bf16[8,123,768]{2,1,0:T(8,128)(2,1)S(1)} %copy.127), channel_id=1, replica_groups=mesh['dp'=8,'tensor'=4] {'dp'}, dimensions={0} | all-to-all | bytes 3022848 | tf_op jit(solution)/shard_map/all_to_all | solution.py:56
  745.0 3.1 reshape.245
  748.2 43.9 %all-gather.10.cloned.1.call-done = bf16[3936,768]{1,0:T(8,128)(2,1)} async-done(((bf16[984,768]{1,0:T(8,128)(2,1)}), bf16[3936,768]{1,0:T(8,128)(2,1)}) %all-gather.10.cloned.1.call-update) | async-done | bytes 6045712 | tf_op jit(solution)/shard_map/all_gather | solution.py:46
  792.1 13.8 %add_convert_fusion = bf16[3936,768]{1,0:T(8,128)(2,1)S(1)} fusion(f32[3936,768]{1,0:T(8,128)} %get-tuple-element.37, f32[3936,768]{1,0:T(8,128)} %get-tuple-element.50, bf16[3936,768]{1,0:T(8,128)(2,1)} %all-gather.10.cloned.1.call-done, bf16[1,768,768]{2,1,0:T(8,128)(2,1)S(1)} %copy-done.69), kind=kOutput, calls=%fused_computation.6 | convolution fusion | flops 4685414400 | bytes 37453824 | tf_op jit(solution)/shard_map/dot_general | solution.py:178
  805.8 2.5 copy-done.71
  808.4 7.8 fusion.28
  816.2 96.0 %reduce-scatter.14.cloned.1.call-done = f32[984,768]{1,0:T(8,128)} async-done(((f32[3936,768]{1,0:T(8,128)}), f32[984,768]{1,0:T(8,128)}) %reduce-scatter.14.cloned.1.call-update) | async-done | bytes 3022864 | tf_op jit(solution)/shard_map/reduce_scatter | solution.py:50
  912.2 3.1 convert_element_type.128
  915.4 3.1 reshape.246
  918.4 5.5 all-to-all-start.3
  924.0 3.1 multiply_reduce_fusion.1
  928.5 35.2 %all-to-all-done.3 = bf16[8,123,768]{2,1,0:T(8,128)(2,1)} async-done(((bf16[8,123,768]{2,1,0:T(8,128)(2,1)}), bf16[8,123,768]{2,1,0:T(8,128)(2,1)}, u32[]{:S(2)}, u32[]{:S(2)}) %all-to-all-start.3) | async-done | bytes 1511456 | tf_op jit(solution)/shard_map/all_to_all | solution.py:60
  963.7 2.3 copy.128
  966.0 14.4 %gather_fusion.1 = bf16[788,768]{1,0:T(8,128)(2,1)} fusion(bf16[8,123,768]{2,0,1:T(8,128)(2,1)S(1)} %copy.128, s32[788]{0:T(1024)S(1)} %get-tuple-element.19), kind=kCustom, calls=%fused_computation.1 | custom fusion | bytes 2427040 | tf_op jit(solution)/shard_map/gather | solution.py:186
  980.3 3.8 reshape.250
  984.2 5.7 reduce_sum.245
  989.9 3.3 multiply_reduce_fusion.3
  996.5 3.7 reshape.301
  1001.7 10.3 convolution_bitcast_fusion
  1012.6 12.9 %all-gather.14.cloned.1.call-done = bf16[4,394,768]{2,1,0:T(8,128)(2,1)} async-done(((bf16[1,394,768]{2,1,0:T(8,128)(2,1)}), bf16[4,394,768]{2,1,0:T(8,128)(2,1)}) %all-gather.14.cloned.1.call-update) | async-done | bytes 2420752 | tf_op jit(solution)/shard_map/all_gather | solution.py:36
  1025.5 3.8 reshape.292
  1029.3 3.6 convolution_convert_fusion.1
  1032.9 3.1 reshape.247
  1036.0 7.0 multiply_reduce_fusion
  1046.7 4.7 multiply_convert_fusion.1
  1054.0 2.6 multiply_bitcast_fusion
  1058.6 3.4 convert_element_type.136
  1062.0 6.2 fusion.61
  1068.1 3.9 fusion.62
  1072.0 46.0 %fusion.1 = f32[400,768]{1,0:T(8,128)S(1)} fusion(f32[1576,768]{1,0:T(8,128)} %fusion.61), kind=kCustom, calls=%all-reduce-scatter.1 | all-reduce-scatter fusion | flops 1228801 | bytes 6070784
  1119.3 9.9 convolution_bitcast_fusion.1
  1129.3 41.8 %psum.49 = f32[]{:T(128)} all-reduce(f32[]{:T(128)} %multiply_reduce_fusion.8), channel_id=1, replica_groups=mesh['dp'=8,'tensor'=4] {'dp','tensor'}, use_global_device_ids=true, to_apply=%region_18.19 | all-reduce | flops 1 | bytes 8 | tf_op jit(solution)/shard_map/psum | solution.py:163
  1172.5 4.3 concatenate.16
  1180.7 36.9 %all-reduce.13 = (f32[768]{0:T(1024)S(1)}, f32[768]{0:T(1024)S(1)}, f32[768]{0:T(1024)S(1)}, f32[768]{0:T(1024)S(1)}) all-reduce(f32[768]{0:T(1024)S(1)} %get-tuple-element.14, f32[768]{0:T(1024)S(1)} %get-tuple-element.16, f32[768]{0:T(1024)S(1)} %get-tuple-element.12, ...), channel_id=6, replica_groups=mesh['dp'=8,'tensor'=4] {'dp'}, use_global_device_ids=true, to_apply=%region_34.35.clone | all-reduce | flops 3072 | bytes 24576
  1217.9 6.6 all-reduce.14
  1224.5 3.3 add_add_fusion.2
  (267 shorter events, 61.6 us)
Async XLA Ops:
  7.2 356.4 %copy-start = (bf16[1,768,768]{2,1,0:T(8,128)(2,1)S(1)}, bf16[1,768,768]{2,1,0:T(8,128)(2,1)}, u32[]{:S(2)}) copy-start(bf16[1,768,768]{2,1,0:T(8,128)(2,1)} %param.24) | copy-start | bytes 3538948
  7.2 34.9 %copy-start.44 = (s32[394,2]{0,1:T(2,128)S(1)}, s32[394,2]{0,1:T(2,128)}, u32[]{:S(2)}) copy-start(s32[394,2]{0,1:T(2,128)} %param.16) | copy-start | bytes 9460
  7.2 35.9 %copy-start.34 = (bf16[96,3,192]{2,0,1:T(8,128)(2,1)S(1)}, bf16[96,3,192]{2,0,1:T(8,128)(2,1)}, u32[]{:S(2)}) copy-start(bf16[96,3,192]{2,0,1:T(8,128)(2,1)} %param.19) | copy-start | bytes 331780
  7.2 110.0 %all-gather.12.cloned.1.call-start = ((), (), s32[]{:S(2)}) async-start(), calls=%async_computation.15 | async-start | bytes 3072000 | tf_op jit(solution)/shard_map/all_gather | solution.py:36
  36.6 3.3 copy-start.35
  39.8 3.3 copy-start.45
  42.0 321.6 %all-gather.8.cloned.1.call-start = ((), (), s32[]{:S(2)}) async-start(), calls=%async_computation.9 | async-start | bytes 7557120 | tf_op jit(solution)/shard_map/all_gather | solution.py:46
  43.1 41.0 %copy-start.43 = (bf16[96,192]{1,0:T(8,128)(2,1)S(1)}, bf16[96,192]{1,0:T(8,128)(2,1)}, u32[]{:S(2)}) copy-start(bf16[96,192]{1,0:T(8,128)(2,1)} %param.20) | copy-start | bytes 110596
  43.3 73.9 %copy-start.53 = (s32[8,197]{1,0:T(8,128)S(1)}, s32[8,197]{1,0:T(8,128)}, u32[]{:S(2)}) copy-start(s32[8,197]{1,0:T(8,128)} %param.15) | copy-start | bytes 18916
  117.2 16.8 %copy-start.47 = (pred[8,197]{1,0:T(8,128)(4,1)}, pred[8,197]{1,0:T(8,128)(4,1)S(1)}, u32[]{:S(2)}) copy-start(pred[8,197]{1,0:T(8,128)(4,1)S(1)} %broadcast_compare_fusion) | copy-start | bytes 4732
  117.2 3.9 copy-start.30
  130.8 3.2 copy-start.19
  141.7 47.6 %copy-start.61 = (s32[788]{0:T(1024)S(1)}, s32[788]{0:T(1024)}, u32[]{:S(2)}) copy-start(s32[788]{0:T(1024)} %fusion.40) | copy-start | bytes 9460
  141.7 47.6 %copy-start.63 = (s32[788,1]{0,1:T(1,128)S(1)}, s32[788,1]{0,1:T(1,128)}, u32[]{:S(2)}) copy-start(s32[788,1]{0,1:T(1,128)} %reshape.239) | copy-start | bytes 9460
  141.7 47.6 %copy-start.67 = (u32[32]{0:T(128)S(1)}, u32[32]{0:T(128)}, u32[]{:S(2)}) copy-start(u32[32]{0:T(128)} %constant.208) | copy-start | bytes 388
  141.7 48.2 %copy-start.66 = (bf16[768]{0:T(1024)(128)(2,1)S(1)}, bf16[768]{0:T(1024)(128)(2,1)}, u32[]{:S(2)}) copy-start(bf16[768]{0:T(1024)(128)(2,1)} %get-tuple-element.33) | copy-start | bytes 4612
  141.7 48.2 %copy-start.65 = (bf16[768]{0:T(1024)(128)(2,1)S(1)}, bf16[768]{0:T(1024)(128)(2,1)}, u32[]{:S(2)}) copy-start(bf16[768]{0:T(1024)(128)(2,1)} %get-tuple-element.32) | copy-start | bytes 4612
  187.6 7.3 copy-start.9
  187.6 3.0 collective-permute-start
  189.9 6.9 copy-start.39
  319.2 79.7 %copy-start.68 = (bf16[1,768,768]{2,1,0:T(8,128)(2,1)S(1)}, bf16[1,768,768]{2,1,0:T(8,128)(2,1)}, u32[]{:S(2)}) copy-start(bf16[1,768,768]{2,1,0:T(8,128)(2,1)} %param.25) | copy-start | bytes 3538948
  319.2 183.5 %reduce-scatter.12.cloned.1.call-start = ((), (), s32[]{:S(2)}) async-start(), calls=%async_computation.10 | async-start | bytes 15114240 | tf_op jit(solution)/shard_map/reduce_scatter | solution.py:50
  504.8 64.1 %copy-start.64 = (bf16[96,8]{0,1:T(8,128)(2,1)S(1)}, bf16[96,8]{0,1:T(8,128)(2,1)}, u32[]{:S(2)}) copy-start(bf16[96,8]{0,1:T(8,128)(2,1)} %param.23) | copy-start | bytes 4612
  506.4 91.4 %all-to-all-start.1 = ((bf16[8,123,768]{2,1,0:T(8,128)(2,1)}), bf16[8,123,768]{2,1,0:T(8,128)(2,1)}, u32[]{:S(2)}, u32[]{:S(2)}) async-start(bf16[8,123,768]{2,1,0:T(8,128)(2,1)} %reshape.244), calls=%async_computation.2 | async-start | bytes 3145728 | tf_op jit(solution)/shard_map/all_to_all | solution.py:60
  511.9 280.2 %all-gather.10.cloned.1.call-start = ((), (), s32[]{:S(2)}) async-start(), calls=%async_computation.11 | async-start | bytes 7557120 | tf_op jit(solution)/shard_map/all_gather | solution.py:46
  618.0 4.8 copy-start.3
  618.0 4.8 copy-start.26
  618.0 4.8 copy-start.58
  627.2 4.2 copy-start.60
  745.0 47.0 %copy-start.69 = (bf16[1,768,768]{2,1,0:T(8,128)(2,1)S(1)}, bf16[1,768,768]{2,1,0:T(8,128)(2,1)}, u32[]{:S(2)}) copy-start(bf16[1,768,768]{2,1,0:T(8,128)(2,1)} %param.25) | copy-start | bytes 3538948
  748.1 164.1 %reduce-scatter.14.cloned.1.call-start = ((), (), s32[]{:S(2)}) async-start(), calls=%async_computation.12 | async-start | bytes 15114240 | tf_op jit(solution)/shard_map/reduce_scatter | solution.py:50
  915.4 8.7 copy-start.6
  918.4 45.2 %all-to-all-start.3 = ((bf16[8,123,768]{2,1,0:T(8,128)(2,1)}), bf16[8,123,768]{2,1,0:T(8,128)(2,1)}, u32[]{:S(2)}, u32[]{:S(2)}) async-start(bf16[8,123,768]{2,1,0:T(8,128)(2,1)} %reshape.246), calls=%async_computation.5 | async-start | bytes 3145728 | tf_op jit(solution)/shard_map/all_to_all | solution.py:60
  924.0 3.3 copy-start.52
  924.0 76.3 %reduce-scatter.20.cloned.1.call-start = ((), (), s32[]{:S(2)}) async-start(), calls=%async_computation.17 | async-start | bytes 442368
  928.5 97.0 %all-gather.14.cloned.1.call-start = ((), (), s32[]{:S(2)}) async-start(), calls=%async_computation.16 | async-start | bytes 3072000 | tf_op jit(solution)/shard_map/all_gather | solution.py:36
  984.1 5.7 copy-start.4
  984.2 5.7 copy-start.27
  984.2 5.7 copy-start.40
  984.2 5.7 copy-start.42
  984.2 5.7 copy-start.50
  989.9 3.3 copy-start.57
  995.8 232.1 %reduce-scatter.18.cloned.1.call-start = ((), (), s32[]{:S(2)}) async-start(), calls=%async_computation.14 | async-start | bytes 884736 | tf_op jit(solution)/shard_map/reduce_scatter | solution.py:236
  1001.7 10.3 copy-start.59
  1012.6 16.6 %copy-start.18 = (bf16[768,192]{1,0:T(8,128)(2,1)S(1)}, bf16[768,192]{1,0:T(8,128)(2,1)}, u32[]{:S(2)}) copy-start(bf16[768,192]{1,0:T(8,128)(2,1)} %all_gather.37) | copy-start | bytes 884740
  1029.3 6.7 copy-start.20
  1029.3 6.7 copy-start.32
  1029.3 6.7 copy-start.48
  1029.3 13.7 %slice-start = ((s8[4915200]{0:T(1024)(128)(4,1)}), s8[720896]{0:T(1024)(128)(4,1)S(1)}, s32[]{:S(2)}) async-start(s8[4915200]{0:T(1024)(128)(4,1)} %bitcast.117), calls=%async_computation.18 | async-start | bytes 1441792
  1036.0 7.1 slice-start.1
  1036.0 7.0 copy-start.21
  1036.0 7.0 copy-start.33
  1046.7 6.1 copy-start.25
  1053.4 174.4 %reduce-scatter.16.cloned.1.call-start = ((), (), s32[]{:S(2)}) async-start(), calls=%async_computation.13 | async-start | bytes 2654208 | tf_op jit(solution)/shard_map/reduce_scatter | solution.py:235
  1062.0 6.2 copy-start.28
  1062.0 6.2 copy-start.29
  1118.0 54.4 %collective-permute-start.1 = (f32[18,768]{1,0:T(8,128)S(1)}, f32[18,768]{1,0:T(8,128)S(1)}, u32[]{:S(2)}, u32[]{:S(2)}) collective-permute-start(f32[18,768]{1,0:T(8,128)S(1)} %slice.38), channel_id=1, source_target_pairs={{0,1},{1,2},{2,3},{4,5},{5,6},{6,7},{8,9},{9,10},{10,11},{12,13},{... | collective-permute-start | bytes 165896
  1129.3 47.5 %copy-start.10 = (bf16[394,768]{1,0:T(8,128)(2,1)S(1)}, bf16[394,768]{1,0:T(8,128)(2,1)}, u32[]{:S(2)}) copy-start(bf16[394,768]{1,0:T(8,128)(2,1)} %param.13) | copy-start | bytes 1815556
  1129.3 47.5 %copy-start.36 = (f32[768]{0:T(1024)S(1)}, f32[768]{0:T(1024)}, u32[]{:S(2)}) copy-start(f32[768]{0:T(1024)} %copy-done.35) | copy-start | bytes 9220
  1129.3 47.5 %copy-start.38 = (f32[394]{0:T(512)S(1)}, f32[394]{0:T(512)}, u32[]{:S(2)}) copy-start(f32[394]{0:T(512)} %copy-done.37) | copy-start | bytes 4732
  1129.3 49.4 %copy-start.55 = (f32[394]{0:T(512)S(1)}, f32[394]{0:T(512)}, u32[]{:S(2)}) copy-start(f32[394]{0:T(512)} %copy-done.54) | copy-start | bytes 4732
  1129.3 49.4 %copy-start.46 = (f32[394]{0:T(512)S(1)}, f32[394]{0:T(512)}, u32[]{:S(2)}) copy-start(f32[394]{0:T(512)} %copy-done.45) | copy-start | bytes 4732
  1176.8 41.1 %copy-start.62 = (f32[96,8]{0,1:T(8,128)S(1)}, f32[96,8]{0,1:T(8,128)}, u32[]{:S(2)}) copy-start(f32[96,8]{0,1:T(8,128)} %copy.141) | copy-start | bytes 9220
  1176.8 47.7 %copy-start.8 = (f32[394,768]{1,0:T(8,128)S(1)}, f32[394,768]{1,0:T(8,128)}, u32[]{:S(2)}) copy-start(f32[394,768]{1,0:T(8,128)} %copy-done.5) | copy-start | bytes 3631108
  (23 other events, 37.8 us)
Sparse Core Ops, SparseCore 0:
  42.2 21.9 all-gather.11
  319.4 44.1 all-gather.7
  406.9 95.8 reduce-scatter.11
  748.3 43.7 all-gather.9
  816.3 95.8 reduce-scatter.13
  928.6 71.0 reduce-scatter.19
  1001.8 23.6 all-gather.13
  1053.5 62.4 reduce-scatter.17
  1120.6 67.9 reduce-scatter.15
where the time goes:
time: 1250 us; the launch traced here: 1240 us
  blocking collectives  428 us (34%)
  waiting for transfers between devices  328 us (26%)
  local copies, waits for them, and re-layouts  270 us (22%)
  matrix products  126 us (10%)
  other arithmetic  49.1 us (4%)
  between operations  20.2 us (2%)
  starting transfers between devices  14.5 us (1%)
    reduce_scatter x2, waiting for transfers between devices, slot_sums(): lax.psum_scatter(contract_last(operand, weights), 'tensor', scatter_dimen...  192 us
    unnamed x4, blocking collectives  153 us
    psum x2, blocking collectives, local(): lax.psum((jnp.sum(own_mask * row_loss), jnp.sum(own_mask)), ('dp', 'tenso...  97.4 us
    all_gather x2, waiting for transfers between devices, slot_gather(): return lax.all_gather(values, 'tensor', axis=0, tiled=True)  88.2 us
    all_to_all x2, blocking collectives, to_experts(): return lax.all_to_all(buffer, 'dp', split_axis=0, concat_axis=0, tiled=True)  76.4 us
    scatter x2, local copies, waits for them, and re-layouts, local(): empty_slots.at[flat_ids, slot_index].set(grad_picked)  75.2 us
    scatter x2, local copies, waits for them, and re-layouts, local(): arrived = to_experts(empty_slots.at[flat_ids, slot_index].set(copies))  75.2 us
    unnamed x173, local copies, waits for them, and re-layouts  40.9 us
  transfers between devices with their start and end apart: 13, of which 6 were waited for; matrix products, arithmetic and copies ran while one was open for 12% of the time, Pallas kernels for 0%

commit v1 on v0

v1 whole, which is shorter than its diff:
```python
import jax
import jax.numpy as jnp
from jax import lax
from jax.sharding import PartitionSpec as P

HD = 64
EPSILON = 1e-06
MASKED = -1000000000.0
BF = jnp.bfloat16
F32 = jnp.float32
TREE = 8


def dot(a, b, ca, cb):
    return lax.dot_general(a, b, (((ca,), (cb,)), ((), ())), preferred_element_type=F32)


def swap(value, axis, k):
    n = lax.axis_size(axis)
    return lax.ppermute(value, axis, [(i, i ^ k) for i in range(n)])


def bit(axis, k):
    return (lax.axis_index(axis) // k) % 2 == 1


def pair(low, high, flip, at):
    return jnp.where(flip, jnp.stack([high, low], at), jnp.stack([low, high], at))


def gather_z(v, at):
    r1, r2, r3 = swap(v, "dp", 2), swap(v, "dp", 4), swap(v, "dp", 6)
    odd, far = bit("dp", 2), bit("dp", 4)
    low, high = pair(v, r1, odd, at), pair(r2, r3, odd, at)
    return jnp.where(far, jnp.concatenate([high, low], at), jnp.concatenate([low, high], at))


def gather_x(v, at):
    return pair(v, swap(v, "dp", 1), bit("dp", 1), at)


def gather_t(v, k):
    return jnp.stack([v, swap(v, "tensor", k)], 0)


def gather_dense(v, order):
    dims = []
    for axis in order:
        if axis in "yc":
            v = gather_t(v, 2 if axis == "y" else 1)
            dims = [axis] + dims
        else:
            lead = sum(d in "yc" for d in dims)
            at = lead + (1 if axis == "x" and "z" in dims else 0)
            v = gather_z(v, at) if axis == "z" else gather_x(v, at)
            dims = dims[:at] + [axis] + dims[at:]
    if dims[0] == "c":
        v = jnp.swapaxes(v, 0, 1)
    return v.reshape(4, 768, v.shape[-1])


def take(v, index, at):
    return lax.dynamic_index_in_dim(v, index, at, keepdims=False)


def scatter_dense(v, order):
    rows = v.shape[1] // 8
    v = v.reshape(2, 2, 4, 2, rows, v.shape[-1])
    dims = ["y", "c", "z", "x"]
    me = lax.axis_index("dp")
    for axis in order:
        at = dims.index(axis)
        if axis in "yc":
            kept, sent = take(v, 0, at), take(v, 1, at)
            v = kept + swap(sent.astype(BF), "tensor", 2 if axis == "y" else 1).astype(F32)
        elif axis == "x":
            x = me % 2
            v = take(v, x, at) + swap(take(v, 1 - x, at).astype(BF), "dp", 1).astype(F32)
        else:
            z = me // 2
            total = take(v, z, at)
            for k in (1, 2, 3):
                total = total + swap(take(v, z ^ k, at).astype(BF), "dp", 2 * k).astype(F32)
            v = total
        dims.pop(at)
    return v


ORDERS = ("zxyc", "zyxc", "yzxc")


def dense_weights(shard):
    if lax.axis_size("dp") == TREE and lax.axis_size("tensor") == 4:
        c = shard.shape[1] // 3
        parts = [gather_dense(shard[:, i * c : (i + 1) * c], ORDERS[i]) for i in range(3)]
        return jnp.concatenate(parts, -1)
    v = lax.all_gather(shard, "dp", axis=0, tiled=True)
    return lax.all_gather(v, "tensor", axis=0)


def dense_sums(v):
    if lax.axis_size("dp") == TREE and lax.axis_size("tensor") == 4:
        c = v.shape[2] // 3
        parts = [scatter_dense(v[:, :, i * c : (i + 1) * c], ORDERS[i][::-1]) for i in range(3)]
        return jnp.concatenate(parts, -1)
    v = lax.psum_scatter(v, "tensor", scatter_dimension=0, tiled=False)
    return lax.psum_scatter(v, "dp", scatter_dimension=0, tiled=True)


def small_gather(v):
    if lax.axis_size("dp") == TREE:
        return gather_x(gather_z(v, 0), 1).reshape((-1,) + v.shape[1:])
    return lax.all_gather(v, "dp", axis=0, tiled=True)


def sum_over(v, axis):
    n = lax.axis_size(axis)
    if n > TREE:
        return lax.psum(v, axis)
    total = v
    for k in range(1, n):
        total = total + swap(v, axis, k)
    return total


def exchange(v):
    n = lax.axis_size("dp")
    if n > TREE:
        return lax.all_to_all(v, "dp", split_axis=0, concat_axis=0, tiled=True)
    return jnp.stack([v[0]] + [swap(v[k], "dp", k) for k in range(1, n)])


def relative(index):
    return index ^ lax.axis_index("dp") if lax.axis_size("dp") <= TREE else index


def gather_experts(v):
    if lax.axis_size("tensor") != 4:
        return lax.all_gather(v, "tensor", axis=0)
    two = jnp.stack([v, swap(v, "tensor", 2)])
    return jnp.concatenate([two, swap(two, "tensor", 1)])


def sum_experts(v):
    if lax.axis_size("tensor") != 4:
        return lax.psum_scatter(v, "tensor", scatter_dimension=0, tiled=False)
    two = v[:2] + swap(v[2:].astype(BF), "tensor", 1).astype(F32)
    return two[0] + swap(two[1].astype(BF), "tensor", 2).astype(F32)


def norm_parts(v):
    center = v - jnp.mean(v, axis=-1, keepdims=True)
    scale = lax.rsqrt(jnp.mean(center * center, axis=-1, keepdims=True) + EPSILON)
    return center * scale, scale


def norm_back(grad, n, scale, gain):
    gy = grad * gain
    back = scale * (
        gy - jnp.mean(gy, -1, keepdims=True) - n * jnp.mean(gy * n, -1, keepdims=True)
    )
    return back, jnp.sum(grad * n, 0), jnp.sum(grad, 0)


def local(
    tokens,
    teacher,
    valid_mask,
    expert_ids,
    attn_gain,
    attn_shift,
    qkv_weight,
    proj_weight,
    moe_gain,
    moe_shift,
    router_weight,
    up_weight,
    down_weight,
):
    rows, width = tokens.shape
    length = valid_mask.shape[1]
    images = rows // length
    experts = router_weight.shape[1]
    top = expert_ids.shape[1]
    capacity = max(2, (top * rows + experts - 1) // experts * 5 // 4)
    slots = -(-capacity // 16) * 16
    padded = -(-length // 16) * 16
    tensor_count = lax.axis_size("tensor")
    tensor_me = lax.axis_index("tensor")

    def pad(v, value=0):
        v = v.reshape((images, length) + v.shape[1:])
        v = jnp.pad(v, ((0, 0), (0, padded - length)) + ((0, 0),) * (v.ndim - 2), constant_values=value)
        return v.reshape((images * padded,) + v.shape[2:])

    def unpad(v):
        return v.reshape(images, padded, -1)[:, :length].reshape(rows, -1)

    heads_width = proj_weight.shape[1]
    shard = jnp.concatenate([qkv_weight.reshape(-1, 3 * heads_width), proj_weight], 1)
    dense = dense_weights(shard)
    small = jnp.concatenate(
        [attn_gain[:, None], attn_shift[:, None], moe_gain[:, None], moe_shift[:, None], router_weight], 1
    )
    small = small_gather(small)
    gain_one, shift_one, gain_two, shift_two = (small[:, i].astype(F32)[None] for i in range(4))
    router = small[:, 4:]
    up_all = gather_experts(up_weight[0])
    down_all = gather_experts(down_weight[0])
    count = sum_over(jnp.sum(valid_mask).astype(F32)[None], "dp")[0]
    own_mask = lax.dynamic_slice_in_dim(valid_mask, tensor_me * images, images)
    own_mask = jnp.pad(own_mask, ((0, 0), (0, padded - length)))
    row_mask = own_mask.reshape(-1, 1).astype(F32)

    ids = pad(expert_ids, -1)
    ids_rel = jnp.where(ids < 0, -1, relative(ids))
    each = lax.iota(jnp.int32, experts)
    names = jnp.any(ids_rel[:, :, None] == each, axis=1)
    padded_rows = images * padded
    row_at = lax.iota(jnp.int32, padded_rows)
    before = (row_at[:, None] > row_at[None, :]).astype(BF)
    slot = dot(before, names.astype(BF), 1, 0).astype(jnp.int32)
    slot = jnp.where(names, slot, -1)
    place = jnp.where(ids < 0, -1, ids_rel * slots + jnp.sum(jnp.where(ids_rel[:, :, None] == each, slot[:, None, :], 0), -1))
    slot_at = lax.iota(jnp.int32, slots)
    to_slots = (slot.T[:, None, :] == slot_at[None, :, None]).astype(BF).reshape(experts * slots, padded_rows)

    x = pad(tokens).astype(F32)
    n_one, scale_one = norm_parts(x)
    h1 = (n_one * gain_one + shift_one).astype(BF)
    heads = heads_width // HD
    qkv = jnp.einsum("rd,tdc->trc", h1, dense[:, :, : 3 * heads_width], preferred_element_type=F32).astype(BF)
    parts = qkv.reshape(tensor_count, images, padded, 3, heads, HD)
    q, k, v = parts[:, :, :, 0], parts[:, :, :, 1], parts[:, :, :, 2]
    scores = jnp.einsum("tbqhe,tbkhe->tbhqk", q, k, preferred_element_type=F32) * HD**-0.5
    scores = jnp.where((own_mask > 0)[None, :, None, None, :], scores, MASKED)
    log_total = jax.nn.logsumexp(scores, axis=-1, keepdims=True)
    probs_f = jnp.exp(scores - log_total)
    probs = probs_f.astype(BF)
    context = jnp.einsum("tbhqk,tbkhe->tbqhe", probs, v, preferred_element_type=F32).astype(BF)
    context = context.reshape(tensor_count, padded_rows, heads_width)
    proj = dense[:, :, 3 * heads_width :]
    attn = jnp.einsum("trc,tdc->rd", context, proj, preferred_element_type=F32)
    residual = x + attn
    n_two, scale_two = norm_parts(residual)
    h2 = (n_two * gain_two + shift_two).astype(BF)
    router_probs = jax.nn.softmax(dot(h2, router, 1, 0), axis=-1)
    choose = (ids[:, :, None] == each).astype(F32)
    gates = jnp.sum(choose * router_probs[:, None, :], -1)
    gates_rel = jnp.sum((ids_rel[:, :, None] == each).astype(F32) * gates[:, :, None], 1)

    sent = dot(to_slots, h2, 1, 0).astype(BF).reshape(experts, slots, width)
    arrived = exchange(sent).reshape(-1, width)
    up = [dot(arrived, up_all[t], 1, 0) for t in range(tensor_count)]
    hidden = [jax.nn.gelu(u, approximate=False).astype(BF) for u in up]
    out = sum(dot(hidden[t], down_all[t], 1, 1) for t in range(tensor_count))
    returned = exchange(out.astype(BF).reshape(experts, slots, width)).reshape(-1, width)
    all_at = lax.iota(jnp.int32, experts * slots)
    picked = [dot((place[:, j : j + 1] == all_at).astype(BF), returned, 1, 0) for j in range(top)]
    result = residual + sum(gates[:, j : j + 1] * picked[j] for j in range(top))
    errors = result - pad(teacher).astype(F32)
    loss_sum = jnp.sum(row_mask * jnp.mean(errors * errors, -1, keepdims=True))
    loss = sum_over(sum_over(loss_sum[None], "tensor"), "dp")[0] / count
    total_rows = rows * lax.axis_size("dp") * tensor_count
    g = row_mask * errors * (total_rows / count)
    grad_gates = jnp.stack([jnp.sum(g * picked[j], -1) for j in range(top)], 1)
    gated = (gates_rel.T[:, :, None] * g[None]).astype(BF)
    grad_sent = jnp.einsum(
        "esr,erd->esd", to_slots.reshape(experts, slots, padded_rows), gated, preferred_element_type=F32
    ).astype(BF)
    grad_out = exchange(grad_sent).reshape(-1, width)
    grad_up = []
    for t in range(tensor_count):
        gh = dot(grad_out, down_all[t], 1, 0)
        grad_up.append(jax.vjp(lambda u: jax.nn.gelu(u, approximate=False), up[t])[1](gh)[0].astype(BF))
    grad_arrived = sum(dot(grad_up[t], up_all[t], 1, 1) for t in range(tensor_count))
    grad_back = exchange(grad_arrived.astype(BF).reshape(experts, slots, width)).reshape(-1, width)
    grad_down_w = sum_experts(jnp.stack([dot(grad_out, hidden[t], 0, 0) for t in range(tensor_count)]))
    grad_up_w = sum_experts(jnp.stack([dot(arrived, grad_up[t], 0, 0) for t in range(tensor_count)]))

    either = jnp.any(place[:, :, None] == all_at, axis=1).astype(BF)
    grad_probs = jnp.sum(choose * grad_gates[:, :, None], 1)
    grad_logits = router_probs * (grad_probs - jnp.sum(router_probs * grad_probs, -1, keepdims=True))
    grad_logits = grad_logits.astype(BF)
    grad_h2 = dot(either, grad_back, 1, 0) + dot(grad_logits, router, 1, 1)
    grad_router = dot(h2, grad_logits, 0, 0)
    back, grad_gain_two, grad_shift_two = norm_back(grad_h2, n_two, scale_two, gain_two)
    grad_residual = g + back

    grad_attn = grad_residual.astype(BF)
    grad_context = jnp.einsum("rd,tdc->trc", grad_attn, proj, preferred_element_type=F32).astype(BF)
    grad_proj = jnp.einsum("rd,trc->tdc", grad_attn, context, preferred_element_type=F32)
    gc = grad_context.reshape(tensor_count, images, padded, heads, HD)
    grad_v = jnp.einsum("tbhqk,tbqhe->tbkhe", probs, gc, preferred_element_type=F32)
    grad_pr = jnp.einsum("tbqhe,tbkhe->tbhqk", gc, v, preferred_element_type=F32)
    delta = jnp.sum(probs_f * grad_pr, -1, keepdims=True)
    grad_scores = (probs_f * (grad_pr - delta)).astype(BF)
    grad_q = jnp.einsum("tbhqk,tbkhe->tbqhe", grad_scores, k, preferred_element_type=F32) * HD**-0.5
    grad_k = jnp.einsum("tbhqk,tbqhe->tbkhe", grad_scores, q, preferred_element_type=F32) * HD**-0.5
    grad_qkv = jnp.stack([grad_q, grad_k, grad_v], 3).astype(BF)
    grad_qkv = grad_qkv.reshape(tensor_count, padded_rows, 3 * heads_width)
    grad_qkv_w = jnp.einsum("rd,trc->tdc", h1, grad_qkv, preferred_element_type=F32)
    grad_h1 = jnp.einsum("trc,tdc->rd", grad_qkv, dense[:, :, : 3 * heads_width], preferred_element_type=F32)
    back, grad_gain_one, grad_shift_one = norm_back(grad_h1, n_one, scale_one, gain_one)
    grad_tokens = grad_residual + back

    summed = dense_sums(jnp.concatenate([grad_qkv_w, grad_proj], -1))
    vectors = jnp.concatenate(
        [jnp.stack([grad_gain_one, grad_shift_one, grad_gain_two, grad_shift_two]), grad_router.T]
    )
    n_dp = lax.axis_size("dp")
    vectors = vectors.reshape(4 + experts, n_dp, width // n_dp).swapaxes(0, 1)
    vectors = sum_over(vectors, "tensor")
    if n_dp > TREE:
        vectors = lax.psum_scatter(vectors, "dp", scatter_dimension=0, tiled=False)
    else:
        me = lax.axis_index("dp")
        own = take(vectors, me, 0)
        for k in range(1, n_dp):
            own = own + swap(take(vectors, me ^ k, 0), "dp", k)
        vectors = own
    return (
        loss,
        unpad(result).astype(BF),
        unpad(grad_tokens),
        vectors[0],
        vectors[1],
        summed[:, : 3 * heads_width].reshape(-1, 3, heads_width),
        summed[:, 3 * heads_width :],
        vectors[2],
        vectors[3],
        vectors[4:].T,
        grad_up_w[None],
        grad_down_w[None],
    )


def solution(mesh):
    rows = P(("dp", "tensor"), None)
    experts = P("dp", None, "tensor")
    in_specs = (
        rows,
        rows,
        P("dp", None),
        rows,
        P("dp"),
        P("dp"),
        experts,
        P("dp", "tensor"),
        P("dp"),
        P("dp"),
        P("dp", None),
        experts,
        experts,
    )
    out_specs = (
        P(),
        rows,
        rows,
        P("dp"),
        P("dp"),
        experts,
        P("dp", "tensor"),
        P("dp"),
        P("dp"),
        P("dp", None),
        experts,
        experts,
    )
    return jax.shard_map(local, mesh=mesh, in_specs=in_specs, out_specs=out_specs, check_vma=False)
```

time: 1250 us -> 725 us (0.58)
  blocking collectives: 428 us -> 0 us
  starting transfers between devices: 14.5 us -> 167 us
  local copies, waits for them, and re-layouts: 270 us -> 129 us
  waiting for transfers between devices: 328 us -> 193 us
  other arithmetic: 49.1 us -> 72.6 us
    ppermute x0 -> x103, waiting for transfers between devices: none -> 193 us  [swap(): return lax.ppermute(value, axis, [(i, i ^ k) for i in range(n)])]
    reduce_scatter x4 -> x0, waiting for transfers between devices: 192 us -> none  [the longest x2 192 us: slot_sums(): lax.psum_scatter(contract_last(operand, weights), 'tensor', scatter_dimen...]
    ppermute x0 -> x103, starting transfers between devices: none -> 167 us  [swap(): return lax.ppermute(value, axis, [(i, i ^ k) for i in range(n)])]
    unnamed x4 -> x0, blocking collectives: 153 us -> none
    scatter x4 -> x0, local copies, waits for them, and re-layouts: 150 us -> none  [the longest x2 75.2 us: local(): empty_slots.at[flat_ids, slot_index].set(grad_picked)]
    psum x3 -> x0, blocking collectives: 104 us -> none  [the longest x2 97.4 us: local(): lax.psum((jnp.sum(own_mask * row_loss), jnp.sum(own_mask)), ('dp', 'tenso...]
    all_gather x4 -> x0, waiting for transfers between devices: 101 us -> none  [the longest x2 88.2 us: slot_gather(): return lax.all_gather(values, 'tensor', axis=0, tiled=True)]
    all_gather x3 -> x0, blocking collectives: 95 us -> none  [the longest x1 35.6 us: local(): lax.all_gather(qkv_weight, 'dp', axis=0, tiled=True)]
  transfers between devices with their start and end apart: 13 -> 103, of which waited for: 6 -> 44; matrix products, arithmetic and copies ran while one was open for 12% -> 37% of each run, Pallas kernels for 0% -> 0%
where the time goes in v1:
time: 725 us; the launch traced here: 714 us
  waiting for transfers between devices  193 us (27%)
  starting transfers between devices  167 us (23%)
  matrix products  137 us (19%)
  local copies, waits for them, and re-layouts  129 us (18%)
  other arithmetic  72.6 us (10%)
  between operations  16.4 us (2%)
    ppermute x103, waiting for transfers between devices, swap(): return lax.ppermute(value, axis, [(i, i ^ k) for i in range(n)])  193 us
    ppermute x103, starting transfers between devices, swap(): return lax.ppermute(value, axis, [(i, i ^ k) for i in range(n)])  167 us
    dot_general x32, matrix products, dot(): lax.dot_general(a, b, (((ca,), (cb,)), ((), ())), preferred_element_type=...  105 us
    unnamed x220, local copies, waits for them, and re-layouts  30.8 us
  transfers between devices with their start and end apart: 103, of which 44 were waited for; matrix products, arithmetic and copies ran while one was open for 37% of the time, Pallas kernels for 0%

profile of v1, /device:TPU:0, one launch (start us, length us, event | category | flops | bytes accessed | tf_op | source)
XLA Modules:
  0.0 713.7 jit_solution(8675349034651668864)
XLA Ops:
  3.3 3.0 collective-permute-start.8
  34.2 4.8 collective-permute-start.53
  39.6 4.0 collective-permute-start.54
  45.1 3.7 collective-permute-start.55
  50.5 3.7 collective-permute-start.56
  65.4 3.1 collective-permute-done.21
  80.9 2.9 collective-permute-start.15
  99.6 28.9 %collective-permute-done.9 = bf16[4,96,256]{1,2,0:T(8,128)(2,1)} collective-permute-done((bf16[4,96,256]{1,2,0:T(8,128)(2,1)}, bf16[4,96,256]{1,2,0:T(8,128)(2,1)}, u32[]{:S(2)}, u32[]{:S(2)}) %collective-permute-start.9) | collective-permute-done | bytes 196640 | tf_op jit(solution)/shard_map/ppermute | solution.py:20
  141.8 3.0 maximum_select_fusion.2
  153.3 2.9 pad_maximum_fusion.3
  156.7 3.2 pad_maximum_fusion.4
  187.6 5.2 convert_bitcast_fusion
  192.8 10.1 %reshape.1395 = bf16[4,2,208,3,3,64]{5,4,3,2,1,0:T(4,128)(2,1)} reshape(bf16[4,416,576]{2,1,0:T(8,128)(2,1)} %convert_bitcast_fusion) | data formatting | bytes 3833856 | tf_op jit(solution)/shard_map/reshape | solution.py:233
  202.9 5.1 fusion.162
  208.0 3.8 copy.246
  239.1 5.3 collective-permute-done.24
  245.9 12.0 %collective-permute-done.25 = bf16[128,768]{1,0:T(8,128)(2,1)S(1)} collective-permute-done((bf16[128,768]{1,0:T(8,128)(2,1)S(1)}, bf16[128,768]{1,0:T(8,128)(2,1)S(1)}, u32[]{:S(2)}, u32[]{:S(2)}) %collective-permute-start.25) | collective-permute-done | bytes 196640 | tf_op jit(solution)/shard_map/ppermute | solution.py:20
  257.9 3.8 collective-permute-start.28
  266.4 9.6 %multiply_convert_fusion.6 = (bf16[1024,768]{1,0:T(8,128)(2,1)S(1)}, f32[1024,768]{1,0:T(8,128)}, f32[1024,768]{1,0:T(8,128)}) fusion(bf16[1024,768]{1,0:T(8,128)(2,1)S(1)} %bitcast.598, bf16[1,768,768]{2,1,0:T(8,128)(2,1)S(1)} %copy-done.35), kind=kOutput, calls=%fused_computation.71 | convolution fusion | flops 1259077632 | bytes 10616832 | tf_op jit(solution)/shard_map/dot_general | solution.py:15
  276.0 3.3 fusion.142
  279.3 10.7 %multiply_convert_fusion.5 = (bf16[1024,768]{1,0:T(8,128)(2,1)S(1)}, f32[1024,768]{1,0:T(8,128)}, f32[1024,768]{1,0:T(8,128)}) fusion(bf16[1024,768]{1,0:T(8,128)(2,1)S(1)} %bitcast.599, bf16[768,768]{1,0:T(8,128)(2,1)} %collective-permute-done.29), kind=kOutput, calls=%fused_computation.58 | convolution fusion | flops 1259077632 | bytes 10616832 | tf_op jit(solution)/shard_map/dot_general | solution.py:15
  290.0 3.3 fusion.171
  293.3 10.8 %multiply_convert_fusion.4 = (bf16[1024,768]{1,0:T(8,128)(2,1)S(1)}, f32[1024,768]{1,0:T(8,128)}, f32[1024,768]{1,0:T(8,128)}) fusion(bf16[1024,768]{1,0:T(8,128)(2,1)S(1)} %bitcast.600, bf16[2,768,768]{2,1,0:T(8,128)(2,1)} %collective-permute-done.31), kind=kOutput, calls=%fused_computation.45 | convolution fusion | flops 1259077632 | bytes 10616832 | tf_op jit(solution)/shard_map/dot_general | solution.py:15
  304.1 11.4 %multiply_convert_fusion.3 = (bf16[1024,768]{1,0:T(8,128)(2,1)S(1)}, f32[1024,768]{1,0:T(8,128)}, f32[1024,768]{1,0:T(8,128)}) fusion(bf16[1024,768]{1,0:T(8,128)(2,1)S(1)} %bitcast.601, bf16[2,768,768]{2,1,0:T(8,128)(2,1)} %collective-permute-done.31), kind=kOutput, calls=%fused_computation.32 | convolution fusion | flops 1259077632 | bytes 10616832 | tf_op jit(solution)/shard_map/dot_general | solution.py:15
  315.6 3.3 fusion.58
  323.7 5.6 collective-permute-start.34
  330.3 2.9 collective-permute-start.36
  335.7 6.2 collective-permute-done.34
  341.9 3.1 collective-permute-start.39
  345.7 13.8 %collective-permute-done.37 = bf16[128,768]{1,0:T(8,128)(2,1)S(1)} collective-permute-done((bf16[128,768]{1,0:T(8,128)(2,1)S(1)}, bf16[128,768]{1,0:T(8,128)(2,1)S(1)}, u32[]{:S(2)}, u32[]{:S(2)}) %collective-permute-start.37) | collective-permute-done | bytes 196640 | tf_op jit(solution)/shard_map/ppermute | solution.py:20
  368.9 6.9 collective-permute-start.58
  391.9 9.5 %collective-permute-done.60 = bf16[128,768]{1,0:T(8,128)(2,1)} collective-permute-done((bf16[128,768]{1,0:T(8,128)(2,1)}, bf16[128,768]{1,0:T(8,128)(2,1)}, u32[]{:S(2)}, u32[]{:S(2)}) %collective-permute-start.60) | collective-permute-done | bytes 196640 | tf_op jit(solution)/shard_map/ppermute | solution.py:20
  403.0 3.5 collective-permute-done.61
  409.5 4.9 add_convert_fusion.4
  417.8 3.4 add_convert_fusion.2
  424.3 3.4 add_convert_fusion.3
  430.9 3.4 add_convert_fusion.1
  434.3 3.0 add_convert_fusion
  441.6 2.9 convolution_bitcast_fusion.4
  447.4 3.0 convolution_bitcast_fusion.1
  457.2 4.0 collective-permute-start.65
  474.3 12.0 %collective-permute-done.67 = bf16[128,768]{1,0:T(8,128)(2,1)S(1)} collective-permute-done((bf16[128,768]{1,0:T(8,128)(2,1)S(1)}, bf16[128,768]{1,0:T(8,128)(2,1)S(1)}, u32[]{:S(2)}, u32[]{:S(2)}) %collective-permute-start.67) | collective-permute-done | bytes 196640 | tf_op jit(solution)/shard_map/ppermute | solution.py:20
  486.3 4.7 collective-permute-done.68
  495.4 3.0 fusion.51
  501.3 3.9 convolution_bitcast_fusion.6
  511.3 3.9 copy.215
  515.2 6.8 convert_element_type.403
  522.0 6.4 multiply_reduce_fusion.2
  533.5 3.5 fusion.161
  537.0 3.6 copy.223
  540.5 3.5 multiply_add_fusion
  546.5 3.5 copy.220
  550.1 2.9 collective-permute-start.80
  554.9 4.4 collective-permute-start.78
  586.8 2.9 collective-permute-done.47
  589.7 3.5 collective-permute-start.48
  594.9 3.9 collective-permute-start.49
  601.3 3.1 collective-permute-start.76
  624.6 5.8 collective-permute-done.81
  636.9 5.0 collective-permute-done.82
  674.6 13.8 %collective-permute-done.100 = bf16[768,768]{1,0:T(8,128)(2,1)} collective-permute-done((bf16[768,768]{1,0:T(8,128)(2,1)S(1)}, bf16[768,768]{1,0:T(8,128)(2,1)}, u32[]{:S(2)}, u32[]{:S(2)}) %collective-permute-start.100) | collective-permute-done | bytes 1179680 | tf_op jit(solution)/shard_map/ppermute | solution.py:20
  688.4 3.6 fusion.33
  692.0 17.3 %collective-permute-done.102 = bf16[768,768]{1,0:T(8,128)(2,1)} collective-permute-done((bf16[768,768]{1,0:T(8,128)(2,1)S(1)}, bf16[768,768]{1,0:T(8,128)(2,1)}, u32[]{:S(2)}, u32[]{:S(2)}) %collective-permute-start.102) | collective-permute-done | bytes 1179680 | tf_op jit(solution)/shard_map/ppermute | solution.py:20
  709.3 3.0 fusion.31
  (597 shorter events, 333.2 us)
Async XLA Ops:
  3.3 69.2 %collective-permute-start.8 = (bf16[96,256]{0,1:T(8,128)(2,1)}, bf16[96,256]{0,1:T(8,128)(2,1)}, u32[]{:S(2)}, u32[]{:S(2)}) collective-permute-start(bf16[96,256]{0,1:T(8,128)(2,1)} %get-tuple-element.128), channel_id=1, source_target_pairs={{0,8},{4,12},{8,0},{12,4},{16,24},{20,28},{24,16},{28,20},{1,9},{5... | collective-permute-start | bytes 147464 | tf_op jit(solution)/shard_map/ppermute | solution.py:20
  6.4 68.1 %collective-permute-start.7 = (bf16[96,256]{0,1:T(8,128)(2,1)}, bf16[96,256]{0,1:T(8,128)(2,1)S(1)}, u32[]{:S(2)}, u32[]{:S(2)}) collective-permute-start(bf16[96,256]{0,1:T(8,128)(2,1)} %get-tuple-element.128), channel_id=1, source_target_pairs={{0,16},{4,20},{8,24},{12,28},{16,0},{20,4},{24,8},{28,12},{1,17},{... | collective-permute-start | bytes 147464 | tf_op jit(solution)/shard_map/ppermute | solution.py:20
  8.9 67.1 %collective-permute-start.6 = (bf16[96,256]{0,1:T(8,128)(2,1)}, bf16[96,256]{0,1:T(8,128)(2,1)S(1)}, u32[]{:S(2)}, u32[]{:S(2)}) collective-permute-start(bf16[96,256]{0,1:T(8,128)(2,1)} %get-tuple-element.128), channel_id=1, source_target_pairs={{0,24},{4,28},{8,16},{12,20},{16,8},{20,12},{24,0},{28,4},{1,25},{... | collective-permute-start | bytes 147464 | tf_op jit(solution)/shard_map/ppermute | solution.py:20
  10.5 49.4 %collective-permute-start.20 = (bf16[96,12]{0,1:T(8,128)(2,1)S(1)}, bf16[96,12]{0,1:T(8,128)(2,1)S(1)}, u32[]{:S(2)}, u32[]{:S(2)}) collective-permute-start(bf16[96,12]{0,1:T(8,128)(2,1)S(1)} %concatenate.389), channel_id=1, source_target_pairs={{0,8},{4,12},{8,0},{12,4},{16,24},{20,28},{24,16},{28,20},{1,9},{5... | collective-permute-start | bytes 6920 | tf_op jit(solution)/shard_map/ppermute | solution.py:20
  13.4 12.6 %collective-permute-start.50 = (f32[1]{0:T(128)}, f32[1]{0:T(128)}, u32[]{:S(2)}, u32[]{:S(2)}) collective-permute-start(f32[1]{0:T(128)} %bitcast.97), channel_id=1, source_target_pairs={{0,4},{4,0},{8,12},{12,8},{16,20},{20,16},{24,28},{28,24},{1,5},{5... | collective-permute-start | bytes 20 | tf_op jit(solution)/shard_map/ppermute | solution.py:20
  62.3 16.3 %collective-permute-start.2 = (bf16[96,256]{0,1:T(8,128)(2,1)}, bf16[96,256]{0,1:T(8,128)(2,1)S(1)}, u32[]{:S(2)}, u32[]{:S(2)}) collective-permute-start(bf16[96,256]{0,1:T(8,128)(2,1)} %get-tuple-element.124), channel_id=1, source_target_pairs={{0,8},{4,12},{8,0},{12,4},{16,24},{20,28},{24,16},{28,20},{1,9},{5... | collective-permute-start | bytes 147464 | tf_op jit(solution)/shard_map/ppermute | solution.py:20
  68.5 16.4 %collective-permute-start = (bf16[96,256]{0,1:T(8,128)(2,1)}, bf16[96,256]{0,1:T(8,128)(2,1)S(1)}, u32[]{:S(2)}, u32[]{:S(2)}) collective-permute-start(bf16[96,256]{0,1:T(8,128)(2,1)} %get-tuple-element.124), channel_id=1, source_target_pairs={{0,24},{4,28},{8,16},{12,20},{16,8},{20,12},{24,0},{28,4},{1,25},{... | collective-permute-start | bytes 147464 | tf_op jit(solution)/shard_map/ppermute | solution.py:20
  72.5 13.9 %collective-permute-start.1 = (bf16[96,256]{0,1:T(8,128)(2,1)}, bf16[96,256]{0,1:T(8,128)(2,1)S(1)}, u32[]{:S(2)}, u32[]{:S(2)}) collective-permute-start(bf16[96,256]{0,1:T(8,128)(2,1)} %get-tuple-element.124), channel_id=1, source_target_pairs={{0,16},{4,20},{8,24},{12,28},{16,0},{20,4},{24,8},{28,12},{1,17},{... | collective-permute-start | bytes 147464 | tf_op jit(solution)/shard_map/ppermute | solution.py:20
  76.1 77.3 %collective-permute-start.29 = (bf16[768,768]{1,0:T(8,128)(2,1)}, bf16[768,768]{1,0:T(8,128)(2,1)}, u32[]{:S(2)}, u32[]{:S(2)}) collective-permute-start(bf16[768,768]{1,0:T(8,128)(2,1)} %bitcast.564), channel_id=1, source_target_pairs={{0,2},{1,3},{2,0},{3,1},{4,6},{5,7},{6,4},{7,5},{8,10},{9,11},{10,... | collective-permute-start | bytes 3538952 | tf_op jit(solution)/shard_map/ppermute | solution.py:20
  78.6 78.0 %collective-permute-start.30 = (bf16[768,768]{1,0:T(8,128)(2,1)}, bf16[768,768]{1,0:T(8,128)(2,1)}, u32[]{:S(2)}, u32[]{:S(2)}) collective-permute-start(bf16[768,768]{1,0:T(8,128)(2,1)} %bitcast.77), channel_id=1, source_target_pairs={{0,2},{1,3},{2,0},{3,1},{4,6},{5,7},{6,4},{7,5},{8,10},{9,11},{10,... | collective-permute-start | bytes 3538952 | tf_op jit(solution)/shard_map/ppermute | solution.py:20
  88.5 39.9 %collective-permute-start.9 = (bf16[4,96,256]{1,2,0:T(8,128)(2,1)}, bf16[4,96,256]{1,2,0:T(8,128)(2,1)}, u32[]{:S(2)}, u32[]{:S(2)}) collective-permute-start(bf16[4,96,256]{1,2,0:T(8,128)(2,1)} %maximum_select_fusion.11), channel_id=1, source_target_pairs={{0,2},{1,3},{2,0},{3,1},{4,6},{5,7},{6,4},{7,5},{8,10},{9,11},{10,... | collective-permute-start | bytes 589832 | tf_op jit(solution)/shard_map/ppermute | solution.py:20
  92.0 38.7 %collective-permute-start.3 = (bf16[4,96,256]{1,2,0:T(8,128)(2,1)}, bf16[4,96,256]{1,2,0:T(8,128)(2,1)}, u32[]{:S(2)}, u32[]{:S(2)}) collective-permute-start(bf16[4,96,256]{1,2,0:T(8,128)(2,1)} %maximum_select_fusion.8), channel_id=1, source_target_pairs={{0,4},{4,0},{8,12},{12,8},{16,20},{20,16},{24,28},{28,24},{1,5},{5... | collective-permute-start | bytes 589832 | tf_op jit(solution)/shard_map/ppermute | solution.py:20
  96.4 39.5 %collective-permute-start.16 = (bf16[2,4,96,256]{2,3,0,1:T(8,128)(2,1)}, bf16[2,4,96,256]{2,3,0,1:T(8,128)(2,1)S(1)}, u32[]{:S(2)}, u32[]{:S(2)}) collective-permute-start(bf16[2,4,96,256]{2,3,0,1:T(8,128)(2,1)} %maximum_select_fusion.6), channel_id=1, source_target_pairs={{0,4},{4,0},{8,12},{12,8},{16,20},{20,16},{24,28},{28,24},{1,5},{5... | collective-permute-start | bytes 1179656 | tf_op jit(solution)/shard_map/ppermute | solution.py:20
  130.7 14.1 %collective-permute-start.10 = (bf16[2,4,96,256]{2,3,0,1:T(8,128)(2,1)}, bf16[2,4,96,256]{2,3,0,1:T(8,128)(2,1)S(1)}, u32[]{:S(2)}, u32[]{:S(2)}) collective-permute-start(bf16[2,4,96,256]{2,3,0,1:T(8,128)(2,1)} %get-tuple-element.117), channel_id=1, source_target_pairs={{0,4},{4,0},{8,12},{12,8},{16,20},{20,16},{24,28},{28,24},{1,5},{5... | collective-permute-start | bytes 1179656 | tf_op jit(solution)/shard_map/ppermute | solution.py:20
  132.7 15.5 %collective-permute-start.4 = (bf16[4,2,96,256]{2,3,0,1:T(8,128)(2,1)}, bf16[4,2,96,256]{2,3,0,1:T(8,128)(2,1)}, u32[]{:S(2)}, u32[]{:S(2)}) collective-permute-start(bf16[4,2,96,256]{2,3,0,1:T(8,128)(2,1)} %maximum_select_fusion.5), channel_id=1, source_target_pairs={{0,2},{1,3},{2,0},{3,1},{4,6},{5,7},{6,4},{7,5},{8,10},{9,11},{10,... | collective-permute-start | bytes 1179656 | tf_op jit(solution)/shard_map/ppermute | solution.py:20
  141.8 18.2 %collective-permute-start.17 = (bf16[2,4,2,96,256]{4,3,2,1,0:T(8,128)(2,1)}, bf16[2,4,2,96,256]{4,3,2,1,0:T(8,128)(2,1)}, u32[]{:S(2)}, u32[]{:S(2)}) collective-permute-start(bf16[2,4,2,96,256]{4,3,2,1,0:T(8,128)(2,1)} %copy.194), channel_id=1, source_target_pairs={{0,1},{1,0},{2,3},{3,2},{4,5},{5,4},{6,7},{7,6},{8,9},{9,8},{10,11... | collective-permute-start | bytes 2359304 | tf_op jit(solution)/shard_map/ppermute | solution.py:20
  147.8 21.5 %collective-permute-start.11 = (bf16[2,4,2,96,256]{4,3,2,1,0:T(8,128)(2,1)}, bf16[2,4,2,96,256]{4,3,2,1,0:T(8,128)(2,1)}, u32[]{:S(2)}, u32[]{:S(2)}) collective-permute-start(bf16[2,4,2,96,256]{4,3,2,1,0:T(8,128)(2,1)} %copy.178), channel_id=1, source_target_pairs={{0,1},{1,0},{2,3},{3,2},{4,5},{5,4},{6,7},{7,6},{8,9},{9,8},{10,11... | collective-permute-start | bytes 2359304 | tf_op jit(solution)/shard_map/ppermute | solution.py:20
  151.9 26.4 %collective-permute-start.5 = (bf16[2,4,2,96,256]{4,3,2,1,0:T(8,128)(2,1)}, bf16[2,4,2,96,256]{4,3,2,1,0:T(8,128)(2,1)}, u32[]{:S(2)}, u32[]{:S(2)}) collective-permute-start(bf16[2,4,2,96,256]{4,3,2,1,0:T(8,128)(2,1)} %copy.174), channel_id=1, source_target_pairs={{0,1},{1,0},{2,3},{3,2},{4,5},{5,4},{6,7},{7,6},{8,9},{9,8},{10,11... | collective-permute-start | bytes 2359304 | tf_op jit(solution)/shard_map/ppermute | solution.py:20
  156.2 137.1 %collective-permute-start.31 = (bf16[2,768,768]{2,1,0:T(8,128)(2,1)}, bf16[2,768,768]{2,1,0:T(8,128)(2,1)}, u32[]{:S(2)}, u32[]{:S(2)}) collective-permute-start(bf16[2,768,768]{2,1,0:T(8,128)(2,1)} %pad_maximum_fusion.3), channel_id=1, source_target_pairs={{0,1},{1,0},{2,3},{3,2},{4,5},{5,4},{6,7},{7,6},{8,9},{9,8},{10,11... | collective-permute-start | bytes 7077896 | tf_op jit(solution)/shard_map/ppermute | solution.py:20
  159.9 155.6 %collective-permute-start.32 = (bf16[2,768,768]{2,1,0:T(8,128)(2,1)}, bf16[2,768,768]{2,1,0:T(8,128)(2,1)}, u32[]{:S(2)}, u32[]{:S(2)}) collective-permute-start(bf16[2,768,768]{2,1,0:T(8,128)(2,1)} %pad_maximum_fusion.4), channel_id=1, source_target_pairs={{0,1},{1,0},{2,3},{3,2},{4,5},{5,4},{6,7},{7,6},{8,9},{9,8},{10,11... | collective-permute-start | bytes 7077896 | tf_op jit(solution)/shard_map/ppermute | solution.py:20
  231.9 12.5 %collective-permute-start.24 = (bf16[128,768]{1,0:T(8,128)(2,1)S(1)}, bf16[128,768]{1,0:T(8,128)(2,1)S(1)}, u32[]{:S(2)}, u32[]{:S(2)}) collective-permute-start(bf16[128,768]{1,0:T(8,128)(2,1)S(1)} %get-tuple-element.104), channel_id=1, source_target_pairs={{0,12},{4,8},{8,4},{12,0},{16,28},{20,24},{24,20},{28,16},{1,13},{... | collective-permute-start | bytes 589832 | tf_op jit(solution)/shard_map/ppermute | solution.py:20
  234.6 23.2 %collective-permute-start.25 = (bf16[128,768]{1,0:T(8,128)(2,1)S(1)}, bf16[128,768]{1,0:T(8,128)(2,1)S(1)}, u32[]{:S(2)}, u32[]{:S(2)}) collective-permute-start(bf16[128,768]{1,0:T(8,128)(2,1)S(1)} %get-tuple-element.103), channel_id=1, source_target_pairs={{0,16},{4,20},{8,24},{12,28},{16,0},{20,4},{24,8},{28,12},{1,17},{... | collective-permute-start | bytes 589832 | tf_op jit(solution)/shard_map/ppermute | solution.py:20
  237.6 25.9 %collective-permute-start.26 = (bf16[128,768]{1,0:T(8,128)(2,1)S(1)}, bf16[128,768]{1,0:T(8,128)(2,1)S(1)}, u32[]{:S(2)}, u32[]{:S(2)}) collective-permute-start(bf16[128,768]{1,0:T(8,128)(2,1)S(1)} %get-tuple-element.102), channel_id=1, source_target_pairs={{0,20},{4,16},{8,28},{12,24},{16,4},{20,0},{24,12},{28,8},{1,21},{... | collective-permute-start | bytes 589832 | tf_op jit(solution)/shard_map/ppermute | solution.py:20
  244.4 19.1 %collective-permute-start.27 = (bf16[128,768]{1,0:T(8,128)(2,1)S(1)}, bf16[128,768]{1,0:T(8,128)(2,1)S(1)}, u32[]{:S(2)}, u32[]{:S(2)}) collective-permute-start(bf16[128,768]{1,0:T(8,128)(2,1)S(1)} %get-tuple-element.101), channel_id=1, source_target_pairs={{0,24},{4,28},{8,16},{12,20},{16,8},{20,12},{24,0},{28,4},{1,25},{... | collective-permute-start | bytes 589832 | tf_op jit(solution)/shard_map/ppermute | solution.py:20
  323.7 18.2 %collective-permute-start.34 = (bf16[128,768]{1,0:T(8,128)(2,1)S(1)}, bf16[128,768]{1,0:T(8,128)(2,1)S(1)}, u32[]{:S(2)}, u32[]{:S(2)}) collective-permute-start(bf16[128,768]{1,0:T(8,128)(2,1)S(1)} %get-tuple-element.98), channel_id=1, source_target_pairs={{0,8},{4,12},{8,0},{12,4},{16,24},{20,28},{24,16},{28,20},{1,9},{5... | collective-permute-start | bytes 589832 | tf_op jit(solution)/shard_map/ppermute | solution.py:20
  329.3 16.3 %collective-permute-start.35 = (bf16[128,768]{1,0:T(8,128)(2,1)S(1)}, bf16[128,768]{1,0:T(8,128)(2,1)S(1)}, u32[]{:S(2)}, u32[]{:S(2)}) collective-permute-start(bf16[128,768]{1,0:T(8,128)(2,1)S(1)} %get-tuple-element.97), channel_id=1, source_target_pairs={{0,12},{4,8},{8,4},{12,0},{16,28},{20,24},{24,20},{28,16},{1,13},{... | collective-permute-start | bytes 589832 | tf_op jit(solution)/shard_map/ppermute | solution.py:20
  330.3 15.3 %collective-permute-start.36 = (bf16[128,768]{1,0:T(8,128)(2,1)S(1)}, bf16[128,768]{1,0:T(8,128)(2,1)S(1)}, u32[]{:S(2)}, u32[]{:S(2)}) collective-permute-start(bf16[128,768]{1,0:T(8,128)(2,1)S(1)} %get-tuple-element.96), channel_id=1, source_target_pairs={{0,16},{4,20},{8,24},{12,28},{16,0},{20,4},{24,8},{28,12},{1,17},{... | collective-permute-start | bytes 589832 | tf_op jit(solution)/shard_map/ppermute | solution.py:20
  333.2 26.2 %collective-permute-start.37 = (bf16[128,768]{1,0:T(8,128)(2,1)S(1)}, bf16[128,768]{1,0:T(8,128)(2,1)S(1)}, u32[]{:S(2)}, u32[]{:S(2)}) collective-permute-start(bf16[128,768]{1,0:T(8,128)(2,1)S(1)} %get-tuple-element.95), channel_id=1, source_target_pairs={{0,20},{4,16},{8,28},{12,24},{16,4},{20,0},{24,12},{28,8},{1,21},{... | collective-permute-start | bytes 589832 | tf_op jit(solution)/shard_map/ppermute | solution.py:20
  333.3 26.2 %collective-permute-start.38 = (bf16[128,768]{1,0:T(8,128)(2,1)S(1)}, bf16[128,768]{1,0:T(8,128)(2,1)S(1)}, u32[]{:S(2)}, u32[]{:S(2)}) collective-permute-start(bf16[128,768]{1,0:T(8,128)(2,1)S(1)} %get-tuple-element.94), channel_id=1, source_target_pairs={{0,24},{4,28},{8,16},{12,20},{16,8},{20,12},{24,0},{28,4},{1,25},{... | collective-permute-start | bytes 589832 | tf_op jit(solution)/shard_map/ppermute | solution.py:20
  341.9 17.5 %collective-permute-start.39 = (bf16[128,768]{1,0:T(8,128)(2,1)S(1)}, bf16[128,768]{1,0:T(8,128)(2,1)S(1)}, u32[]{:S(2)}, u32[]{:S(2)}) collective-permute-start(bf16[128,768]{1,0:T(8,128)(2,1)S(1)} %get-tuple-element.93), channel_id=1, source_target_pairs={{0,28},{4,24},{8,20},{12,16},{16,12},{20,8},{24,4},{28,0},{1,29},{... | collective-permute-start | bytes 589832 | tf_op jit(solution)/shard_map/ppermute | solution.py:20
  366.9 13.4 %collective-permute-start.57 = (bf16[128,768]{1,0:T(8,128)(2,1)}, bf16[128,768]{1,0:T(8,128)(2,1)}, u32[]{:S(2)}, u32[]{:S(2)}) collective-permute-start(bf16[128,768]{1,0:T(8,128)(2,1)} %get-tuple-element.91), channel_id=1, source_target_pairs={{0,4},{4,0},{8,12},{12,8},{16,20},{20,16},{24,28},{28,24},{1,5},{5... | collective-permute-start | bytes 589832 | tf_op jit(solution)/shard_map/ppermute | solution.py:20
  368.9 17.8 %collective-permute-start.58 = (bf16[128,768]{1,0:T(8,128)(2,1)}, bf16[128,768]{1,0:T(8,128)(2,1)}, u32[]{:S(2)}, u32[]{:S(2)}) collective-permute-start(bf16[128,768]{1,0:T(8,128)(2,1)} %get-tuple-element.90), channel_id=1, source_target_pairs={{0,8},{4,12},{8,0},{12,4},{16,24},{20,28},{24,16},{28,20},{1,9},{5... | collective-permute-start | bytes 589832 | tf_op jit(solution)/shard_map/ppermute | solution.py:20
  375.8 14.5 %collective-permute-start.59 = (bf16[128,768]{1,0:T(8,128)(2,1)}, bf16[128,768]{1,0:T(8,128)(2,1)}, u32[]{:S(2)}, u32[]{:S(2)}) collective-permute-start(bf16[128,768]{1,0:T(8,128)(2,1)} %get-tuple-element.89), channel_id=1, source_target_pairs={{0,12},{4,8},{8,4},{12,0},{16,28},{20,24},{24,20},{28,16},{1,13},{... | collective-permute-start | bytes 589832 | tf_op jit(solution)/shard_map/ppermute | solution.py:20
  375.8 25.6 %collective-permute-start.60 = (bf16[128,768]{1,0:T(8,128)(2,1)}, bf16[128,768]{1,0:T(8,128)(2,1)}, u32[]{:S(2)}, u32[]{:S(2)}) collective-permute-start(bf16[128,768]{1,0:T(8,128)(2,1)} %get-tuple-element.88), channel_id=1, source_target_pairs={{0,16},{4,20},{8,24},{12,28},{16,0},{20,4},{24,8},{28,12},{1,17},{... | collective-permute-start | bytes 589832 | tf_op jit(solution)/shard_map/ppermute | solution.py:20
  378.6 27.9 %collective-permute-start.61 = (bf16[128,768]{1,0:T(8,128)(2,1)}, bf16[128,768]{1,0:T(8,128)(2,1)}, u32[]{:S(2)}, u32[]{:S(2)}) collective-permute-start(bf16[128,768]{1,0:T(8,128)(2,1)} %get-tuple-element.87), channel_id=1, source_target_pairs={{0,20},{4,16},{8,28},{12,24},{16,4},{20,0},{24,12},{28,8},{1,21},{... | collective-permute-start | bytes 589832 | tf_op jit(solution)/shard_map/ppermute | solution.py:20
  380.3 27.8 %collective-permute-start.62 = (bf16[128,768]{1,0:T(8,128)(2,1)}, bf16[128,768]{1,0:T(8,128)(2,1)S(1)}, u32[]{:S(2)}, u32[]{:S(2)}) collective-permute-start(bf16[128,768]{1,0:T(8,128)(2,1)} %get-tuple-element.86), channel_id=1, source_target_pairs={{0,24},{4,28},{8,16},{12,20},{16,8},{20,12},{24,0},{28,4},{1,25},{... | collective-permute-start | bytes 589832 | tf_op jit(solution)/shard_map/ppermute | solution.py:20
  386.7 22.2 %collective-permute-start.63 = (bf16[128,768]{1,0:T(8,128)(2,1)S(1)}, bf16[128,768]{1,0:T(8,128)(2,1)S(1)}, u32[]{:S(2)}, u32[]{:S(2)}) collective-permute-start(bf16[128,768]{1,0:T(8,128)(2,1)S(1)} %get-tuple-element.85), channel_id=1, source_target_pairs={{0,28},{4,24},{8,20},{12,16},{16,12},{20,8},{24,4},{28,0},{1,29},{... | collective-permute-start | bytes 589832 | tf_op jit(solution)/shard_map/ppermute | solution.py:20
  457.2 13.5 %collective-permute-start.65 = (bf16[128,768]{1,0:T(8,128)(2,1)S(1)}, bf16[128,768]{1,0:T(8,128)(2,1)S(1)}, u32[]{:S(2)}, u32[]{:S(2)}) collective-permute-start(bf16[128,768]{1,0:T(8,128)(2,1)S(1)} %get-tuple-element.83), channel_id=1, source_target_pairs={{0,8},{4,12},{8,0},{12,4},{16,24},{20,28},{24,16},{28,20},{1,9},{5... | collective-permute-start | bytes 589832 | tf_op jit(solution)/shard_map/ppermute | solution.py:20
  461.2 13.1 %collective-permute-start.66 = (bf16[128,768]{1,0:T(8,128)(2,1)S(1)}, bf16[128,768]{1,0:T(8,128)(2,1)S(1)}, u32[]{:S(2)}, u32[]{:S(2)}) collective-permute-start(bf16[128,768]{1,0:T(8,128)(2,1)S(1)} %get-tuple-element.82), channel_id=1, source_target_pairs={{0,12},{4,8},{8,4},{12,0},{16,28},{20,24},{24,20},{28,16},{1,13},{... | collective-permute-start | bytes 589832 | tf_op jit(solution)/shard_map/ppermute | solution.py:20
  461.6 24.7 %collective-permute-start.67 = (bf16[128,768]{1,0:T(8,128)(2,1)S(1)}, bf16[128,768]{1,0:T(8,128)(2,1)S(1)}, u32[]{:S(2)}, u32[]{:S(2)}) collective-permute-start(bf16[128,768]{1,0:T(8,128)(2,1)S(1)} %get-tuple-element.81), channel_id=1, source_target_pairs={{0,16},{4,20},{8,24},{12,28},{16,0},{20,4},{24,8},{28,12},{1,17},{... | collective-permute-start | bytes 589832 | tf_op jit(solution)/shard_map/ppermute | solution.py:20
  464.4 26.6 %collective-permute-start.68 = (bf16[128,768]{1,0:T(8,128)(2,1)S(1)}, bf16[128,768]{1,0:T(8,128)(2,1)S(1)}, u32[]{:S(2)}, u32[]{:S(2)}) collective-permute-start(bf16[128,768]{1,0:T(8,128)(2,1)S(1)} %get-tuple-element.80), channel_id=1, source_target_pairs={{0,20},{4,16},{8,28},{12,24},{16,4},{20,0},{24,12},{28,8},{1,21},{... | collective-permute-start | bytes 589832 | tf_op jit(solution)/shard_map/ppermute | solution.py:20
  468.4 22.6 %collective-permute-start.69 = (bf16[128,768]{1,0:T(8,128)(2,1)S(1)}, bf16[128,768]{1,0:T(8,128)(2,1)S(1)}, u32[]{:S(2)}, u32[]{:S(2)}) collective-permute-start(bf16[128,768]{1,0:T(8,128)(2,1)S(1)} %get-tuple-element.79), channel_id=1, source_target_pairs={{0,24},{4,28},{8,16},{12,20},{16,8},{20,12},{24,0},{28,4},{1,25},{... | collective-permute-start | bytes 589832 | tf_op jit(solution)/shard_map/ppermute | solution.py:20
  470.7 20.4 %collective-permute-start.70 = (bf16[128,768]{1,0:T(8,128)(2,1)S(1)}, bf16[128,768]{1,0:T(8,128)(2,1)S(1)}, u32[]{:S(2)}, u32[]{:S(2)}) collective-permute-start(bf16[128,768]{1,0:T(8,128)(2,1)S(1)} %get-tuple-element.78), channel_id=1, source_target_pairs={{0,28},{4,24},{8,20},{12,16},{16,12},{20,8},{24,4},{28,0},{1,29},{... | collective-permute-start | bytes 589832 | tf_op jit(solution)/shard_map/ppermute | solution.py:20
  495.0 69.5 %collective-permute-start.40 = (f32[1]{0:T(128)}, f32[1]{0:T(128)}, u32[]{:S(2)}, u32[]{:S(2)}) collective-permute-start(f32[1]{0:T(128)} %bitcast.96), channel_id=1, source_target_pairs={{0,1},{1,0},{2,3},{3,2},{4,5},{5,4},{6,7},{7,6},{8,9},{9,8},{10,11... | collective-permute-start | bytes 20 | tf_op jit(solution)/shard_map/ppermute | solution.py:20
  495.0 71.3 %collective-permute-start.41 = (f32[1]{0:T(128)}, f32[1]{0:T(128)}, u32[]{:S(2)}, u32[]{:S(2)}) collective-permute-start(f32[1]{0:T(128)} %bitcast.96), channel_id=1, source_target_pairs={{0,2},{1,3},{2,0},{3,1},{4,6},{5,7},{6,4},{7,5},{8,10},{9,11},{10,... | collective-permute-start | bytes 20 | tf_op jit(solution)/shard_map/ppermute | solution.py:20
  528.7 21.3 %collective-permute-start.73 = (f32[8,12,96]{2,0,1:T(8,128)S(1)}, f32[8,12,96]{2,0,1:T(8,128)S(1)}, u32[]{:S(2)}, u32[]{:S(2)}) collective-permute-start(f32[8,12,96]{2,0,1:T(8,128)S(1)} %bitcast.584), channel_id=1, source_target_pairs={{0,3},{1,2},{2,1},{3,0},{4,7},{5,6},{6,5},{7,4},{8,11},{9,10},{10,... | collective-permute-start | bytes 110600 | tf_op jit(solution)/shard_map/ppermute | solution.py:20
  530.3 19.7 %collective-permute-start.72 = (f32[8,12,96]{2,0,1:T(8,128)S(1)}, f32[8,12,96]{2,0,1:T(8,128)S(1)}, u32[]{:S(2)}, u32[]{:S(2)}) collective-permute-start(f32[8,12,96]{2,0,1:T(8,128)S(1)} %bitcast.585), channel_id=1, source_target_pairs={{0,2},{1,3},{2,0},{3,1},{4,6},{5,7},{6,4},{7,5},{8,10},{9,11},{10,... | collective-permute-start | bytes 110600 | tf_op jit(solution)/shard_map/ppermute | solution.py:20
  530.6 19.4 %collective-permute-start.71 = (f32[8,12,96]{2,0,1:T(8,128)S(1)}, f32[8,12,96]{2,0,1:T(8,128)S(1)}, u32[]{:S(2)}, u32[]{:S(2)}) collective-permute-start(f32[8,12,96]{2,0,1:T(8,128)S(1)} %bitcast.586), channel_id=1, source_target_pairs={{0,1},{1,0},{2,3},{3,2},{4,5},{5,4},{6,7},{7,6},{8,9},{9,8},{10,11... | collective-permute-start | bytes 110600 | tf_op jit(solution)/shard_map/ppermute | solution.py:20
  550.1 51.2 %collective-permute-start.80 = (f32[12,96]{1,0:T(8,128)S(1)}, f32[12,96]{1,0:T(8,128)S(1)}, u32[]{:S(2)}, u32[]{:S(2)}) collective-permute-start(f32[12,96]{1,0:T(8,128)S(1)} %bitcast.625), channel_id=1, source_target_pairs={{0,28},{4,24},{8,20},{12,16},{16,12},{20,8},{24,4},{28,0},{1,29},{... | collective-permute-start | bytes 13832 | tf_op jit(solution)/shard_map/ppermute | solution.py:20
  553.0 51.4 %collective-permute-start.79 = (f32[12,96]{1,0:T(8,128)S(1)}, f32[12,96]{1,0:T(8,128)S(1)}, u32[]{:S(2)}, u32[]{:S(2)}) collective-permute-start(f32[12,96]{1,0:T(8,128)S(1)} %bitcast.624), channel_id=1, source_target_pairs={{0,24},{4,28},{8,16},{12,20},{16,8},{20,12},{24,0},{28,4},{1,25},{... | collective-permute-start | bytes 13832 | tf_op jit(solution)/shard_map/ppermute | solution.py:20
  554.9 49.5 %collective-permute-start.78 = (f32[12,96]{1,0:T(8,128)S(1)}, f32[12,96]{1,0:T(8,128)S(1)}, u32[]{:S(2)}, u32[]{:S(2)}) collective-permute-start(f32[12,96]{1,0:T(8,128)S(1)} %bitcast.623), channel_id=1, source_target_pairs={{0,20},{4,16},{8,28},{12,24},{16,4},{20,0},{24,12},{28,8},{1,21},{... | collective-permute-start | bytes 13832 | tf_op jit(solution)/shard_map/ppermute | solution.py:20
  566.3 55.9 %collective-permute-start.93 = (bf16[2,4,2,96,256]{4,3,0,1,2:T(8,128)(2,1)}, bf16[2,4,2,96,256]{4,3,0,1,2:T(8,128)(2,1)}, u32[]{:S(2)}, u32[]{:S(2)}) collective-permute-start(bf16[2,4,2,96,256]{4,3,0,1,2:T(8,128)(2,1)} %fusion.70), channel_id=1, source_target_pairs={{0,1},{1,0},{2,3},{3,2},{4,5},{5,4},{6,7},{7,6},{8,9},{9,8},{10,11... | collective-permute-start | bytes 2359304 | tf_op jit(solution)/shard_map/ppermute | solution.py:20
  601.3 18.6 %collective-permute-start.77 = (f32[12,96]{1,0:T(8,128)S(1)}, f32[12,96]{1,0:T(8,128)S(1)}, u32[]{:S(2)}, u32[]{:S(2)}) collective-permute-start(f32[12,96]{1,0:T(8,128)S(1)} %bitcast.622), channel_id=1, source_target_pairs={{0,16},{4,20},{8,24},{12,28},{16,0},{20,4},{24,8},{28,12},{1,17},{... | collective-permute-start | bytes 13832 | tf_op jit(solution)/shard_map/ppermute | solution.py:20
  601.3 18.7 %collective-permute-start.76 = (f32[12,96]{1,0:T(8,128)S(1)}, f32[12,96]{1,0:T(8,128)S(1)}, u32[]{:S(2)}, u32[]{:S(2)}) collective-permute-start(f32[12,96]{1,0:T(8,128)S(1)} %bitcast.621), channel_id=1, source_target_pairs={{0,12},{4,8},{8,4},{12,0},{16,28},{20,24},{24,20},{28,16},{1,13},{... | collective-permute-start | bytes 13832 | tf_op jit(solution)/shard_map/ppermute | solution.py:20
  604.4 16.1 %collective-permute-start.75 = (f32[12,96]{1,0:T(8,128)S(1)}, f32[12,96]{1,0:T(8,128)S(1)}, u32[]{:S(2)}, u32[]{:S(2)}) collective-permute-start(f32[12,96]{1,0:T(8,128)S(1)} %bitcast.620), channel_id=1, source_target_pairs={{0,8},{4,12},{8,0},{12,4},{16,24},{20,28},{24,16},{28,20},{1,9},{5... | collective-permute-start | bytes 13832 | tf_op jit(solution)/shard_map/ppermute | solution.py:20
  604.4 16.2 %collective-permute-start.74 = (f32[12,96]{1,0:T(8,128)S(1)}, f32[12,96]{1,0:T(8,128)S(1)}, u32[]{:S(2)}, u32[]{:S(2)}) collective-permute-start(f32[12,96]{1,0:T(8,128)S(1)} %bitcast.619), channel_id=1, source_target_pairs={{0,4},{4,0},{8,12},{12,8},{16,20},{20,16},{24,28},{28,24},{1,5},{5... | collective-permute-start | bytes 13832 | tf_op jit(solution)/shard_map/ppermute | solution.py:20
  619.9 36.8 %collective-permute-start.99 = (bf16[2,768,768]{2,1,0:T(8,128)(2,1)}, bf16[2,768,768]{2,1,0:T(8,128)(2,1)S(1)}, u32[]{:S(2)}, u32[]{:S(2)}) collective-permute-start(bf16[2,768,768]{2,1,0:T(8,128)(2,1)} %pad_maximum_fusion.5), channel_id=1, source_target_pairs={{0,1},{1,0},{2,3},{3,2},{4,5},{5,4},{6,7},{7,6},{8,9},{9,8},{10,11... | collective-permute-start | bytes 7077896 | tf_op jit(solution)/shard_map/ppermute | solution.py:20
  620.0 39.3 %collective-permute-start.101 = (bf16[2,768,768]{2,1,0:T(8,128)(2,1)}, bf16[2,768,768]{2,1,0:T(8,128)(2,1)S(1)}, u32[]{:S(2)}, u32[]{:S(2)}) collective-permute-start(bf16[2,768,768]{2,1,0:T(8,128)(2,1)} %pad_maximum_fusion.6), channel_id=1, source_target_pairs={{0,1},{1,0},{2,3},{3,2},{4,5},{5,4},{6,7},{7,6},{8,9},{9,8},{10,11... | collective-permute-start | bytes 7077896 | tf_op jit(solution)/shard_map/ppermute | solution.py:20
  631.9 12.2 %collective-permute-start.88 = (bf16[2,4,96,256]{3,2,1,0:T(8,128)(2,1)S(1)}, bf16[2,4,96,256]{3,2,1,0:T(8,128)(2,1)S(1)}, u32[]{:S(2)}, u32[]{:S(2)}) collective-permute-start(bf16[2,4,96,256]{3,2,1,0:T(8,128)(2,1)S(1)} %fusion.90), channel_id=1, source_target_pairs={{0,4},{4,0},{8,12},{12,8},{16,20},{20,16},{24,28},{28,24},{1,5},{5... | collective-permute-start | bytes 1179656 | tf_op jit(solution)/shard_map/ppermute | solution.py:20
  650.2 15.3 %collective-permute-start.83 = (bf16[4,96,256]{2,1,0:T(8,128)(2,1)S(1)}, bf16[4,96,256]{2,1,0:T(8,128)(2,1)S(1)}, u32[]{:S(2)}, u32[]{:S(2)}) collective-permute-start(bf16[4,96,256]{2,1,0:T(8,128)(2,1)S(1)} %fusion.97), channel_id=1, source_target_pairs={{0,4},{4,0},{8,12},{12,8},{16,20},{20,16},{24,28},{28,24},{1,5},{5... | collective-permute-start | bytes 589832 | tf_op jit(solution)/shard_map/ppermute | solution.py:20
  654.3 12.2 %collective-permute-start.92 = (bf16[96,256]{1,0:T(8,128)(2,1)S(1)}, bf16[96,256]{1,0:T(8,128)(2,1)S(1)}, u32[]{:S(2)}, u32[]{:S(2)}) collective-permute-start(bf16[96,256]{1,0:T(8,128)(2,1)S(1)} %get-tuple-element.122), channel_id=1, source_target_pairs={{0,24},{4,28},{8,16},{12,20},{16,8},{20,12},{24,0},{28,4},{1,25},{... | collective-permute-start | bytes 147464 | tf_op jit(solution)/shard_map/ppermute | solution.py:20
  656.3 12.2 %collective-permute-start.91 = (bf16[96,256]{1,0:T(8,128)(2,1)S(1)}, bf16[96,256]{1,0:T(8,128)(2,1)S(1)}, u32[]{:S(2)}, u32[]{:S(2)}) collective-permute-start(bf16[96,256]{1,0:T(8,128)(2,1)S(1)} %get-tuple-element.123), channel_id=1, source_target_pairs={{0,16},{4,20},{8,24},{12,28},{16,0},{20,4},{24,8},{28,12},{1,17},{... | collective-permute-start | bytes 147464 | tf_op jit(solution)/shard_map/ppermute | solution.py:20
  659.4 29.1 %collective-permute-start.100 = (bf16[768,768]{1,0:T(8,128)(2,1)S(1)}, bf16[768,768]{1,0:T(8,128)(2,1)}, u32[]{:S(2)}, u32[]{:S(2)}) collective-permute-start(bf16[768,768]{1,0:T(8,128)(2,1)S(1)} %fusion.52), channel_id=1, source_target_pairs={{0,2},{1,3},{2,0},{3,1},{4,6},{5,7},{6,4},{7,5},{8,10},{9,11},{10,... | collective-permute-start | bytes 3538952 | tf_op jit(solution)/shard_map/ppermute | solution.py:20
  665.5 43.8 %collective-permute-start.102 = (bf16[768,768]{1,0:T(8,128)(2,1)S(1)}, bf16[768,768]{1,0:T(8,128)(2,1)}, u32[]{:S(2)}, u32[]{:S(2)}) collective-permute-start(bf16[768,768]{1,0:T(8,128)(2,1)S(1)} %fusion.53), channel_id=1, source_target_pairs={{0,2},{1,3},{2,0},{3,1},{4,6},{5,7},{6,4},{7,5},{8,10},{9,11},{10,... | collective-permute-start | bytes 3538952 | tf_op jit(solution)/shard_map/ppermute | solution.py:20
  (127 other events, 1566.6 us)

commit v2 on v1

v2 whole, which is shorter than its diff:
```python
import functools
import jax
import jax.numpy as jnp
from jax import lax
from jax.experimental import pallas as pl
from jax.experimental.pallas import tpu as pltpu
from jax.sharding import PartitionSpec as P

HD = 64
EPSILON = 1e-06
MASKED = -1000000000.0
BF = jnp.bfloat16
F32 = jnp.float32
LOG2E = 1.4426950408889634
MIB = 1 << 20


def dot(a, b, ca, cb):
    return lax.dot_general(a, b, (((ca,), (cb,)), ((), ())), preferred_element_type=F32)


def swap(value, k):
    n = lax.axis_size("tensor")
    return lax.ppermute(value, "tensor", [(i, i ^ k) for i in range(n)])


def to_all(v):
    return lax.all_to_all(v, "dp", split_axis=0, concat_axis=0, tiled=True)


def norm_parts(v):
    center = v - jnp.mean(v, axis=-1, keepdims=True)
    scale = lax.rsqrt(jnp.mean(center * center, axis=-1, keepdims=True) + EPSILON)
    return center * scale, scale


def norm_back(grad, n, scale, gain):
    gy = grad * gain
    return scale * (
        gy - jnp.mean(gy, -1, keepdims=True) - n * jnp.mean(gy * n, -1, keepdims=True)
    )


def col_sum(v):
    return jnp.sum(v, axis=0, keepdims=True)


def scores_of(q, k, keep):
    s = dot(q, k, 1, 1) * HD**-0.5
    return jnp.where(keep, s, MASKED)


def one_image(x, keep, w, gain, shift, heads):
    n, _ = norm_parts(x.astype(F32))
    h1 = (n * gain + shift).astype(BF)
    c = heads * HD
    qkv = dot(h1, w[:, : 3 * c], 1, 0).astype(BF)
    contexts, totals = [], []
    for h in range(heads):
        q, k, v = (qkv[:, i * c + h * HD : i * c + (h + 1) * HD] for i in range(3))
        s = scores_of(q, k, keep)
        top = jnp.max(s, -1, keepdims=True)
        total = top + jnp.log(jnp.sum(jnp.exp(s - top), -1, keepdims=True))
        contexts.append(dot(jnp.exp(s - total).astype(BF), v, 1, 0).astype(BF))
        totals.append(total)
    context = jnp.concatenate(contexts, 1)
    return qkv, context, jnp.concatenate(totals, 1), dot(context, w[:, 3 * c :], 1, 1)


def attn_fwd_kernel(heads, xa, xb, ka, kb, w_ref, gains, pa, pb, qa, qb, ca, cb, la, lb):
    w = w_ref[...]
    gain, shift = gains[0:1], gains[1:2]
    for x, k, p, q, c, total in ((xa, ka, pa, qa, ca, la), (xb, kb, pb, qb, cb, lb)):
        qkv, context, lse, part = one_image(x[0], k[0] > 0, w, gain, shift, heads)
        q[0], c[0], total[0], p[0] = qkv, context, lse, part.astype(p.dtype)


def whole(shape):
    return pl.BlockSpec(shape, lambda *i: (0,) * len(shape))


def each(shape):
    return pl.BlockSpec((1,) + shape, lambda i: (i,) + (0,) * len(shape))


def params(vmem):
    return pltpu.CompilerParams(vmem_limit_bytes=vmem * MIB)


def attn_fwd(xa, xb, ka, kb, w, gains, heads):
    images, rows, width = xa.shape
    c = heads * HD
    one = lambda shape, dtype: jax.ShapeDtypeStruct((images,) + shape, dtype)
    kinds = [((rows, 3 * c), BF), ((rows, c), BF), ((rows, heads), F32)]
    outs = [((rows, width), BF), ((rows, width), F32)] + [k for k in kinds for _ in range(2)]
    return pl.pallas_call(
        functools.partial(attn_fwd_kernel, heads),
        grid=(images,),
        in_specs=[each((rows, width))] * 2 + [each((1, rows))] * 2 + [whole(w.shape), whole(gains.shape)],
        out_specs=[each(s) for s, _ in outs],
        out_shape=[one(s, d) for s, d in outs],
        compiler_params=params(32),
        cost_estimate=pl.CostEstimate(
            flops=4 * images * rows * width * width, bytes_accessed=8 * images * rows * width, transcendentals=0
        ),
    )(xa, xb, ka, kb, w, gains)


def one_image_back(x, ga, qkv, context, lse, keep, w, gain, shift, heads):
    n, _ = norm_parts(x.astype(F32))
    h1 = (n * gain + shift).astype(BF)
    c = heads * HD
    gc_all = dot(ga, w[:, 3 * c :], 1, 0).astype(BF)
    parts = [[], [], []]
    for h in range(heads):
        q, k, v = (qkv[:, i * c + h * HD : i * c + (h + 1) * HD] for i in range(3))
        gc = gc_all[:, h * HD : (h + 1) * HD]
        p = jnp.exp(scores_of(q, k, keep) - lse[:, h : h + 1])
        gv = dot(p.astype(BF), gc, 0, 0)
        gp = dot(gc, v, 1, 1)
        delta = jnp.sum(p * gp, -1, keepdims=True)
        gs = (p * (gp - delta)).astype(BF)
        parts[0].append((dot(gs, k, 1, 0) * HD**-0.5).astype(BF))
        parts[1].append((dot(gs, q, 0, 0) * HD**-0.5).astype(BF))
        parts[2].append(gv.astype(BF))
    gqkv = jnp.concatenate(parts[0] + parts[1] + parts[2], 1)
    gh1 = dot(gqkv, w[:, : 3 * c], 1, 1)
    dw = jnp.concatenate([dot(h1, gqkv, 0, 0), dot(ga, context, 0, 0)], 1)
    return gh1, dw, col_sum(gh1 * n), col_sum(gh1)


def attn_bwd_kernel(heads, xa, xb, ga, gb, qa, qb, ca, cb, la, lb, ka, kb, w_ref, gains, dw_in, vec_in, ha, hb, dw, vec):
    @pl.when(pl.program_id(0) == 0)
    def _():
        dw[...] = dw_in[...]
        vec[...] = vec_in[...]

    w = w_ref[...]
    gain, shift = gains[0:1], gains[1:2]
    for x, g, q, c, total, k, out in ((xa, ga, qa, ca, la, ka, ha), (xb, gb, qb, cb, lb, kb, hb)):
        gh1, part, gg, gs = one_image_back(x[0], g[0], q[0], c[0], total[0], k[0] > 0, w, gain, shift, heads)
        out[0] = gh1.astype(out.dtype)
        dw[...] += part
        vec[0:1] += gg
        vec[1:2] += gs


def attn_bwd(xa, xb, ga, gb, qa, qb, ca, cb, la, lb, ka, kb, w, gains, dw, vec, heads, out_types):
    images, rows, width = xa.shape
    c = heads * HD
    specs = [each((rows, k)) for k in (width, width, 3 * c, c, heads) for _ in range(2)] + [each((1, rows))] * 2
    return pl.pallas_call(
        functools.partial(attn_bwd_kernel, heads),
        grid=(images,),
        in_specs=specs + [whole(v.shape) for v in (w, gains, dw, vec)],
        out_specs=[each((rows, width))] * 2 + [whole(dw.shape), whole(vec.shape)],
        out_shape=[jax.ShapeDtypeStruct(xa.shape, t) for t in out_types]
        + [jax.ShapeDtypeStruct(v.shape, F32) for v in (dw, vec)],
        compiler_params=params(40),
        cost_estimate=pl.CostEstimate(
            flops=10 * images * rows * width * width, bytes_accessed=16 * images * rows * width, transcendentals=0
        ),
    )(xa, xb, ga, gb, qa, qb, ca, cb, la, lb, ka, kb, w, gains, dw, vec)


def chosen(slot_row, slots):
    at = lax.broadcasted_iota(jnp.int32, (slots, slot_row.shape[1]), 0)
    return jnp.where(slot_row == at, 1.0, 0.0).astype(BF)


def dispatch_kernel(slots, x, p0, r1, r2, gains, router, slot, residual, probs, sent):
    res = x[...].astype(F32) + p0[...] + r1[...].astype(F32) + r2[...].astype(F32)
    residual[...] = res
    n, _ = norm_parts(res)
    h2 = (n * gains[2:3] + gains[3:4]).astype(BF)
    logits = dot(h2, router[...], 1, 1)
    grown = jnp.exp(logits - jnp.max(logits, -1, keepdims=True))
    probs[...] = grown / jnp.sum(grown, -1, keepdims=True)
    for e in range(slot.shape[0]):
        sent[e * slots : (e + 1) * slots] = dot(chosen(slot[e : e + 1], slots), h2, 1, 0).astype(BF)


def picks(place, total):
    at = lax.broadcasted_iota(jnp.int32, (place.shape[0], total), 1)
    return jnp.where(place == at, 1.0, 0.0)


def combine_kernel(slots, back, place, ids, probs_in, residual, teacher, mask, factor, slot, out, g_out, gl_out, loss, sent):
    probs = probs_in[...]
    experts = probs.shape[1]
    at = lax.broadcasted_iota(jnp.int32, probs.shape, 1)
    choose = [jnp.where(ids[:, j : j + 1] == at, 1.0, 0.0) for j in range(ids.shape[1])]
    gates = [jnp.sum(c * probs, -1, keepdims=True) for c in choose]
    picked = [dot(picks(place[:, j : j + 1], back.shape[0]).astype(BF), back[...], 1, 0) for j in range(len(gates))]
    result = residual[...]
    result = result + sum(gate * p for gate, p in zip(gates, picked))
    out[...] = result.astype(BF)
    errors = result - teacher[...].astype(F32)
    m = mask[...]
    row_loss = jnp.mean(errors * errors, -1, keepdims=True) * m
    loss[...] = jnp.broadcast_to(col_sum(row_loss), loss.shape)
    g = m * errors * factor[0:1, 0:1]
    g_out[...] = g
    grad_probs = sum(c * jnp.sum(g * p, -1, keepdims=True) for c, p in zip(choose, picked))
    grad_logits = probs * (grad_probs - jnp.sum(probs * grad_probs, -1, keepdims=True))
    gl_out[...] = grad_logits.astype(BF)
    for e in range(experts):
        gated = (probs[:, e : e + 1] * g).astype(BF)
        sent[e * slots : (e + 1) * slots] = dot(chosen(slot[e : e + 1], slots), gated, 1, 0).astype(BF)


def back_kernel(back, place, residual, g, gl, gains, router, grad_residual, grad_attn, vec, grad_router):
    either = sum(picks(place[:, j : j + 1], back.shape[0]) for j in range(place.shape[1])).astype(BF)
    grad_h2 = dot(either, back[...], 1, 0) + dot(gl[...], router[...], 1, 0)
    n, scale = norm_parts(residual[...])
    gain = gains[2:3]
    h2 = (n * gain + gains[3:4]).astype(BF)
    vec[0:1] = col_sum(grad_h2 * n)
    vec[1:2] = col_sum(grad_h2)
    grad_router[...] = dot(gl[...], h2, 0, 0)
    total = g[...] + norm_back(grad_h2, n, scale, gain)
    grad_residual[...] = total
    grad_attn[...] = total.astype(BF)


def last_kernel(x, p0, r1, r2, gains, grad_residual, out):
    grad_h1 = p0[...] + r1[...].astype(F32) + r2[...].astype(F32)
    n, scale = norm_parts(x[...].astype(F32))
    out[...] = grad_residual[...] + norm_back(grad_h1, n, scale, gains[0:1])


def plain(kernel, outs, *args, vmem=32, flops=1 << 30):
    return pl.pallas_call(
        kernel,
        out_shape=[jax.ShapeDtypeStruct(s, d) for s, d in outs],
        compiler_params=params(vmem),
        cost_estimate=pl.CostEstimate(flops=flops, bytes_accessed=8 * MIB, transcendentals=0),
    )(*args)


TAIL_AT = 0.33 * 0.7071067811865476
TAIL = (
    -0.06767145544290543,
    0.23011283576488495,
    -0.17556501924991608,
    0.20424090325832367,
    0.02361520379781723,
    0.10061042755842209,
    0.09147822111845016,
    0.0931788831949234,
)


def gelu_parts(u):
    bell = jnp.exp2(u * u * (-0.5 * LOG2E))
    t = 1.0 / (1.0 + TAIL_AT * jnp.abs(u))
    poly = TAIL[0]
    for c in TAIL[1:]:
        poly = poly * t + c
    tail = t * poly * bell
    phi = jnp.where(u < 0, tail, 1.0 - tail)
    return u * phi, phi + u * bell * 0.3989422804014327


def expert_fwd_kernel(n, x, *refs):
    ups, downs, (out, hidden, slope) = refs[:n], refs[n : 2 * n], refs[2 * n :]
    total = None
    f = ups[0].shape[1]
    for t in range(n):
        value, der = gelu_parts(dot(x[...], ups[t][...], 1, 0))
        value = value.astype(BF)
        hidden[:, t * f : (t + 1) * f] = value
        slope[:, t * f : (t + 1) * f] = der.astype(BF)
        part = dot(value, downs[t][...], 1, 1)
        total = part if total is None else total + part
    out[...] = total.astype(BF)


def expert_bwd_kernel(n, go, slope, *refs):
    ups, downs, (grad_up, out) = refs[:n], refs[n : 2 * n], refs[2 * n :]
    total = None
    f = ups[0].shape[1]
    for t in range(n):
        at = slice(t * f, (t + 1) * f)
        gu = (dot(go[...], downs[t][...], 1, 0) * slope[:, at].astype(F32)).astype(BF)
        grad_up[:, at] = gu
        part = dot(gu, ups[t][...], 1, 1)
        total = part if total is None else total + part
    out[...] = total.astype(BF)


def over_rows(kernel, ins, weights, widths, step):
    rows = ins[0].shape[0]
    block = lambda k: pl.BlockSpec((step, k), lambda i: (i, 0))
    fixed = lambda s: pl.BlockSpec(s, lambda i: (0, 0), pipeline_mode=pl.Buffered(1))
    return pl.pallas_call(
        kernel,
        grid=(rows // step,),
        in_specs=[block(v.shape[1]) for v in ins] + [fixed(w.shape) for w in weights],
        out_specs=[block(k) for k in widths],
        out_shape=[jax.ShapeDtypeStruct((rows, k), BF) for k in widths],
        compiler_params=params(48),
        cost_estimate=pl.CostEstimate(
            flops=2 * rows * sum(w.size for w in weights), bytes_accessed=32 * MIB, transcendentals=0
        ),
    )(*ins, *weights)


def after(value, *others):
    return lax.optimization_barrier((value,) + others)[0]


def local(
    tokens,
    teacher,
    valid_mask,
    expert_ids,
    attn_gain,
    attn_shift,
    qkv_weight,
    proj_weight,
    moe_gain,
    moe_shift,
    router_weight,
    up_weight,
    down_weight,
):
    rows, width = tokens.shape
    length = valid_mask.shape[1]
    images = rows // length
    experts = router_weight.shape[1]
    top = expert_ids.shape[1]
    capacity = max(2, (top * rows + experts - 1) // experts * 5 // 4)
    slots = -(-capacity // 16) * 16
    padded = -(-length // 16) * 16
    own = images * padded
    n_dp = lax.axis_size("dp")
    n_tensor = lax.axis_size("tensor")
    tensor_me = lax.axis_index("tensor")
    heads_width = proj_weight.shape[1]
    heads = heads_width // HD

    def pad(v, value=0):
        v = v.reshape((images, length) + v.shape[1:])
        return jnp.pad(v, ((0, 0), (0, padded - length)) + ((0, 0),) * (v.ndim - 2), constant_values=value)

    def unpad(v):
        return v.reshape(images, padded, -1)[:, :length].reshape(rows, -1)

    x0 = pad(tokens)
    x1 = swap(x0, 1)
    x2 = swap(x0, 2)
    x3 = swap(x2, 1)
    x = (x0, x1, x2, x3)

    dense_rows = proj_weight.shape[0]
    valid_here = jnp.sum(valid_mask)
    count_parts = jnp.stack([valid_here // 128, valid_here % 128]).astype(BF)
    vectors = jnp.concatenate([attn_gain, attn_shift, moe_gain, moe_shift, count_parts])
    extra = jnp.concatenate([jnp.pad(vectors, (0, width - vectors.size)), router_weight.T.reshape(-1)])
    shard = jnp.concatenate(
        [jnp.concatenate([qkv_weight.reshape(-1, 3 * heads_width), proj_weight], 1), extra.reshape(-1, width)], 0
    )
    got = to_all(jnp.broadcast_to(shard[None], (n_dp,) + shard.shape))
    w = got[:, :dense_rows].reshape(width, width)
    extras = got[:, dense_rows]
    gains = extras[:, : 4 * dense_rows].reshape(n_dp, 4, dense_rows).swapaxes(0, 1).reshape(4, width).astype(F32)
    counts = jnp.sum(extras[:, 4 * dense_rows : 4 * dense_rows + 2].astype(F32), 0)
    count = counts[0] * 128 + counts[1]
    router = got[:, dense_rows + 1].reshape(n_dp, experts, dense_rows).swapaxes(0, 1).reshape(experts, width)

    up0, down0 = after((up_weight[0], down_weight[0]), x2)
    up2 = swap(up0, 2)
    down2 = swap(after(down0, up2), 2)
    ups = (up0, swap(up0, 1), up2, swap(up2, 1))
    downs = (down0, swap(down0, 1), down2, swap(down2, 1))

    mask = jnp.pad(valid_mask, ((0, 0), (0, padded - length))).reshape(n_tensor, images, 1, padded)
    masks = [lax.dynamic_index_in_dim(mask, tensor_me ^ k, 0, keepdims=False) for k in range(4)]
    row_mask = masks[0].reshape(own, 1).astype(F32)
    ids = pad(expert_ids, -1).reshape(own, top)
    each_expert = lax.iota(jnp.int32, experts)
    named = ids[:, :, None] == each_expert
    names = jnp.any(named, axis=1)
    row_at = lax.iota(jnp.int32, own)
    before = (row_at[:, None] > row_at[None, :]).astype(BF)
    slot = jnp.where(names, dot(before, names.astype(BF), 1, 0).astype(jnp.int32), -1)
    place = jnp.where(ids < 0, -1, ids * slots + jnp.sum(jnp.where(named, slot[:, None, :], 0), -1))
    slot = slot.T

    p3, p2, q3, q2, c3, c2, l3, l2 = attn_fwd(x3, x2, masks[3], masks[2], w, gains, heads)
    far = (p2 + swap(p3, 1).astype(F32)).astype(BF)
    r2 = swap(far, 2)
    p1, p0, q1, q0, c1, c0, l1, l0 = attn_fwd(x1, x0, masks[1], masks[0], w, gains, heads)
    r1 = swap(p1, 1)
    flat = lambda v: v.reshape(own, v.shape[-1])
    row_f32 = ((own, width), F32)
    row_bf = ((own, width), BF)
    all_slots = ((experts * slots, width), BF)
    residual, probs, sent = plain(
        functools.partial(dispatch_kernel, slots),
        [row_f32, ((own, experts), F32), all_slots],
        *(flat(x0), flat(p0), flat(r1), flat(r2), gains, router, slot),
    )

    exchange = lambda v: to_all(v.reshape(n_dp, slots, width)).reshape(n_dp * slots, width)
    arrived = exchange(sent)
    step = min(256, n_dp * slots)
    hidden_width = n_tensor * up0.shape[1]
    out, hidden, slope = over_rows(
        functools.partial(expert_fwd_kernel, n_tensor), (arrived,), ups + downs, (width, hidden_width, hidden_width), step
    )
    returned = exchange(out)
    factor = jnp.full((1, 128), rows * n_dp * n_tensor / count, F32)
    result, g, grad_logits, loss_part, grad_sent = plain(
        functools.partial(combine_kernel, slots),
        [row_bf, row_f32, ((own, experts), BF), ((1, 128), F32), all_slots],
        *(returned, place, ids, probs, residual, flat(pad(teacher)), row_mask, factor, slot),
    )
    grad_out = exchange(grad_sent)
    grad_up, grad_arrived = over_rows(
        functools.partial(expert_bwd_kernel, n_tensor), (grad_out, slope), ups + downs, (hidden_width, width), step
    )
    grad_back = exchange(grad_arrived)

    f = up0.shape[1]
    cut = lambda v, t: v[:, t * f : (t + 1) * f]

    def expert_sums(part):
        kept2 = part(2) + swap(part(3).astype(BF), 1).astype(F32)
        own_part = part(0) + swap(part(1).astype(BF), 1).astype(F32)
        return own_part, kept2.astype(BF)

    down_own, down_far = expert_sums(lambda t: dot(grad_out, cut(hidden, t), 0, 0))
    up_own, up_far = expert_sums(lambda t: dot(arrived, cut(grad_up, t), 0, 0))

    grad_residual, grad_attn, vec_two, grad_router = plain(
        back_kernel,
        [row_f32, row_bf, ((2, width), F32), ((experts, width), F32)],
        *(grad_back, place, residual, g, grad_logits, gains, router),
    )

    g0 = grad_attn.reshape(x0.shape)
    g1 = swap(g0, 1)
    g2 = swap(g0, 2)
    g3 = swap(g2, 1)
    grad_down_w = down_own + swap(down_far, 2).astype(F32)
    grad_up_w = up_own + swap(after(up_far, g2), 2).astype(F32)
    dw = jnp.zeros(w.shape, F32)
    vec_one = jnp.zeros((2, width), F32)
    h1, h0, dw, vec_one = attn_bwd(
        *(x1, x0, g1, g0, q1, q0, c1, c0, l1, l0, masks[1], masks[0], w, gains, dw, vec_one, heads, (BF, F32))
    )
    h3, h2, dw, vec_one = attn_bwd(
        *(x3, x2, g3, g2, q3, q2, c3, c2, l3, l2, masks[3], masks[2], w, gains, dw, vec_one, heads, (BF, F32))
    )
    t1 = swap(h1, 1)
    t2 = swap((h2 + swap(h3, 1).astype(F32)).astype(BF), 2)
    dense = to_all(dw.astype(BF).reshape(n_dp, dense_rows, width)).astype(F32).sum(0)
    [grad_tokens] = plain(
        last_kernel, [row_f32], *(flat(x0), flat(h0), flat(t1), flat(t2), gains, grad_residual)
    )

    small = jnp.concatenate([vec_one, vec_two, grad_router]).reshape(4 + experts, n_dp, dense_rows).swapaxes(0, 1)
    small = small.reshape(n_dp, -1)
    small = jnp.concatenate([small, jnp.broadcast_to(loss_part[:, :1], (n_dp, 1))], 1)
    size = small.shape[1]
    lanes = -(-size // 1024) * 1024
    small = jnp.pad(small, ((0, 0), (0, lanes - size))).reshape(n_dp, lanes // 128, 128)
    small = to_all(small).sum(0)
    small = small + swap(small, 1)
    small = (small + swap(small, 2)).reshape(-1)
    loss = small[size - 1] / count
    small = small[: size - 1].reshape(4 + experts, dense_rows)
    return (
        loss,
        unpad(result),
        unpad(grad_tokens),
        small[0],
        small[1],
        dense[:, : 3 * heads_width].reshape(-1, 3, heads_width),
        dense[:, 3 * heads_width :],
        small[2],
        small[3],
        small[4:].T,
        grad_up_w[None],
        grad_down_w[None],
    )


def solution(mesh):
    rows = P(("dp", "tensor"), None)
    experts = P("dp", None, "tensor")
    in_specs = (
        rows,
        rows,
        P("dp", None),
        rows,
        P("dp"),
        P("dp"),
        experts,
        P("dp", "tensor"),
        P("dp"),
        P("dp"),
        P("dp", None),
        experts,
        experts,
    )
    out_specs = (
        P(),
        rows,
        rows,
        P("dp"),
        P("dp"),
        experts,
        P("dp", "tensor"),
        P("dp"),
        P("dp"),
        P("dp", None),
        experts,
        experts,
    )
    return jax.shard_map(local, mesh=mesh, in_specs=in_specs, out_specs=out_specs, check_vma=False)
```

time: 725 us -> 461 us (0.64)
  starting transfers between devices: 167 us -> 43.5 us
  matrix products: 137 us -> 37.4 us
  Pallas kernels: 0 us -> 81.7 us
  local copies, waits for them, and re-layouts: 129 us -> 50.3 us
  other arithmetic: 72.6 us -> 9.57 us
  blocking collectives: 0 us -> 40.9 us
  waiting for transfers between devices: 193 us -> 182 us
  between operations: 16.4 us -> 7.5 us
    ppermute x103 -> x26, starting transfers between devices: 167 us -> 13.6 us  [swap(): return lax.ppermute(value, 'tensor', [(i, i ^ k) for i in range(n)])]
    ppermute x103 -> x26, waiting for transfers between devices: 193 us -> 99.1 us  [swap(): return lax.ppermute(value, 'tensor', [(i, i ^ k) for i in range(n)])]
    all_to_all x0 -> x6, waiting for transfers between devices: none -> 82.9 us  [to_all(): return lax.all_to_all(v, 'dp', split_axis=0, concat_axis=0, tiled=True)]
    pallas_call x0 -> x10, Pallas kernels: none -> 81.7 us  [the longest x2 39.2 us: over_rows(): pl.pallas_call(kernel, grid=(rows // step,), in_specs=[block(v.shape[1])...]
    dot_general x32 -> x9, matrix products: 105 us -> 37.4 us  [dot(): lax.dot_general(a, b, (((ca,), (cb,)), ((), ())), preferred_element_type=...]
    all_to_all x0 -> x1, blocking collectives: none -> 40.9 us  [to_all(): return lax.all_to_all(v, 'dp', split_axis=0, concat_axis=0, tiled=True)]
    dot_general x13 -> x0, matrix products: 32 us -> none  [the longest x1 6.37 us: local(): jnp.einsum('trc,tdc->rd', grad_qkv, dense[:, :, :3 * heads_width], prefer...]
    all_to_all x0 -> x6, starting transfers between devices: none -> 30 us  [to_all(): return lax.all_to_all(v, 'dp', split_axis=0, concat_axis=0, tiled=True)]
  transfers between devices with their start and end apart: 103 -> 32, of which waited for: 44 -> 12; matrix products, arithmetic and copies ran while one was open for 37% -> 13% of each run, Pallas kernels for 0% -> 9%
where the time goes in v2:
time: 461 us; the launch traced here: 453 us
  waiting for transfers between devices  182 us (39%)
  Pallas kernels  81.7 us (18%)
  local copies, waits for them, and re-layouts  50.3 us (11%)
  starting transfers between devices  43.5 us (9%)
  blocking collectives  40.9 us (9%)
  matrix products  37.4 us (8%)
  other arithmetic  9.57 us (2%)
  between operations  7.5 us (2%)
    ppermute x26, waiting for transfers between devices, swap(): return lax.ppermute(value, 'tensor', [(i, i ^ k) for i in range(n)])  99.1 us
    all_to_all x6, waiting for transfers between devices, to_all(): return lax.all_to_all(v, 'dp', split_axis=0, concat_axis=0, tiled=True)  82.9 us
    all_to_all x1, blocking collectives, to_all(): return lax.all_to_all(v, 'dp', split_axis=0, concat_axis=0, tiled=True)  40.9 us
    pallas_call x2, Pallas kernels, over_rows(): pl.pallas_call(kernel, grid=(rows // step,), in_specs=[block(v.shape[1])...  39.2 us
    dot_general x9, matrix products, dot(): lax.dot_general(a, b, (((ca,), (cb,)), ((), ())), preferred_element_type=...  37.4 us
    unnamed x151, local copies, waits for them, and re-layouts  30.4 us
    all_to_all x6, starting transfers between devices, to_all(): return lax.all_to_all(v, 'dp', split_axis=0, concat_axis=0, tiled=True)  30 us
    pallas_call x2, Pallas kernels, attn_bwd(): pl.pallas_call(functools.partial(attn_bwd_kernel, heads), grid=(images,),...  22.7 us
  transfers between devices with their start and end apart: 32, of which 12 were waited for; matrix products, arithmetic and copies ran while one was open for 13% of the time, Pallas kernels for 9%

profile of v2, /device:TPU:0, one launch (start us, length us, event | category | flops | bytes accessed | tf_op | source)
XLA Modules:
  0.0 452.9 jit_solution(12407927392890529490)
XLA Ops:
  0.6 1.3 reduce_sum.45
  5.4 2.8 concatenate.20
  10.7 1.1 broadcast_in_dim.50
  11.8 7.4 %all-to-all-start = ((bf16[8,98,768]{2,1,0:T(8,128)(2,1)}), bf16[8,98,768]{2,1,0:T(8,128)(2,1)}, u32[]{:S(2)}, u32[]{:S(2)}) async-start(bf16[8,98,768]{2,1,0:T(8,128)(2,1)} %broadcast_in_dim.50), calls=%async_computation | async-start | bytes 2555904 | tf_op jit(solution)/shard_map/all_to_all | solution.py:28
  19.4 1.6 collective-permute-start
  21.0 14.3 %collective-permute-done.xb = bf16[2,208,768]{2,1,0:T(8,128)(2,1)S(1)} collective-permute-done((bf16[2,208,768]{2,1,0:T(8,128)(2,1)S(1)}, bf16[2,208,768]{2,1,0:T(8,128)(2,1)S(1)}, u32[]{:S(2)}, u32[]{:S(2)}) %collective-permute-start) | collective-permute-done | bytes 639008 | tf_op jit(solution)/shard_map/ppermute | solution.py:24
  35.3 14.7 %all-to-all-done = bf16[8,98,768]{2,1,0:T(8,128)(2,1)} async-done(((bf16[8,98,768]{2,1,0:T(8,128)(2,1)}), bf16[8,98,768]{2,1,0:T(8,128)(2,1)}, u32[]{:S(2)}, u32[]{:S(2)}) %all-to-all-start) | async-done | bytes 1204256 | tf_op jit(solution)/shard_map/all_to_all | solution.py:28
  51.7 1.3 slice.114
  54.0 1.1 copy-done.31
  55.0 1.1 copy-done.34
  56.1 5.7 %shard_map.221 = (bf16[2,208,768]{2,1,0:T(8,128)(2,1)}, f32[2,208,768]{2,1,0:T(8,128)S(1)}, bf16[2,208,576]{2,1,0:T(8,128)(2,1)S(1)}, bf16[2,208,576]{2,1,0:T(8,...) custom-call(bf16[2,208,768]{2,1,0:T(8,128)(2,1)S(1)} %copy-done.34, ...), custom_call_target="tpu_custom_call" | custom-call | flops 981467136 | bytes 2555904 | tf_op jit(solution)/shard_map/pallas_call | solution.py:96
  65.5 1.6 collective-permute-start.7
  67.1 6.8 %shard_map.220 = (bf16[2,208,768]{2,1,0:T(8,128)(2,1)}, f32[2,208,768]{2,1,0:T(8,128)S(1)}, bf16[2,208,576]{2,1,0:T(8,128)(2,1)S(1)}, bf16[2,208,576]{2,1,0:T(8,...) custom-call(bf16[2,208,768]{2,1,0:T(8,128)(2,1)} %collective-permute, ...), custom_call_target="tpu_custom_call" | custom-call | flops 981467136 | bytes 2555904 | tf_op jit(solution)/shard_map/pallas_call | solution.py:96
  76.2 2.5 add_convert_fusion.3
  81.0 26.9 %collective-permute-done.5 = bf16[2,208,768]{2,1,0:T(8,128)(2,1)S(1)} collective-permute-done((bf16[2,208,768]{2,1,0:T(8,128)(2,1)}, bf16[2,208,768]{2,1,0:T(8,128)(2,1)S(1)}, u32[]{:S(2)}, u32[]{:S(2)}) %collective-permute-start.5) | collective-permute-done | bytes 639008 | tf_op jit(solution)/shard_map/ppermute | solution.py:24
  107.8 1.1 copy-done.39
  108.9 1.3 copy-done.41
  110.2 1.6 shard_map.222
  112.5 1.1 copy-done.3
  113.7 4.9 %all-to-all-start.1 = ((bf16[8,128,768]{2,1,0:T(8,128)(2,1)}), bf16[8,128,768]{2,1,0:T(8,128)(2,1)}, u32[]{:S(2)}, u32[]{:S(2)}) async-start(bf16[8,128,768]{2,1,0:T(8,128)(2,1)} %bitcast.91), calls=%async_computation.1 | async-start | bytes 3145728 | tf_op jit(solution)/shard_map/all_to_all | solution.py:28
  118.6 1.6 collective-permute-start.10
  120.7 25.7 %collective-permute-done.10.refs_6_ = bf16[768,768]{1,0:T(8,128)(2,1)S(1)} collective-permute-done((bf16[768,768]{1,0:T(8,128)(2,1)}, bf16[768,768]{1,0:T(8,128)(2,1)S(1)}, u32[]{:S(2)}, u32[]{:S(2)}) %collective-permute-start.10) | collective-permute-done | bytes 1179680 | tf_op jit(solution)/shard_map/ppermute | solution.py:24
  149.5 6.2 %all-to-all-done.1 = bf16[8,128,768]{2,1,0:T(8,128)(2,1)} async-done(((bf16[8,128,768]{2,1,0:T(8,128)(2,1)}), bf16[8,128,768]{2,1,0:T(8,128)(2,1)}, u32[]{:S(2)}, u32[]{:S(2)}) %all-to-all-start.1) | async-done | bytes 1572896 | tf_op jit(solution)/shard_map/all_to_all | solution.py:28
  155.7 1.3 copy-done.22
  157.0 1.3 copy-done.25
  158.2 1.3 copy-done.28
  159.5 23.6 %shard_map.223 = (bf16[1024,768]{1,0:T(8,128)(2,1)}, bf16[1024,3072]{1,0:T(8,128)(2,1)}, bf16[1024,3072]{1,0:T(8,128)(2,1)}) custom-call(bf16[1024,768]{1,0:T(8,128)(2,1)} %bitcast.19.x, bf16[768,768]{1,0:T(8,128)(2,1)S(1)} %bitcast.108, bf16[768,768]{1,0:T(8,128)(2,1)S(1)} %copy-done.25, bf16[768,768]{1,0:T(8,128)(2,1)} %collective-permute-done.7.refs_2_, ...), custom_call_target="tpu_custom_call" | custom-call | flops 9663676416 | bytes 33554432 | tf_op jit(solution)/shard_map/pallas_call | solution.py:296
  183.1 3.6 all-to-all-start.2
  187.8 2.0 reshape.188
  189.8 1.9 pad.28
  195.3 28.5 %all-to-all-done.2 = bf16[8,128,768]{2,1,0:T(8,128)(2,1)S(1)} async-done(((bf16[8,128,768]{2,1,0:T(8,128)(2,1)}), bf16[8,128,768]{2,1,0:T(8,128)(2,1)S(1)}, u32[]{:S(2)}, u32[]{:S(2)}) %all-to-all-start.2) | async-done | bytes 1572896 | tf_op jit(solution)/shard_map/all_to_all | solution.py:28
  223.9 1.1 copy-done.2
  225.9 3.1 shard_map.224
  229.0 40.9 %all_to_all.35 = bf16[8,128,768]{2,1,0:T(8,128)(2,1)} all-to-all(bf16[8,128,768]{2,1,0:T(8,128)(2,1)S(1)} %bitcast.92), channel_id=1, replica_groups=mesh['dp'=8,'tensor'=4] {'dp'}, dimensions={0} | all-to-all | bytes 3145728 | tf_op jit(solution)/shard_map/all_to_all | solution.py:28
  270.0 15.7 %shard_map.225 = (bf16[1024,3072]{1,0:T(8,128)(2,1)}, bf16[1024,768]{1,0:T(8,128)(2,1)}) custom-call(bf16[1024,768]{1,0:T(8,128)(2,1)} %bitcast.121, bf16[1024,3072]{1,0:T(8,128)(2,1)} %get-tuple-element.69.slope, bf16[768,768]{1,0:T(8,128)(2,1)S(1)} %bitcast.109, bf16[768,768]{1,0:T(8,128)(2,1)S(1)} %copy-done.26, ...), custom_call_target="tpu_custom_call" | custom-call | flops 9663676416 | bytes 33554432 | tf_op jit(solution)/shard_map/pallas_call | solution.py:296
  285.7 3.8 all-to-all-start.4
  289.6 4.4 fusion.25
  294.0 32.2 %all-to-all-done.4 = bf16[8,128,768]{2,1,0:T(8,128)(2,1)S(1)} async-done(((bf16[8,128,768]{2,1,0:T(8,128)(2,1)}), bf16[8,128,768]{2,1,0:T(8,128)(2,1)S(1)}, u32[]{:S(2)}, u32[]{:S(2)}) %all-to-all-start.4) | async-done | bytes 1572896 | tf_op jit(solution)/shard_map/all_to_all | solution.py:28
  326.1 1.3 copy-done.11
  327.4 1.6 shard_map.226
  329.1 1.6 collective-permute-start.12
  330.6 3.9 fusion.22
  335.1 4.3 fusion.19
  339.4 4.3 collective-permute-done.12.gb
  343.8 4.3 add_convert_fusion
  348.1 1.5 collective-permute-start.25
  350.0 11.7 %shard_map.227 = (bf16[2,208,768]{2,1,0:T(8,128)(2,1)S(1)}, f32[2,208,768]{2,1,0:T(8,128)S(1)}, f32[768,768]{1,0:T(8,128)S(1)}, f32[2,768]{1,0:T(2,128)S(1)}) custom-call(bf16[2,208,768]{2,1,0:T(8,128)(2,1)} %collective-permute-done.2.xa, bf16[2,208,768]{2,1,0:T(8,128)(2,1)S(1)} %copy-done.1, bf16[2,208,768]{2,1,0:T(8,128)(2,1)S(1)} %collective-permute-done.14.ga, ...), custom_call_target="tpu_custom_call" | custom-call | flops 2453667840 | bytes 5111808 | tf_op jit(solution)/shard_map/pallas_call | solution.py:152
  363.7 10.9 %shard_map.228 = (bf16[2,208,768]{2,1,0:T(8,128)(2,1)}, f32[2,208,768]{2,1,0:T(8,128)S(1)}, f32[768,768]{1,0:T(8,128)S(1)}, f32[2,768]{1,0:T(2,128)S(1)}) custom-call(bf16[2,208,768]{2,1,0:T(8,128)(2,1)S(1)} %copy-done.35, bf16[2,208,768]{2,1,0:T(8,128)(2,1)S(1)} %copy-done.32, bf16[2,208,768]{2,1,0:T(8,128)(2,1)S(1)} %collective-permute-done.13.ga, ...), custom_call_target="tpu_custom_call" | custom-call | flops 2453667840 | bytes 5111808 | tf_op jit(solution)/shard_map/pallas_call | solution.py:152
  376.5 5.4 %all-to-all-start.5 = ((f32[8,16,128]{2,1,0:T(8,128)}), f32[8,16,128]{2,1,0:T(8,128)S(1)}, u32[]{:S(2)}, u32[]{:S(2)}) async-start(f32[8,16,128]{2,1,0:T(8,128)} %copy.100), calls=%async_computation.5 | async-start | bytes 131072 | tf_op jit(solution)/shard_map/all_to_all | solution.py:28
  381.9 4.4 fusion.16
  386.3 1.1 convert_element_type.98
  387.4 1.4 all-to-all-done.5
  388.8 4.9 %all-to-all-start.6 = ((bf16[8,96,768]{2,1,0:T(8,128)(2,1)}), bf16[8,96,768]{2,1,0:T(8,128)(2,1)}, u32[]{:S(2)}, u32[]{:S(2)}) async-start(bf16[8,96,768]{2,1,0:T(8,128)(2,1)} %bitcast.120), calls=%async_computation.6 | async-start | bytes 2359296 | tf_op jit(solution)/shard_map/all_to_all | solution.py:28
  393.7 4.7 %add_convert_fusion.1 = bf16[768,768]{1,0:T(8,128)(2,1)} fusion(bf16[768,768]{1,0:T(8,128)(2,1)} %collective-permute-done.21, bf16[1024,768]{1,0:T(8,128)(2,1)} %bitcast.19.x, bf16[1024,3072]{1,0:T(8,128)(2,1)} %get-tuple-element.99), kind=kOutput, calls=%fused_computation.3 | convolution fusion | flops 1209729024 | bytes 5505024 | tf_op jit(solution)/shard_map/dot_general | solution.py:19
  398.5 1.3 collective-permute-start.22
  399.8 1.2 collective-permute-done.15
  403.0 5.5 %add_bitcast_fusion = f32[1,768,768]{2,1,0:T(8,128)} fusion(bf16[768,768]{1,0:T(8,128)(2,1)} %collective-permute-done.25, bf16[768,768]{1,0:T(8,128)(2,1)} %collective-permute-done.23, bf16[1024,768]{1,0:T(8,128)(2,1)} %bitcast.123, bf16[1024,3072]{1,0:T(8,128)(2,1)} %get-tuple-element.101), kind=kOutput, calls=%fused_computation | convolution fusion | flops 1210318848 | bytes 7864320 | tf_op jit(solution)/shard_map/dot_general | solution.py:19
  408.6 18.4 %collective-permute-done.16 = f32[16,128]{1,0:T(8,128)S(1)} collective-permute-done((f32[16,128]{1,0:T(8,128)S(1)}, f32[16,128]{1,0:T(8,128)S(1)}, u32[]{:S(2)}, u32[]{:S(2)}) %collective-permute-start.16) | collective-permute-done | bytes 8224 | tf_op jit(solution)/shard_map/ppermute | solution.py:24
  428.9 1.2 add_convert_fusion.2
  430.1 1.4 collective-permute-start.19
  432.0 5.6 %add_bitcast_fusion.1 = f32[1,768,768]{2,1,0:T(8,128)} fusion(bf16[768,768]{1,0:T(8,128)(2,1)} %collective-permute-done.22, bf16[768,768]{1,0:T(8,128)(2,1)} %collective-permute-done.20, bf16[1024,768]{1,0:T(8,128)(2,1)} %bitcast.19.x, bf16[1024,3072]{1,0:T(8,128)(2,1)} %get-tuple-element.99), kind=kOutput, calls=%fused_computation.2 | convolution fusion | flops 1210318848 | bytes 7864320 | tf_op jit(solution)/shard_map/dot_general | solution.py:19
  437.7 8.3 %collective-permute-done.19 = bf16[2,208,768]{2,1,0:T(8,128)(2,1)S(1)} collective-permute-done((bf16[2,208,768]{2,1,0:T(8,128)(2,1)S(1)}, bf16[2,208,768]{2,1,0:T(8,128)(2,1)S(1)}, u32[]{:S(2)}, u32[]{:S(2)}) %collective-permute-start.19) | collective-permute-done | bytes 639008 | tf_op jit(solution)/shard_map/ppermute | solution.py:24
  447.1 1.1 reshape.205
  448.2 1.5 convert_reduce_fusion
  (238 shorter events, 34.3 us)
Async XLA Ops:
  11.8 7.4 %copy-start.67 = (bf16[394,768]{1,0:T(8,128)(2,1)S(1)}, bf16[394,768]{1,0:T(8,128)(2,1)}, u32[]{:S(2)}) copy-start(bf16[394,768]{1,0:T(8,128)(2,1)} %param.13) | copy-start | bytes 1815556
  11.8 38.2 %all-to-all-start = ((bf16[8,98,768]{2,1,0:T(8,128)(2,1)}), bf16[8,98,768]{2,1,0:T(8,128)(2,1)}, u32[]{:S(2)}, u32[]{:S(2)}) async-start(bf16[8,98,768]{2,1,0:T(8,128)(2,1)} %broadcast_in_dim.50), calls=%async_computation | async-start | bytes 2555904 | tf_op jit(solution)/shard_map/all_to_all | solution.py:28
  19.4 88.5 %copy-start = (bf16[2,208,768]{2,1,0:T(8,128)(2,1)}, bf16[2,208,768]{2,1,0:T(8,128)(2,1)S(1)}, u32[]{:S(2)}) copy-start(bf16[2,208,768]{2,1,0:T(8,128)(2,1)S(1)} %pad.24.xb) | copy-start | bytes 1916932
  19.4 15.9 %collective-permute-start = (bf16[2,208,768]{2,1,0:T(8,128)(2,1)S(1)}, bf16[2,208,768]{2,1,0:T(8,128)(2,1)S(1)}, u32[]{:S(2)}, u32[]{:S(2)}) collective-permute-start(bf16[2,208,768]{2,1,0:T(8,128)(2,1)S(1)} %pad.24.xb), channel_id=1, source_target_pairs={{0,2},{1,3},{2,0},{3,1},{4,6},{5,7},{6,4},{7,5},{8,10},{9,11},{10,... | collective-permute-start | bytes 1916936 | tf_op jit(solution)/shard_map/ppermute | solution.py:24
  21.0 46.1 %collective-permute-start.2 = (bf16[2,208,768]{2,1,0:T(8,128)(2,1)S(1)}, bf16[2,208,768]{2,1,0:T(8,128)(2,1)}, u32[]{:S(2)}, u32[]{:S(2)}) collective-permute-start(bf16[2,208,768]{2,1,0:T(8,128)(2,1)S(1)} %pad.24.xb), channel_id=1, source_target_pairs={{0,1},{1,0},{2,3},{3,2},{4,5},{5,4},{6,7},{7,6},{8,9},{9,8},{10,11... | collective-permute-start | bytes 1916936 | tf_op jit(solution)/shard_map/ppermute | solution.py:24
  35.3 18.7 %copy-start.30 = (bf16[2,208,768]{2,1,0:T(8,128)(2,1)}, bf16[2,208,768]{2,1,0:T(8,128)(2,1)S(1)}, u32[]{:S(2)}) copy-start(bf16[2,208,768]{2,1,0:T(8,128)(2,1)S(1)} %collective-permute-done.xb) | copy-start | bytes 1916932
  35.3 17.8 %collective-permute-start.1 = (bf16[2,208,768]{2,1,0:T(8,128)(2,1)S(1)}, bf16[2,208,768]{2,1,0:T(8,128)(2,1)S(1)}, u32[]{:S(2)}, u32[]{:S(2)}) collective-permute-start(bf16[2,208,768]{2,1,0:T(8,128)(2,1)S(1)} %collective-permute-done.xb), channel_id=1, source_target_pairs={{0,1},{1,0},{2,3},{3,2},{4,5},{5,4},{6,7},{7,6},{8,9},{9,8},{10,11... | collective-permute-start | bytes 1916936 | tf_op jit(solution)/shard_map/ppermute | solution.py:24
  53.1 14.0 %copy-start.12 = (bf16[8,96,768]{2,1,0:T(8,128)(2,1)}, bf16[8,96,768]{2,1,0:T(8,128)(2,1)S(1)}, u32[]{:S(2)}) copy-start(bf16[8,96,768]{2,1,0:T(8,128)(2,1)S(1)} %slice.114) | copy-start | bytes 3538948
  65.5 8.4 %copy-start.50 = (bf16[2,208,192]{2,1,0:T(8,128)(2,1)}, bf16[2,208,192]{2,1,0:T(8,128)(2,1)S(1)}, u32[]{:S(2)}) copy-start(bf16[2,208,192]{2,1,0:T(8,128)(2,1)S(1)} %get-tuple-element.76.ca) | copy-start | bytes 479236
  65.5 10.8 %collective-permute-start.4 = (bf16[2,208,768]{2,1,0:T(8,128)(2,1)}, bf16[2,208,768]{2,1,0:T(8,128)(2,1)}, u32[]{:S(2)}, u32[]{:S(2)}) collective-permute-start(bf16[2,208,768]{2,1,0:T(8,128)(2,1)} %get-tuple-element.60), channel_id=1, source_target_pairs={{0,1},{1,0},{2,3},{3,2},{4,5},{5,4},{6,7},{7,6},{8,9},{9,8},{10,11... | collective-permute-start | bytes 1916936 | tf_op jit(solution)/shard_map/ppermute | solution.py:24
  65.5 53.1 %collective-permute-start.7 = (bf16[768,768]{1,0:T(8,128)(2,1)}, bf16[768,768]{1,0:T(8,128)(2,1)}, u32[]{:S(2)}, u32[]{:S(2)}) collective-permute-start(bf16[768,768]{1,0:T(8,128)(2,1)} %bitcast.106), channel_id=1, source_target_pairs={{0,2},{1,3},{2,0},{3,1},{4,6},{5,7},{6,4},{7,5},{8,10},{9,11},{10,... | collective-permute-start | bytes 3538952 | tf_op jit(solution)/shard_map/ppermute | solution.py:24
  76.0 4.2 collective-permute-start.3
  78.8 29.1 %collective-permute-start.5 = (bf16[2,208,768]{2,1,0:T(8,128)(2,1)}, bf16[2,208,768]{2,1,0:T(8,128)(2,1)S(1)}, u32[]{:S(2)}, u32[]{:S(2)}) collective-permute-start(bf16[2,208,768]{2,1,0:T(8,128)(2,1)} %add_convert_fusion.3), channel_id=1, source_target_pairs={{0,2},{1,3},{2,0},{3,1},{4,6},{5,7},{6,4},{7,5},{8,10},{9,11},{10,... | collective-permute-start | bytes 1916936 | tf_op jit(solution)/shard_map/ppermute | solution.py:24
  113.7 6.5 %copy-start.20 = (bf16[1,768,768]{2,1,0:T(8,128)(2,1)S(1)}, bf16[1,768,768]{2,1,0:T(8,128)(2,1)}, u32[]{:S(2)}) copy-start(bf16[1,768,768]{2,1,0:T(8,128)(2,1)} %param.24) | copy-start | bytes 3538948
  113.7 42.0 %all-to-all-start.1 = ((bf16[8,128,768]{2,1,0:T(8,128)(2,1)}), bf16[8,128,768]{2,1,0:T(8,128)(2,1)}, u32[]{:S(2)}, u32[]{:S(2)}) async-start(bf16[8,128,768]{2,1,0:T(8,128)(2,1)} %bitcast.91), calls=%async_computation.1 | async-start | bytes 3145728 | tf_op jit(solution)/shard_map/all_to_all | solution.py:28
  118.6 27.9 %collective-permute-start.10 = (bf16[768,768]{1,0:T(8,128)(2,1)}, bf16[768,768]{1,0:T(8,128)(2,1)S(1)}, u32[]{:S(2)}, u32[]{:S(2)}) collective-permute-start(bf16[768,768]{1,0:T(8,128)(2,1)} %bitcast.110), channel_id=1, source_target_pairs={{0,2},{1,3},{2,0},{3,1},{4,6},{5,7},{6,4},{7,5},{8,10},{9,11},{10,... | collective-permute-start | bytes 3538952 | tf_op jit(solution)/shard_map/ppermute | solution.py:24
  120.1 26.3 %collective-permute-start.6 = (bf16[768,768]{1,0:T(8,128)(2,1)S(1)}, bf16[768,768]{1,0:T(8,128)(2,1)S(1)}, u32[]{:S(2)}, u32[]{:S(2)}) collective-permute-start(bf16[768,768]{1,0:T(8,128)(2,1)S(1)} %bitcast.107), channel_id=1, source_target_pairs={{0,1},{1,0},{2,3},{3,2},{4,5},{5,4},{6,7},{7,6},{8,9},{9,8},{10,11... | collective-permute-start | bytes 3538952 | tf_op jit(solution)/shard_map/ppermute | solution.py:24
  120.2 27.3 %collective-permute-start.9 = (bf16[768,768]{1,0:T(8,128)(2,1)}, bf16[768,768]{1,0:T(8,128)(2,1)S(1)}, u32[]{:S(2)}, u32[]{:S(2)}) collective-permute-start(bf16[768,768]{1,0:T(8,128)(2,1)} %bitcast.111), channel_id=1, source_target_pairs={{0,1},{1,0},{2,3},{3,2},{4,5},{5,4},{6,7},{7,6},{8,9},{9,8},{10,11... | collective-permute-start | bytes 3538952 | tf_op jit(solution)/shard_map/ppermute | solution.py:24
  120.7 26.8 %collective-permute-start.8 = (bf16[768,768]{1,0:T(8,128)(2,1)}, bf16[768,768]{1,0:T(8,128)(2,1)S(1)}, u32[]{:S(2)}, u32[]{:S(2)}) collective-permute-start(bf16[768,768]{1,0:T(8,128)(2,1)} %collective-permute-done.7.refs_2_), channel_id=1, source_target_pairs={{0,1},{1,0},{2,3},{3,2},{4,5},{5,4},{6,7},{7,6},{8,9},{9,8},{10,11... | collective-permute-start | bytes 3538952 | tf_op jit(solution)/shard_map/ppermute | solution.py:24
  146.4 3.1 collective-permute-start.11
  183.1 40.8 %all-to-all-start.2 = ((bf16[8,128,768]{2,1,0:T(8,128)(2,1)}), bf16[8,128,768]{2,1,0:T(8,128)(2,1)S(1)}, u32[]{:S(2)}, u32[]{:S(2)}) async-start(bf16[8,128,768]{2,1,0:T(8,128)(2,1)} %bitcast.126), calls=%async_computation.2 | async-start | bytes 3145728 | tf_op jit(solution)/shard_map/all_to_all | solution.py:28
  225.9 44.1 %copy-start.26 = (bf16[768,768]{1,0:T(8,128)(2,1)S(1)}, bf16[768,768]{1,0:T(8,128)(2,1)}, u32[]{:S(2)}) copy-start(bf16[768,768]{1,0:T(8,128)(2,1)} %copy-done.24) | copy-start | bytes 3538948
  225.9 44.1 %copy-start.29 = (bf16[768,768]{1,0:T(8,128)(2,1)S(1)}, bf16[768,768]{1,0:T(8,128)(2,1)}, u32[]{:S(2)}) copy-start(bf16[768,768]{1,0:T(8,128)(2,1)} %copy-done.27) | copy-start | bytes 3538948
  229.0 41.0 %copy-start.10 = (f32[416,768]{1,0:T(8,128)}, f32[416,768]{1,0:T(8,128)S(1)}, u32[]{:S(2)}) copy-start(f32[416,768]{1,0:T(8,128)S(1)} %get-tuple-element.71.g) | copy-start | bytes 3833860
  229.0 41.0 %copy-start.14 = (bf16[416,768]{1,0:T(8,128)(2,1)}, bf16[416,768]{1,0:T(8,128)(2,1)S(1)}, u32[]{:S(2)}) copy-start(bf16[416,768]{1,0:T(8,128)(2,1)S(1)} %get-tuple-element.92) | copy-start | bytes 1916932
  229.0 41.0 %copy-start.18 = (bf16[416,8]{1,0:T(8,128)(2,1)}, bf16[416,8]{1,0:T(8,128)(2,1)S(1)}, u32[]{:S(2)}) copy-start(bf16[416,8]{1,0:T(8,128)(2,1)S(1)} %get-tuple-element.72.gl) | copy-start | bytes 19972
  229.0 41.0 %copy-start.21 = (bf16[1,768,768]{2,1,0:T(8,128)(2,1)S(1)}, bf16[1,768,768]{2,1,0:T(8,128)(2,1)}, u32[]{:S(2)}) copy-start(bf16[1,768,768]{2,1,0:T(8,128)(2,1)} %param.24) | copy-start | bytes 3538948
  229.0 41.0 %copy-start.23 = (bf16[1,768,768]{2,1,0:T(8,128)(2,1)S(1)}, bf16[1,768,768]{2,1,0:T(8,128)(2,1)}, u32[]{:S(2)}) copy-start(bf16[1,768,768]{2,1,0:T(8,128)(2,1)} %param.25) | copy-start | bytes 3538948
  285.7 40.4 %all-to-all-start.4 = ((bf16[8,128,768]{2,1,0:T(8,128)(2,1)}), bf16[8,128,768]{2,1,0:T(8,128)(2,1)S(1)}, u32[]{:S(2)}, u32[]{:S(2)}) async-start(bf16[8,128,768]{2,1,0:T(8,128)(2,1)} %bitcast.127), calls=%async_computation.4 | async-start | bytes 3145728 | tf_op jit(solution)/shard_map/all_to_all | solution.py:28
  289.5 36.6 %copy-start.19 = (bf16[416,8]{1,0:T(8,128)(2,1)S(1)}, bf16[416,8]{1,0:T(8,128)(2,1)}, u32[]{:S(2)}) copy-start(bf16[416,8]{1,0:T(8,128)(2,1)} %copy-done.18) | copy-start | bytes 19972
  294.0 49.8 %collective-permute-start.24 = (bf16[768,768]{1,0:T(8,128)(2,1)}, bf16[768,768]{1,0:T(8,128)(2,1)}, u32[]{:S(2)}, u32[]{:S(2)}) collective-permute-start(bf16[768,768]{1,0:T(8,128)(2,1)} %fusion.25), channel_id=1, source_target_pairs={{0,1},{1,0},{2,3},{3,2},{4,5},{5,4},{6,7},{7,6},{8,9},{9,8},{10,11... | collective-permute-start | bytes 3538952 | tf_op jit(solution)/shard_map/ppermute | solution.py:24
  329.1 14.7 %collective-permute-start.12 = (bf16[2,208,768]{2,1,0:T(8,128)(2,1)S(1)}, bf16[2,208,768]{2,1,0:T(8,128)(2,1)S(1)}, u32[]{:S(2)}, u32[]{:S(2)}) collective-permute-start(bf16[2,208,768]{2,1,0:T(8,128)(2,1)S(1)} %bitcast.114), channel_id=1, source_target_pairs={{0,2},{1,3},{2,0},{3,1},{4,6},{5,7},{6,4},{7,5},{8,10},{9,11},{10,... | collective-permute-start | bytes 1916936 | tf_op jit(solution)/shard_map/ppermute | solution.py:24
  334.5 67.6 %collective-permute-start.23 = (bf16[768,768]{1,0:T(8,128)(2,1)}, bf16[768,768]{1,0:T(8,128)(2,1)}, u32[]{:S(2)}, u32[]{:S(2)}) collective-permute-start(bf16[768,768]{1,0:T(8,128)(2,1)} %fusion.22), channel_id=1, source_target_pairs={{0,1},{1,0},{2,3},{3,2},{4,5},{5,4},{6,7},{7,6},{8,9},{9,8},{10,11... | collective-permute-start | bytes 3538952 | tf_op jit(solution)/shard_map/ppermute | solution.py:24
  334.5 15.1 %collective-permute-start.14 = (bf16[2,208,768]{2,1,0:T(8,128)(2,1)S(1)}, bf16[2,208,768]{2,1,0:T(8,128)(2,1)S(1)}, u32[]{:S(2)}, u32[]{:S(2)}) collective-permute-start(bf16[2,208,768]{2,1,0:T(8,128)(2,1)S(1)} %bitcast.115), channel_id=1, source_target_pairs={{0,1},{1,0},{2,3},{3,2},{4,5},{5,4},{6,7},{7,6},{8,9},{9,8},{10,11... | collective-permute-start | bytes 1916936 | tf_op jit(solution)/shard_map/ppermute | solution.py:24
  339.4 54.3 %collective-permute-start.21 = (bf16[768,768]{1,0:T(8,128)(2,1)}, bf16[768,768]{1,0:T(8,128)(2,1)}, u32[]{:S(2)}, u32[]{:S(2)}) collective-permute-start(bf16[768,768]{1,0:T(8,128)(2,1)} %fusion.19), channel_id=1, source_target_pairs={{0,1},{1,0},{2,3},{3,2},{4,5},{5,4},{6,7},{7,6},{8,9},{9,8},{10,11... | collective-permute-start | bytes 3538952 | tf_op jit(solution)/shard_map/ppermute | solution.py:24
  343.7 19.9 %collective-permute-start.13 = (bf16[2,208,768]{2,1,0:T(8,128)(2,1)S(1)}, bf16[2,208,768]{2,1,0:T(8,128)(2,1)S(1)}, u32[]{:S(2)}, u32[]{:S(2)}) collective-permute-start(bf16[2,208,768]{2,1,0:T(8,128)(2,1)S(1)} %collective-permute-done.12.gb), channel_id=1, source_target_pairs={{0,1},{1,0},{2,3},{3,2},{4,5},{5,4},{6,7},{7,6},{8,9},{9,8},{10,11... | collective-permute-start | bytes 1916936 | tf_op jit(solution)/shard_map/ppermute | solution.py:24
  343.7 6.1 %copy-start.49 = (bf16[2,208,576]{2,1,0:T(8,128)(2,1)S(1)}, bf16[2,208,576]{2,1,0:T(8,128)(2,1)}, u32[]{:S(2)}) copy-start(bf16[2,208,576]{2,1,0:T(8,128)(2,1)} %copy-done.48) | copy-start | bytes 1437700
  343.7 6.1 %copy-start.59 = (bf16[2,208,192]{2,1,0:T(8,128)(2,1)S(1)}, bf16[2,208,192]{2,1,0:T(8,128)(2,1)}, u32[]{:S(2)}) copy-start(bf16[2,208,192]{2,1,0:T(8,128)(2,1)} %copy-done.58) | copy-start | bytes 479236
  343.7 6.1 %copy-start.61 = (bf16[2,208,192]{2,1,0:T(8,128)(2,1)S(1)}, bf16[2,208,192]{2,1,0:T(8,128)(2,1)}, u32[]{:S(2)}) copy-start(bf16[2,208,192]{2,1,0:T(8,128)(2,1)} %copy-done.60) | copy-start | bytes 479236
  343.8 6.1 %copy-start.63 = (f32[2,208,3]{2,1,0:T(8,128)S(1)}, f32[2,208,3]{2,1,0:T(8,128)}, u32[]{:S(2)}) copy-start(f32[2,208,3]{2,1,0:T(8,128)} %copy-done.62) | copy-start | bytes 14980
  343.8 6.1 %copy-start.65 = (f32[2,208,3]{2,1,0:T(8,128)S(1)}, f32[2,208,3]{2,1,0:T(8,128)}, u32[]{:S(2)}) copy-start(f32[2,208,3]{2,1,0:T(8,128)} %copy-done.64) | copy-start | bytes 14980
  348.1 54.9 %collective-permute-start.25 = (bf16[768,768]{1,0:T(8,128)(2,1)}, bf16[768,768]{1,0:T(8,128)(2,1)}, u32[]{:S(2)}, u32[]{:S(2)}) collective-permute-start(bf16[768,768]{1,0:T(8,128)(2,1)} %add_convert_fusion), channel_id=1, source_target_pairs={{0,2},{1,3},{2,0},{3,1},{4,6},{5,7},{6,4},{7,5},{8,10},{9,11},{10,... | collective-permute-start | bytes 3538952 | tf_op jit(solution)/shard_map/ppermute | solution.py:24
  349.9 13.7 %copy-start.32 = (bf16[2,208,768]{2,1,0:T(8,128)(2,1)S(1)}, bf16[2,208,768]{2,1,0:T(8,128)(2,1)}, u32[]{:S(2)}) copy-start(bf16[2,208,768]{2,1,0:T(8,128)(2,1)} %copy-done.30) | copy-start | bytes 1916932
  349.9 13.7 %copy-start.35 = (bf16[2,208,768]{2,1,0:T(8,128)(2,1)S(1)}, bf16[2,208,768]{2,1,0:T(8,128)(2,1)}, u32[]{:S(2)}) copy-start(bf16[2,208,768]{2,1,0:T(8,128)(2,1)} %copy-done.33) | copy-start | bytes 1916932
  349.9 13.7 %copy-start.43 = (bf16[2,208,576]{2,1,0:T(8,128)(2,1)S(1)}, bf16[2,208,576]{2,1,0:T(8,128)(2,1)}, u32[]{:S(2)}) copy-start(bf16[2,208,576]{2,1,0:T(8,128)(2,1)} %copy-done.42) | copy-start | bytes 1437700
  349.9 13.7 %copy-start.45 = (bf16[2,208,576]{2,1,0:T(8,128)(2,1)S(1)}, bf16[2,208,576]{2,1,0:T(8,128)(2,1)}, u32[]{:S(2)}) copy-start(bf16[2,208,576]{2,1,0:T(8,128)(2,1)} %copy-done.44) | copy-start | bytes 1437700
  349.9 13.7 %copy-start.51 = (bf16[2,208,192]{2,1,0:T(8,128)(2,1)S(1)}, bf16[2,208,192]{2,1,0:T(8,128)(2,1)}, u32[]{:S(2)}) copy-start(bf16[2,208,192]{2,1,0:T(8,128)(2,1)} %copy-done.50) | copy-start | bytes 479236
  349.9 13.7 %copy-start.53 = (bf16[2,208,192]{2,1,0:T(8,128)(2,1)S(1)}, bf16[2,208,192]{2,1,0:T(8,128)(2,1)}, u32[]{:S(2)}) copy-start(bf16[2,208,192]{2,1,0:T(8,128)(2,1)} %copy-done.52) | copy-start | bytes 479236
  349.9 13.7 %copy-start.55 = (f32[2,208,3]{2,1,0:T(8,128)S(1)}, f32[2,208,3]{2,1,0:T(8,128)}, u32[]{:S(2)}) copy-start(f32[2,208,3]{2,1,0:T(8,128)} %copy-done.54) | copy-start | bytes 14980
  350.0 13.7 %copy-start.57 = (f32[2,208,3]{2,1,0:T(8,128)S(1)}, f32[2,208,3]{2,1,0:T(8,128)}, u32[]{:S(2)}) copy-start(f32[2,208,3]{2,1,0:T(8,128)} %copy-done.56) | copy-start | bytes 14980
  376.5 12.3 %all-to-all-start.5 = ((f32[8,16,128]{2,1,0:T(8,128)}), f32[8,16,128]{2,1,0:T(8,128)S(1)}, u32[]{:S(2)}, u32[]{:S(2)}) async-start(f32[8,16,128]{2,1,0:T(8,128)} %copy.100), calls=%async_computation.5 | async-start | bytes 131072 | tf_op jit(solution)/shard_map/all_to_all | solution.py:28
  386.3 45.7 %collective-permute-start.20 = (bf16[768,768]{1,0:T(8,128)(2,1)}, bf16[768,768]{1,0:T(8,128)(2,1)}, u32[]{:S(2)}, u32[]{:S(2)}) collective-permute-start(bf16[768,768]{1,0:T(8,128)(2,1)} %fusion.16), channel_id=1, source_target_pairs={{0,1},{1,0},{2,3},{3,2},{4,5},{5,4},{6,7},{7,6},{8,9},{9,8},{10,11... | collective-permute-start | bytes 3538952 | tf_op jit(solution)/shard_map/ppermute | solution.py:24
  388.8 59.4 %all-to-all-start.6 = ((bf16[8,96,768]{2,1,0:T(8,128)(2,1)}), bf16[8,96,768]{2,1,0:T(8,128)(2,1)}, u32[]{:S(2)}, u32[]{:S(2)}) async-start(bf16[8,96,768]{2,1,0:T(8,128)(2,1)} %bitcast.120), calls=%async_computation.6 | async-start | bytes 2359296 | tf_op jit(solution)/shard_map/all_to_all | solution.py:28
  393.7 7.5 %copy-start.15 = (bf16[416,768]{1,0:T(8,128)(2,1)S(1)}, bf16[416,768]{1,0:T(8,128)(2,1)}, u32[]{:S(2)}) copy-start(bf16[416,768]{1,0:T(8,128)(2,1)} %copy-done.14) | copy-start | bytes 1916932
  398.5 33.5 %collective-permute-start.22 = (bf16[768,768]{1,0:T(8,128)(2,1)}, bf16[768,768]{1,0:T(8,128)(2,1)}, u32[]{:S(2)}, u32[]{:S(2)}) collective-permute-start(bf16[768,768]{1,0:T(8,128)(2,1)} %add_convert_fusion.1), channel_id=1, source_target_pairs={{0,2},{1,3},{2,0},{3,1},{4,6},{5,7},{6,4},{7,5},{8,10},{9,11},{10,... | collective-permute-start | bytes 3538952 | tf_op jit(solution)/shard_map/ppermute | solution.py:24
  399.8 1.2 collective-permute-start.15
  401.0 27.9 %collective-permute-start.18 = (bf16[2,208,768]{2,1,0:T(8,128)(2,1)}, bf16[2,208,768]{2,1,0:T(8,128)(2,1)}, u32[]{:S(2)}, u32[]{:S(2)}) collective-permute-start(bf16[2,208,768]{2,1,0:T(8,128)(2,1)} %get-tuple-element.96), channel_id=1, source_target_pairs={{0,1},{1,0},{2,3},{3,2},{4,5},{5,4},{6,7},{7,6},{8,9},{9,8},{10,11... | collective-permute-start | bytes 1916936 | tf_op jit(solution)/shard_map/ppermute | solution.py:24
  402.2 6.3 %copy-start.37 = (bf16[2,208,768]{2,1,0:T(8,128)(2,1)S(1)}, bf16[2,208,768]{2,1,0:T(8,128)(2,1)}, u32[]{:S(2)}) copy-start(bf16[2,208,768]{2,1,0:T(8,128)(2,1)} %copy-done.36) | copy-start | bytes 1916932
  402.2 26.7 %copy-start.9 = (f32[2,208,768]{2,1,0:T(8,128)S(1)}, f32[2,208,768]{2,1,0:T(8,128)}, u32[]{:S(2)}) copy-start(f32[2,208,768]{2,1,0:T(8,128)} %copy-done.8) | copy-start | bytes 3833860
  402.2 24.8 %collective-permute-start.16 = (f32[16,128]{1,0:T(8,128)S(1)}, f32[16,128]{1,0:T(8,128)S(1)}, u32[]{:S(2)}, u32[]{:S(2)}) collective-permute-start(f32[16,128]{1,0:T(8,128)S(1)} %add.77), channel_id=1, source_target_pairs={{0,2},{1,3},{2,0},{3,1},{4,6},{5,7},{6,4},{7,5},{8,10},{9,11},{10,... | collective-permute-start | bytes 24584 | tf_op jit(solution)/shard_map/ppermute | solution.py:24
  408.5 29.2 %collective-permute-start.17 = (bf16[2,208,768]{2,1,0:T(8,128)(2,1)S(1)}, bf16[2,208,768]{2,1,0:T(8,128)(2,1)S(1)}, u32[]{:S(2)}, u32[]{:S(2)}) collective-permute-start(bf16[2,208,768]{2,1,0:T(8,128)(2,1)S(1)} %copy-done.37), channel_id=1, source_target_pairs={{0,1},{1,0},{2,3},{3,2},{4,5},{5,4},{6,7},{7,6},{8,9},{9,8},{10,11... | collective-permute-start | bytes 1916936 | tf_op jit(solution)/shard_map/ppermute | solution.py:24
  430.1 15.8 %collective-permute-start.19 = (bf16[2,208,768]{2,1,0:T(8,128)(2,1)S(1)}, bf16[2,208,768]{2,1,0:T(8,128)(2,1)S(1)}, u32[]{:S(2)}, u32[]{:S(2)}) collective-permute-start(bf16[2,208,768]{2,1,0:T(8,128)(2,1)S(1)} %add_convert_fusion.2), channel_id=1, source_target_pairs={{0,2},{1,3},{2,0},{3,1},{4,6},{5,7},{6,4},{7,5},{8,10},{9,11},{10,... | collective-permute-start | bytes 1916936 | tf_op jit(solution)/shard_map/ppermute | solution.py:24
  432.0 14.0 %copy-start.5 = (f32[416,768]{1,0:T(8,128)S(1)}, f32[416,768]{1,0:T(8,128)}, u32[]{:S(2)}) copy-start(f32[416,768]{1,0:T(8,128)} %copy-done.4) | copy-start | bytes 3833860
  432.0 14.0 %copy-start.7 = (f32[2,208,768]{2,1,0:T(8,128)S(1)}, f32[2,208,768]{2,1,0:T(8,128)}, u32[]{:S(2)}) copy-start(f32[2,208,768]{2,1,0:T(8,128)} %copy-done.6) | copy-start | bytes 3833860
  (41 other events, 59.5 us)

commit v3 on v2

v3 whole, which is shorter than its diff:
```python
import functools
import jax
import jax.numpy as jnp
from jax import lax
from jax.experimental import pallas as pl
from jax.experimental.pallas import tpu as pltpu
from jax.sharding import PartitionSpec as P

HD = 64
EPSILON = 1e-06
MASKED = -1000000000.0
BF = jnp.bfloat16
F32 = jnp.float32
LOG2E = 1.4426950408889634
MIB = 1 << 20
PLAIN = 10


def dot(a, b, ca, cb):
    return lax.dot_general(a, b, (((ca,), (cb,)), ((), ())), preferred_element_type=F32)


def swap(value, k):
    n = lax.axis_size("tensor")
    return lax.ppermute(value, "tensor", [(i, i ^ k) for i in range(n)])


def to_all(v):
    return lax.all_to_all(v, "dp", split_axis=0, concat_axis=0, tiled=True)


def norm_parts(v):
    center = v - jnp.mean(v, axis=-1, keepdims=True)
    scale = lax.rsqrt(jnp.mean(center * center, axis=-1, keepdims=True) + EPSILON)
    return center * scale, scale


def norm_back(grad, n, scale, gain):
    gy = grad * gain
    return scale * (
        gy - jnp.mean(gy, -1, keepdims=True) - n * jnp.mean(gy * n, -1, keepdims=True)
    )


def col_sum(v):
    return jnp.sum(v, axis=0, keepdims=True)


def scores_of(q, k, keep):
    s = dot(q, k, 1, 1) * HD**-0.5
    return jnp.where(keep, s, MASKED)


def one_image(x, keep, w, gain, shift, heads):
    n, _ = norm_parts(x.astype(F32))
    h1 = (n * gain + shift).astype(BF)
    c = heads * HD
    qkv = dot(h1, w[:, : 3 * c], 1, 0).astype(BF)
    contexts, totals = [], []
    for h in range(heads):
        q, k, v = (qkv[:, i * c + h * HD : i * c + (h + 1) * HD] for i in range(3))
        s = scores_of(q, k, keep)
        top = jnp.max(s, -1, keepdims=True)
        total = top + jnp.log(jnp.sum(jnp.exp(s - top), -1, keepdims=True))
        contexts.append(dot(jnp.exp(s - total).astype(BF), v, 1, 0).astype(BF))
        totals.append(total)
    context = jnp.concatenate(contexts, 1)
    return qkv, context, jnp.concatenate(totals, 1), dot(context, w[:, 3 * c :], 1, 1)


def attn_fwd_kernel(heads, n, *refs):
    xs, keeps, (w_ref, gains), outs = refs[:n], refs[n : 2 * n], refs[2 * n : 2 * n + 2], refs[2 * n + 2 :]
    w = w_ref[...]
    gain, shift = gains[0:1], gains[1:2]
    for i in range(n):
        values = one_image(xs[i][0], keeps[i][0] > 0, w, gain, shift, heads)
        for out, value in zip(outs[4 * i : 4 * i + 4], values):
            out[0] = value.astype(out.dtype)


CHEAP = pl.CostEstimate(flops=1 << 20, bytes_accessed=1 << 10, transcendentals=0)
NEAR = pl.CostEstimate(flops=1 << 28, bytes_accessed=8 * MIB, transcendentals=0)
ALL = 58


def whole(shape):
    return pl.BlockSpec(shape, lambda *i: (0,) * len(shape))


def each(shape):
    return pl.BlockSpec((1,) + shape, lambda i: (i,) + (0,) * len(shape))


def params(vmem):
    return pltpu.CompilerParams(vmem_limit_bytes=vmem * MIB)


def attn_fwd(xs, keeps, part_types, w, gains, heads):
    images, rows, width = xs[0].shape
    c = heads * HD
    outs = []
    for part_type in part_types:
        outs += [((rows, 3 * c), BF), ((rows, c), BF), ((rows, heads), F32), ((rows, width), part_type)]
    made = pl.pallas_call(
        functools.partial(attn_fwd_kernel, heads, len(xs)),
        grid=(images,),
        in_specs=[each((rows, width)) for _ in xs] + [each((1, rows)) for _ in xs] + [whole(w.shape), whole(gains.shape)],
        out_specs=[each(s) for s, _ in outs],
        out_shape=[jax.ShapeDtypeStruct((images,) + s, d) for s, d in outs],
        compiler_params=params(ALL),
        cost_estimate=CHEAP,
    )(*xs, *keeps, w, gains)
    return [made[4 * i : 4 * i + 4] for i in range(len(xs))]


def one_image_back(x, ga, qkv, context, lse, keep, w, gain, shift, heads):
    n, _ = norm_parts(x.astype(F32))
    h1 = (n * gain + shift).astype(BF)
    c = heads * HD
    gc_all = dot(ga, w[:, 3 * c :], 1, 0).astype(BF)
    parts = [[], [], []]
    for h in range(heads):
        q, k, v = (qkv[:, i * c + h * HD : i * c + (h + 1) * HD] for i in range(3))
        gc = gc_all[:, h * HD : (h + 1) * HD]
        p = jnp.exp(scores_of(q, k, keep) - lse[:, h : h + 1])
        gv = dot(p.astype(BF), gc, 0, 0)
        gp = dot(gc, v, 1, 1)
        delta = jnp.sum(p * gp, -1, keepdims=True)
        gs = (p * (gp - delta)).astype(BF)
        parts[0].append((dot(gs, k, 1, 0) * HD**-0.5).astype(BF))
        parts[1].append((dot(gs, q, 0, 0) * HD**-0.5).astype(BF))
        parts[2].append(gv.astype(BF))
    gqkv = jnp.concatenate(parts[0] + parts[1] + parts[2], 1)
    gh1 = dot(gqkv, w[:, : 3 * c], 1, 1)
    return gh1, h1, gqkv, col_sum(gh1 * n), col_sum(gh1)


def split_float(v):
    high = v.astype(BF)
    return high, (v - high.astype(F32)).astype(BF)


def attn_bwd_kernel(heads, xa, xb, ga, gb, qa, qb, ca, cb, la, lb, ka, kb, w_ref, gains, *refs):
    others, (ha, hb, dw_out, vec, h_all, q_all, g_all, c_all) = refs[:-8], refs[-8:]

    @pl.when(pl.program_id(0) == 0)
    def _():
        vec[...] = others[1][...] if others else jnp.zeros_like(vec)

    w = w_ref[...]
    gain, shift = gains[0:1], gains[1:2]
    length = xa.shape[1]
    groups = ((xa, ga, qa, ca, la, ka, ha), (xb, gb, qb, cb, lb, kb, hb))
    for i, (x, g, q, c, total, k, out) in enumerate(groups):
        gh1, h1, gqkv, gg, gs = one_image_back(x[0], g[0], q[0], c[0], total[0], k[0] > 0, w, gain, shift, heads)
        out[0] = gh1.astype(out.dtype)
        at = pl.ds(pl.multiple_of((2 * pl.program_id(0) + i) * length, length), length)
        h_all[at], q_all[at], g_all[at], c_all[at] = h1, gqkv, g[0], c[0]
        vec[0:1] += gg
        vec[1:2] += gs

    @pl.when(pl.program_id(0) == pl.num_programs(0) - 1)
    def _():
        dw = jnp.concatenate([dot(h_all[...], q_all[...], 0, 0), dot(g_all[...], c_all[...], 0, 0)], 1)
        if others:
            dw = dw + others[0][...]
        if not others:
            dw_out[...] = dw
        else:
            rows = dw.shape[0] // dw_out.shape[0]
            vec_two, router, loss = others[2:]
            experts, width = router.shape
            rest = jnp.zeros((experts - 5, width), F32)
            named = jnp.concatenate([vec[...], vec_two[...], loss[...], rest], 0)
            pieces = [p.astype(F32) for v in (router[...], named) for p in split_float(v)]
            for k in range(dw_out.shape[0]):
                at = slice(k * rows, (k + 1) * rows)
                last = jnp.concatenate([p[:, at] for p in pieces] + [jnp.zeros((experts, width - 4 * rows), F32)], 1)
                dw_out[k] = jnp.concatenate([dw[at], last], 0).astype(BF)


def attn_bwd(xa, xb, ga, gb, qa, qb, ca, cb, la, lb, ka, kb, w, gains, others, heads, pack):
    images, rows, width = xa.shape
    c = heads * HD
    vec_shape = (2, width)
    specs = [each((rows, k)) for k in (width, width, 3 * c, c, heads) for _ in range(2)] + [each((1, rows))] * 2
    return pl.pallas_call(
        functools.partial(attn_bwd_kernel, heads),
        grid=(images,),
        in_specs=specs + [whole(v.shape) for v in (w, gains) + others],
        out_specs=[each((rows, width))] * 2 + [whole(pack[0] if pack else w.shape), whole(vec_shape)],
        out_shape=[jax.ShapeDtypeStruct(xa.shape, t) for t in (BF, F32)]
        + [jax.ShapeDtypeStruct(*(pack or (w.shape, F32))), jax.ShapeDtypeStruct(vec_shape, F32)],
        scratch_shapes=[pltpu.VMEM((2 * images * rows, k), BF) for k in (width, 3 * c, width, c)],
        compiler_params=params(ALL),
        cost_estimate=NEAR,
    )(xa, xb, ga, gb, qa, qb, ca, cb, la, lb, ka, kb, w, gains, *others)


def chosen(slot_row, slots):
    at = lax.broadcasted_iota(jnp.int32, (slots, slot_row.shape[1]), 0)
    return jnp.where(slot_row == at, 1.0, 0.0).astype(BF)


def dispatch_kernel(slots, x, p0, r1, r2, gains, router, slot, residual, probs, sent):
    res = x[...].astype(F32) + p0[...] + r1[...].astype(F32) + r2[...].astype(F32)
    residual[...] = res
    n, _ = norm_parts(res)
    h2 = (n * gains[2:3] + gains[3:4]).astype(BF)
    logits = dot(h2, router[...], 1, 1)
    grown = jnp.exp(logits - jnp.max(logits, -1, keepdims=True))
    probs[...] = grown / jnp.sum(grown, -1, keepdims=True)
    for e in range(slot.shape[0]):
        at = slice(e * slots, (e + 1) * slots)
        sent[at] = dot(chosen(slot[e : e + 1], slots), h2, 1, 0).astype(BF)


def picks(place, total):
    at = lax.broadcasted_iota(jnp.int32, (place.shape[0], total), 1)
    return jnp.where(place == at, 1.0, 0.0)


def combine_kernel(slots, back, place, ids, probs_in, residual, teacher, mask, factor, slot, out, g_out, gl_out, loss, sent):
    probs = probs_in[...]
    experts = probs.shape[1]
    at = lax.broadcasted_iota(jnp.int32, probs.shape, 1)
    choose = [jnp.where(ids[:, j : j + 1] == at, 1.0, 0.0) for j in range(ids.shape[1])]
    gates = [jnp.sum(c * probs, -1, keepdims=True) for c in choose]
    picked = [dot(picks(place[:, j : j + 1], back.shape[0]).astype(BF), back[...], 1, 0) for j in range(len(gates))]
    result = residual[...]
    result = result + sum(gate * p for gate, p in zip(gates, picked))
    out[...] = result.astype(BF)
    errors = result - teacher[...].astype(F32)
    m = mask[...]
    row_loss = jnp.mean(errors * errors, -1, keepdims=True) * m
    loss[...] = jnp.broadcast_to(col_sum(row_loss), loss.shape)
    g = m * errors * factor[0:1, 0:1]
    g_out[...] = g
    grad_probs = sum(c * jnp.sum(g * p, -1, keepdims=True) for c, p in zip(choose, picked))
    grad_logits = probs * (grad_probs - jnp.sum(probs * grad_probs, -1, keepdims=True))
    gl_out[...] = grad_logits.astype(BF)
    for e in range(experts):
        at = slice(e * slots, (e + 1) * slots)
        gated = (probs[:, e : e + 1] * g).astype(BF)
        sent[at] = dot(chosen(slot[e : e + 1], slots), gated, 1, 0).astype(BF)


def back_kernel(back, place, residual, g, gl, gains, router, grad_residual, grad_attn, vec, grad_router):
    either = sum(picks(place[:, j : j + 1], back.shape[0]) for j in range(place.shape[1])).astype(BF)
    grad_h2 = dot(either, back[...], 1, 0) + dot(gl[...], router[...], 1, 0)
    n, scale = norm_parts(residual[...])
    gain = gains[2:3]
    h2 = (n * gain + gains[3:4]).astype(BF)
    vec[0:1] = col_sum(grad_h2 * n)
    vec[1:2] = col_sum(grad_h2)
    grad_router[...] = dot(gl[...], h2, 0, 0)
    total = g[...] + norm_back(grad_h2, n, scale, gain)
    grad_residual[...] = total
    grad_attn[...] = total.astype(BF)


def last_kernel(images, x, p0, r1, r2, gains, grad_residual, out):
    grad_h1 = p0[...] + r1[...].astype(F32) + r2[...].astype(F32)
    n, scale = norm_parts(x[...].astype(F32))
    total = grad_residual[...] + norm_back(grad_h1, n, scale, gains[0:1])
    padded, length = x.shape[0] // images, out.shape[0] // images
    for i in range(images):
        out[i * length : (i + 1) * length] = total[i * padded : i * padded + length]


def plain(kernel, outs, *args):
    return pl.pallas_call(
        kernel,
        grid=(1,),
        in_specs=[whole(v.shape) for v in args],
        out_specs=[whole(s) for s, _ in outs],
        out_shape=[jax.ShapeDtypeStruct(s, d) for s, d in outs],
        compiler_params=params(ALL),
        cost_estimate=CHEAP,
    )(*args)


class Copies:
    def __init__(self, sems):
        self.sems, self.made = sems, []

    def start(self, source, target):
        copy = pltpu.make_async_copy(source, target, self.sems.at[len(self.made)])
        copy.start()
        self.made.append(copy)
        return copy


def dense_kernel(parts, qkv, proj, small):
    total = parts[0].astype(F32)
    for k in range(1, parts.shape[0]):
        total = total + parts[k].astype(F32)
    rows, c = proj.shape
    for i in range(3):
        qkv[:, i, :] = total[:rows, i * c : (i + 1) * c]
    proj[...] = total[:rows, 3 * c :]
    last = total[rows:]
    piece = lambda i: last[:, i * rows : (i + 1) * rows]
    small[...] = jnp.concatenate([piece(0) + piece(1), piece(2) + piece(3)], 0)


def shard_kernel(qkv, proj, g1, s1, g2, s2, router, mask, out, block, sems):
    weights = jnp.concatenate([qkv[:, i, :] for i in range(3)] + [proj[...]], 1)
    rows, width = weights.shape
    count = jnp.sum(jnp.sum(mask[...].astype(F32), 1, keepdims=True), 0, keepdims=True)
    high = jnp.floor(count / 128)
    vectors = [v[...].astype(F32) for v in (g1, s1, g2, s2)] + [high, count - 128 * high]
    vectors.append(jnp.zeros((1, width - 4 * rows - 2), F32))
    at = [lax.broadcasted_iota(jnp.int32, (rows, rows), i) for i in (0, 1)]
    turned = dot(router[...], jnp.where(at[0] == at[1], 1.0, 0.0).astype(BF), 0, 0)
    last = jnp.concatenate([turned[e : e + 1] for e in range(turned.shape[0])], 1)
    extra = jnp.concatenate([jnp.concatenate(vectors, 1), last], 0)
    block[...] = jnp.concatenate([weights, extra.astype(BF)], 0)
    copies = Copies(sems)
    for k in range(out.shape[0]):
        copies.start(block, out.at[k])
    for copy in copies.made:
        copy.wait()


def gelu_parts(u):
    phi = 0.5 * lax.erf(u * 0.7071067811865476) + 0.5
    bell = jnp.exp2(u * u * (-0.5 * LOG2E))
    return u * phi, phi + u * bell * 0.3989422804014327


def side_by_side(refs):
    return jnp.concatenate([r[...] for r in refs], 1)


def over_chunks(rows, step, body):
    def one(i, carry):
        body(pl.ds(pl.multiple_of(i * step, step), step))
        return carry

    lax.fori_loop(0, rows // step, one, 0)


def expert_fwd_kernel(n, step, x, *refs):
    ups, downs, (out, hidden, slope) = refs[:n], refs[n : 2 * n], refs[2 * n : 2 * n + 3]
    wu, wd, hs, ss, os, sems = refs[2 * n + 3 :]
    copies = Copies(sems)
    f = wu.shape[2]
    up_in = [copies.start(ups[t], wu.at[t]) for t in range(n)]
    down_in = []
    outgoing = []
    for row in range(0, x.shape[0], step):
        at = slice(row, row + step)
        for t in range(n):
            cols = slice(t * f, (t + 1) * f)
            if row == 0:
                up_in[t].wait()
                if t == 0:
                    down_in = [copies.start(downs[i], wd.at[i]) for i in range(n)]
            value, der = gelu_parts(dot(x[at], wu[t], 1, 0))
            hs[at, cols] = value.astype(BF)
            ss[at, cols] = der.astype(BF)
        outgoing.append(copies.start(hs.at[at], hidden.at[at]))
        outgoing.append(copies.start(ss.at[at], slope.at[at]))
        if row == 0:
            for copy in down_in:
                copy.wait()
        os[at] = dot(hs[at], jnp.concatenate([wd[t] for t in range(n)], 1), 1, 1).astype(BF)
        outgoing.append(copies.start(os.at[at], out.at[at]))
    for copy in outgoing:
        copy.wait()


def expert_bwd_kernel(n, step, go, slope, *refs):
    ups, downs, (grad_up, out) = refs[:n], refs[n : 2 * n], refs[2 * n : 2 * n + 2]
    wu, wd, gs, ss, os, sems = refs[2 * n + 2 :]
    copies = Copies(sems)
    f = wu.shape[2]
    rows = go.shape[0]
    chunks = [slice(row, row + step) for row in range(0, rows, step)]
    down_in = [copies.start(downs[0], wd.at[0])]
    slope_in = [copies.start(slope.at[chunks[0]], ss.at[chunks[0]])]
    up_in = []
    outgoing = []
    for i, at in enumerate(chunks):
        for t in range(n):
            cols = slice(t * f, (t + 1) * f)
            if i == 0:
                down_in[t].wait()
            if t == 0:
                slope_in[i].wait()
                if i == 0:
                    down_in += [copies.start(downs[j], wd.at[j]) for j in range(1, n)]
                    up_in = [copies.start(ups[j], wu.at[j]) for j in range(n)]
                    slope_in += [copies.start(slope.at[later], ss.at[later]) for later in chunks[1:]]
            grad_hidden = dot(go[at], wd[t], 1, 0)
            gs[at, cols] = (grad_hidden * ss[at, cols].astype(F32)).astype(BF)
        outgoing.append(copies.start(gs.at[at], grad_up.at[at]))
        if i == 0:
            for copy in up_in:
                copy.wait()
        os[at] = dot(gs[at], jnp.concatenate([wu[t] for t in range(n)], 1), 1, 1).astype(BF)
        outgoing.append(copies.start(os.at[at], out.at[at]))
    for copy in outgoing:
        copy.wait()


def expert_weights_kernel(n, rows, cols, *refs):
    outs, (rs, cs, os, sems) = refs[:n], refs[n:]
    copies = Copies(sems)
    f = os.shape[2]
    rows_in = copies.start(rows, rs)
    cols_in = [copies.start(cols.at[:, slice(t * f, (t + 1) * f)], cs.at[t]) for t in range(n)]
    rows_in.wait()
    outgoing = []
    for t in range(n):
        cols_in[t].wait()
        os[t] = dot(rs[...], cs[t], 0, 0).astype(BF)
        outgoing.append(copies.start(os.at[t], outs[t]))
    for copy in outgoing:
        copy.wait()


IN_HBM = pl.BlockSpec(memory_space=pltpu.HBM)
IN_VMEM = pl.BlockSpec(memory_space=pltpu.VMEM)


def copying(kernel, ins, in_hbm, outs, out_hbm, scratch, copies, vmem=PLAIN):
    spec = lambda far: IN_HBM if far else IN_VMEM
    return pl.pallas_call(
        kernel,
        in_specs=[spec(far) for far in in_hbm],
        out_specs=[spec(far) for far in out_hbm],
        out_shape=[jax.ShapeDtypeStruct(s, d) for s, d in outs],
        scratch_shapes=[pltpu.VMEM(s, d) for s, d in scratch] + [pltpu.SemaphoreType.DMA((copies,))],
        compiler_params=params(vmem),
        cost_estimate=CHEAP if vmem == ALL else NEAR,
    )(*ins)


def after(value, *others):
    return lax.optimization_barrier((value,) + others)[0]


def local(
    tokens,
    teacher,
    valid_mask,
    expert_ids,
    attn_gain,
    attn_shift,
    qkv_weight,
    proj_weight,
    moe_gain,
    moe_shift,
    router_weight,
    up_weight,
    down_weight,
):
    rows, width = tokens.shape
    length = valid_mask.shape[1]
    images = rows // length
    experts = router_weight.shape[1]
    top = expert_ids.shape[1]
    capacity = max(2, (top * rows + experts - 1) // experts * 5 // 4)
    slots = -(-capacity // 16) * 16
    padded = -(-length // 16) * 16
    own = images * padded
    n_dp = lax.axis_size("dp")
    n_tensor = lax.axis_size("tensor")
    tensor_me = lax.axis_index("tensor")
    heads_width = proj_weight.shape[1]
    heads = heads_width // HD

    def pad(v, value=0):
        v = v.reshape((images, length) + v.shape[1:])
        return jnp.pad(v, ((0, 0), (0, padded - length)) + ((0, 0),) * (v.ndim - 2), constant_values=value)

    def unpad(v):
        return v.reshape(images, padded, -1)[:, :length].reshape(rows, -1)

    x0 = pad(tokens)
    x1 = swap(x0, 1)
    x2 = swap(x0, 2)
    x3 = swap(x2, 1)
    x = (x0, x1, x2, x3)

    dense_rows = proj_weight.shape[0]
    row = lambda v: v.reshape(1, dense_rows)
    block = (dense_rows + 2, width)
    [shards] = copying(
        shard_kernel,
        (qkv_weight, proj_weight)
        + tuple(row(v) for v in (attn_gain, attn_shift, moe_gain, moe_shift))
        + (router_weight, valid_mask),
        (0,) * 8,
        [((n_dp,) + block, BF)],
        (1,),
        [(block, BF)],
        n_dp,
        PLAIN,
    )
    got = to_all(shards)
    w = got[:, :dense_rows].reshape(width, width)
    extras = got[:, dense_rows]
    gains = extras[:, : 4 * dense_rows].reshape(n_dp, 4, dense_rows).swapaxes(0, 1).reshape(4, width).astype(F32)
    counts = jnp.sum(extras[:, 4 * dense_rows : 4 * dense_rows + 2].astype(F32), 0)
    count = counts[0] * 128 + counts[1]
    router = got[:, dense_rows + 1].reshape(n_dp, experts, dense_rows).swapaxes(0, 1).reshape(experts, width)

    up0, down0 = up_weight[0], down_weight[0]
    part = lambda eighths: width * eighths // 8
    up2 = [swap(up0[: part(4)], 2)]

    mask = jnp.pad(valid_mask, ((0, 0), (0, padded - length))).reshape(n_tensor, images, 1, padded)
    masks = [lax.dynamic_index_in_dim(mask, tensor_me ^ k, 0, keepdims=False) for k in range(4)]
    row_mask = masks[0].reshape(own, 1).astype(F32)
    ids = pad(expert_ids, -1).reshape(own, top)
    each_expert = lax.iota(jnp.int32, experts)
    named = ids[:, :, None] == each_expert
    names = jnp.any(named, axis=1)
    row_at = lax.iota(jnp.int32, own)
    before = (row_at[:, None] > row_at[None, :]).astype(BF)
    slot = jnp.where(names, dot(before, names.astype(BF), 1, 0).astype(jnp.int32), -1)
    place = jnp.where(ids < 0, -1, ids * slots + jnp.sum(jnp.where(named, slot[:, None, :], 0), -1))
    slot = slot.T

    w, up2[0] = lax.optimization_barrier((w, up2[0]))
    (q3, c3, l3, p3), (q2, c2, l2, p2), (q1, c1, l1, p1) = attn_fwd(
        (x3, x2, x1), (masks[3], masks[2], masks[1]), (BF, F32, BF), w, gains, heads
    )
    far = (p2 + swap(p3, 1).astype(F32)).astype(BF)
    r2 = swap(far, 2)
    [(q0, c0, l0, p0)] = attn_fwd((x0,), (masks[0],), (F32,), w, gains, heads)
    r1 = swap(p1, 1)
    up2.append(swap(after(up0[part(4) :], r2), 2))
    up2 = jnp.concatenate(up2)
    ups = (up0, swap(up0, 1), up2, swap(up2, 1))
    down2 = swap(after(down0, r2), 2)
    downs = (down0, swap(down0, 1), down2, swap(down2, 1))
    flat = lambda v: v.reshape(own, v.shape[-1])
    row_f32 = ((own, width), F32)
    row_bf = ((own, width), BF)
    all_slots = ((experts * slots, width), BF)
    residual, probs, sent = plain(
        functools.partial(dispatch_kernel, slots),
        [row_f32, ((own, experts), F32), all_slots],
        *(flat(x0), flat(p0), flat(r1), flat(r2), gains, router, slot),
    )

    exchange = lambda v: to_all(v.reshape(n_dp, slots, width)).reshape(n_dp * slots, width)
    arrived = exchange(sent)
    total = n_dp * slots
    step = min(256, total)
    f = up0.shape[1]
    wide = ((total, n_tensor * f), BF)
    weights_in = [((n_tensor, width, f), BF)] * 2
    chunks = total // step
    out, hidden, slope = copying(
        functools.partial(expert_fwd_kernel, n_tensor, step),
        (arrived, *ups, *downs),
        (0,) + (1,) * (2 * n_tensor),
        [all_slots, wide, wide],
        (1, 1, 1),
        weights_in + [wide, wide, all_slots],
        2 * n_tensor + 3 * chunks,
        ALL,
    )
    returned = exchange(out)
    factor = jnp.full((1, 128), rows * n_dp * n_tensor / count, F32)
    result, g, grad_logits, loss_part, grad_sent = plain(
        functools.partial(combine_kernel, slots),
        [row_bf, row_f32, ((own, experts), BF), ((1, width), F32), all_slots],
        *(returned, place, ids, probs, residual, flat(pad(teacher)), row_mask, factor, slot),
    )
    grad_out = exchange(grad_sent)
    grad_up, grad_arrived = copying(
        functools.partial(expert_bwd_kernel, n_tensor, step),
        (grad_out, slope, *ups, *downs),
        (0, 1) + (1,) * (2 * n_tensor),
        [wide, all_slots],
        (1, 1),
        weights_in + [wide, wide, all_slots],
        2 * n_tensor + 3 * chunks,
        ALL,
    )
    grad_back = exchange(grad_arrived)

    def weight_parts(rows_in, cols_in):
        return copying(
            functools.partial(expert_weights_kernel, n_tensor),
            (rows_in, cols_in),
            (1, 1),
            [((width, f), BF)] * n_tensor,
            (1,) * n_tensor,
            [all_slots, ((n_tensor, total, f), BF), ((n_tensor, width, f), BF)],
            2 * n_tensor + 1,
            ALL,
        )

    widened = lambda v: v.astype(F32)
    downs_part = weight_parts(grad_out, hidden)
    down_near = swap(downs_part[1], 1)
    down_far = (widened(downs_part[2]) + widened(swap(downs_part[3], 1))).astype(BF)
    down_got = [swap(down_far[: part(7)], 2)]
    ups_part = weight_parts(arrived, after(grad_up, down_far))
    grad_back, down_got[0], ups_part = lax.optimization_barrier((grad_back, down_got[0], ups_part))
    down_got.append(swap(down_far[part(7) :], 2))
    up_near = swap(ups_part[1], 1)
    up_far = (widened(ups_part[2]) + widened(swap(ups_part[3], 1))).astype(BF)

    grad_residual, grad_attn, vec_two, grad_router = plain(
        back_kernel,
        [row_f32, row_bf, ((2, width), F32), ((experts, width), F32)],
        *(grad_back, place, residual, g, grad_logits, gains, router),
    )

    g0 = grad_attn.reshape(x0.shape)
    g1 = swap(g0, 1)
    g2 = swap(g0, 2)
    packed = ((n_dp, dense_rows + experts, width), BF)
    others = (vec_two, grad_router, loss_part)
    h1, h0, dw, vec_one = attn_bwd(
        *(x1, x0, g1, g0, q1, q0, c1, c0, l1, l0, masks[1], masks[0], w, gains, (), heads, None)
    )
    g2, dw, up_far, down_got[1] = lax.optimization_barrier((g2, dw, up_far, down_got[1]))
    down_got = jnp.concatenate(down_got)
    up_got = [swap(up_far[: part(5)], 2)]
    g3 = swap(g2, 1)
    h3, h2, sums, _ = attn_bwd(
        *(x3, x2, g3, g2, q3, q2, c3, c2, l3, l2, masks[3], masks[2], w, gains, (dw, vec_one) + others, heads, packed)
    )
    sums, up_got[0] = lax.optimization_barrier((sums, up_got[0]))
    t1 = swap(h1, 1)
    t2 = swap((h2 + swap(h3, 1).astype(F32)).astype(BF), 2)
    up_got.append(swap(after(up_far[part(5) :], t2), 2))
    up_got = jnp.concatenate(up_got)
    grad_down_w = widened(downs_part[0]) + widened(down_near) + widened(down_got)
    grad_up_w = widened(ups_part[0]) + widened(up_near) + widened(up_got)
    [grad_tokens] = plain(
        functools.partial(last_kernel, images), [((rows, width), F32)], *(flat(x0), flat(h0), flat(t1), flat(t2), gains, grad_residual)
    )
    gathered, grad_tokens, grad_down_w, grad_up_w = lax.optimization_barrier(
        (to_all(sums), grad_tokens, grad_down_w, grad_up_w)
    )
    grad_qkv_w, grad_proj_w, small = plain(
        dense_kernel,
        [(qkv_weight.shape, F32), (proj_weight.shape, F32), ((2 * experts, dense_rows), F32)],
        gathered,
    )
    small = small + swap(small, 1) + swap(small, 2) + swap(small, 3)
    vectors = small[experts:]
    loss = vectors[4, 0] / count
    return (
        loss,
        unpad(result),
        grad_tokens,
        vectors[0],
        vectors[1],
        grad_qkv_w,
        grad_proj_w,
        vectors[2],
        vectors[3],
        small[:experts].T,
        grad_up_w[None],
        grad_down_w[None],
    )


def solution(mesh):
    rows = P(("dp", "tensor"), None)
    experts = P("dp", None, "tensor")
    in_specs = (
        rows,
        rows,
        P("dp", None),
        rows,
        P("dp"),
        P("dp"),
        experts,
        P("dp", "tensor"),
        P("dp"),
        P("dp"),
        P("dp", None),
        experts,
        experts,
    )
    out_specs = (
        P(),
        rows,
        rows,
        P("dp"),
        P("dp"),
        experts,
        P("dp", "tensor"),
        P("dp"),
        P("dp"),
        P("dp", None),
        experts,
        experts,
    )
    return jax.shard_map(local, mesh=mesh, in_specs=in_specs, out_specs=out_specs, check_vma=False)
```

time: 461 us -> 411 us (0.89)
  Pallas kernels: 81.7 us -> 123 us
  waiting for transfers between devices: 182 us -> 141 us
  matrix products: 37.4 us -> 0.81 us
  local copies, waits for them, and re-layouts: 50.3 us -> 33.8 us
    all_to_all x6 -> x5, waiting for transfers between devices: 82.9 us -> 43.4 us  [to_all(): return lax.all_to_all(v, 'dp', split_axis=0, concat_axis=0, tiled=True)]
    dot_general x9 -> x1, matrix products: 37.4 us -> 0.81 us  [dot(): lax.dot_general(a, b, (((ca,), (cb,)), ((), ())), preferred_element_type=...]
    pallas_call x8 -> x12, Pallas kernels: 59 us -> 94.2 us  [the longest x5 55.4 us: copying(): pl.pallas_call(kernel, in_specs=[spec(far) for far in in_hbm], out_specs=...]
    unnamed x151 -> x90, local copies, waits for them, and re-layouts: 30.4 us -> 18.3 us
    pallas_call x2, Pallas kernels: 22.7 us -> 29.3 us  [attn_bwd(): pl.pallas_call(functools.partial(attn_bwd_kernel, heads), grid=(images,),...]
    ppermute x26 -> x30, starting transfers between devices: 13.6 us -> 19.2 us  [swap(): return lax.ppermute(value, 'tensor', [(i, i ^ k) for i in range(n)])]
    add x2 -> x3, other arithmetic: 0.01 us -> 4.94 us  [the longest x1 3.15 us: local(): widened(downs_part[0]) + widened(down_near) + widened(down_got)]
    all_to_all x6 -> x5, starting transfers between devices: 30 us -> 27.6 us  [to_all(): return lax.all_to_all(v, 'dp', split_axis=0, concat_axis=0, tiled=True)]
  transfers between devices with their start and end apart: 32 -> 35, of which waited for: 12 -> 18; matrix products, arithmetic and copies ran while one was open for 13% -> 7% of each run, Pallas kernels for 9% -> 16%
where the time goes in v3:
time: 411 us; the launch traced here: 403 us
  waiting for transfers between devices  141 us (34%)
  Pallas kernels  123 us (30%)
  starting transfers between devices  46.8 us (11%)
  blocking collectives  41 us (10%)
  local copies, waits for them, and re-layouts  33.8 us (8%)
  other arithmetic  12 us (3%)
  between operations  4.45 us (1%)
    ppermute x30, waiting for transfers between devices, swap(): return lax.ppermute(value, 'tensor', [(i, i ^ k) for i in range(n)])  97.6 us
    pallas_call x5, Pallas kernels, copying(): pl.pallas_call(kernel, in_specs=[spec(far) for far in in_hbm], out_specs=...  55.4 us
    all_to_all x5, waiting for transfers between devices, to_all(): return lax.all_to_all(v, 'dp', split_axis=0, concat_axis=0, tiled=True)  43.4 us
    all_to_all x1, blocking collectives, to_all(): return lax.all_to_all(v, 'dp', split_axis=0, concat_axis=0, tiled=True)  41 us
    pallas_call x2, Pallas kernels, attn_bwd(): pl.pallas_call(functools.partial(attn_bwd_kernel, heads), grid=(images,),...  29.3 us
    all_to_all x5, starting transfers between devices, to_all(): return lax.all_to_all(v, 'dp', split_axis=0, concat_axis=0, tiled=True)  27.6 us
    pallas_call x5, Pallas kernels, plain(): pl.pallas_call(kernel, grid=(1,), in_specs=[whole(v.shape) for v in args]...  22.9 us
    ppermute x30, starting transfers between devices, swap(): return lax.ppermute(value, 'tensor', [(i, i ^ k) for i in range(n)])  19.2 us
  transfers between devices with their start and end apart: 35, of which 18 were waited for; matrix products, arithmetic and copies ran while one was open for 7% of the time, Pallas kernels for 16%

profile of v3, /device:TPU:0, one launch (start us, length us, event | category | flops | bytes accessed | tf_op | source)
XLA Modules:
  0.0 403.3 jit_solution(11124339106946510751)
XLA Ops:
  0.6 1.0 copy.50.qkv
  6.6 1.4 shard_map.220
  8.0 7.4 %all-to-all-start = ((bf16[8,98,768]{2,1,0:T(8,128)(2,1)}), bf16[8,98,768]{2,1,0:T(8,128)(2,1)}, u32[]{:S(2)}, u32[]{:S(2)}) async-start(bf16[8,98,768]{2,1,0:T(8,128)(2,1)} %shard_map.220), calls=%async_computation | async-start | bytes 2555904 | tf_op jit(solution)/shard_map/all_to_all | solution.py:29
  15.6 1.6 collective-permute-start
  17.2 1.1 slice_bitcast_fusion
  18.3 1.2 collective-permute-start.2
  20.2 12.8 %collective-permute-done.refs_1_.xb = bf16[2,208,768]{2,1,0:T(8,128)(2,1)S(1)} collective-permute-done((bf16[2,208,768]{2,1,0:T(8,128)(2,1)S(1)}, bf16[2,208,768]{2,1,0:T(8,128)(2,1)S(1)}, u32[]{:S(2)}, u32[]{:S(2)}) %collective-permute-start) | collective-permute-done | bytes 639008 | tf_op jit(solution)/shard_map/ppermute | solution.py:25
  33.6 12.6 %all-to-all-done = bf16[8,98,768]{2,1,0:T(8,128)(2,1)} async-done(((bf16[8,98,768]{2,1,0:T(8,128)(2,1)}), bf16[8,98,768]{2,1,0:T(8,128)(2,1)}, u32[]{:S(2)}, u32[]{:S(2)}) %all-to-all-start) | async-done | bytes 1204256 | tf_op jit(solution)/shard_map/all_to_all | solution.py:29
  46.2 1.1 slice_reduce_fusion
  48.6 2.4 slice.94
  51.0 0.9 copy-done.20
  51.9 10.6 %shard_map.222 = (bf16[2,208,576]{2,1,0:T(8,128)(2,1)}, bf16[2,208,192]{2,1,0:T(8,128)(2,1)}, f32[2,208,3]{2,1,0:T(8,128)}, bf16[2,208,768]{2,1,0:T(8,128)(2,1)}...) custom-call(bf16[2,208,768]{2,1,0:T(8,128)(2,1)} %copy-done.20, ...), custom_call_target="tpu_custom_call" | custom-call | flops 1048576 | bytes 1024 | tf_op jit(solution)/shard_map/pallas_call | solution.py:104
  63.1 1.8 collective-permute-done.5
  64.8 1.5 add_convert_fusion.3
  66.3 1.6 collective-permute-start.6
  71.0 5.3 %shard_map.221 = (bf16[2,208,576]{2,1,0:T(8,128)(2,1)}, bf16[2,208,192]{2,1,0:T(8,128)(2,1)}, f32[2,208,3]{2,1,0:T(8,128)}, f32[2,208,768]{2,1,0:T(8,128)}) custom-call(bf16[2,208,768]{2,1,0:T(8,128)(2,1)} %copy-done.7, s32[2,1,208]{2,1,0:T(1,128)} %squeeze.39.refs_1_.kb, bf16[768,768]{1,0:T(8,128)(2,1)} %bitcast.73, f32[4,768]{1,0:T(4,128)} %reshape.170.refs_3_.refs_7_.gains), custom_call_target="tpu_custom_call" | custom-call | flops 1048576 | bytes 1024 | tf_op jit(solution)/shard_map/pallas_call | solution.py:104
  76.3 6.5 %collective-permute-done.6 = bf16[2,208,768]{2,1,0:T(8,128)(2,1)S(1)} collective-permute-done((bf16[2,208,768]{2,1,0:T(8,128)(2,1)S(1)}, bf16[2,208,768]{2,1,0:T(8,128)(2,1)S(1)}, u32[]{:S(2)}, u32[]{:S(2)}) %collective-permute-start.6) | collective-permute-done | bytes 639008 | tf_op jit(solution)/shard_map/ppermute | solution.py:25
  83.6 4.6 %shard_map.223 = (f32[416,768]{1,0:T(8,128)}, f32[416,8]{1,0:T(8,128)}, bf16[1024,768]{1,0:T(8,128)(2,1)}) custom-call(bf16[416,768]{1,0:T(8,128)(2,1)} %bitcast.76, f32[416,768]{1,0:T(8,128)} %bitcast.101, bf16[416,768]{1,0:T(8,128)(2,1)} %bitcast.102, bf16[416,768]{1,0:T(8,128)(2,1)} %bitcast.103, f32[4,768]{1,0:T(4,128)} %reshape.170.refs_3_.refs_7_.gains, ...), custom_call_target="tpu_custom_call" | custom-call | flops 1048576 | bytes 1024 | tf_op jit(solution)/shard_map/pallas_call | solution.py:272
  88.2 4.3 %all-to-all-start.1 = ((bf16[8,128,768]{2,1,0:T(8,128)(2,1)}), bf16[8,128,768]{2,1,0:T(8,128)(2,1)S(1)}, u32[]{:S(2)}, u32[]{:S(2)}) async-start(bf16[8,128,768]{2,1,0:T(8,128)(2,1)} %bitcast.96), calls=%async_computation.1 | async-start | bytes 3145728 | tf_op jit(solution)/shard_map/all_to_all | solution.py:29
  92.6 1.6 collective-permute-start.11
  95.2 1.1 constant_dynamic-update-slice_fusion.1
  96.3 36.3 %collective-permute-done.8 = bf16[384,768]{1,0:T(8,128)(2,1)S(1)} collective-permute-done((bf16[384,768]{1,0:T(8,128)(2,1)S(1)}, bf16[384,768]{1,0:T(8,128)(2,1)S(1)}, u32[]{:S(2)}, u32[]{:S(2)}) %collective-permute-start.8) | collective-permute-done | bytes 589856 | tf_op jit(solution)/shard_map/ppermute | solution.py:25
  133.2 3.0 collective-permute-done.9.refs_3_
  136.3 1.0 copy-done.17
  137.4 1.1 copy-done.8
  138.5 16.0 %shard_map.224 = (bf16[1024,768]{1,0:T(8,128)(2,1)}, bf16[1024,3072]{1,0:T(8,128)(2,1)}, bf16[1024,3072]{1,0:T(8,128)(2,1)}) custom-call(bf16[1024,768]{1,0:T(8,128)(2,1)} %bitcast.80, bf16[768,768]{1,0:T(8,128)(2,1)} %bitcast.82, bf16[768,768]{1,0:T(8,128)(2,1)} %copy-done.16, bf16[768,768]{1,0:T(8,128)(2,1)} %copy-done.10, bf16[768,768]{1,0:T(8,128)(2,1)} %copy-done.17, ...), custom_call_target="tpu_custom_call" | custom-call | flops 1048576 | bytes 1024 | tf_op jit(solution)/shard_map/pallas_call | solution.py:430
  154.6 5.9 %all-to-all-start.2 = ((bf16[8,128,768]{2,1,0:T(8,128)(2,1)}), bf16[8,128,768]{2,1,0:T(8,128)(2,1)S(1)}, u32[]{:S(2)}, u32[]{:S(2)}) async-start(bf16[8,128,768]{2,1,0:T(8,128)(2,1)} %bitcast.98), calls=%async_computation.2 | async-start | bytes 3145728 | tf_op jit(solution)/shard_map/all_to_all | solution.py:29
  160.5 0.9 convert_element_type.102.mask
  161.6 1.2 reshape.158
  162.8 0.9 pad.18
  167.0 30.7 %all-to-all-done.2 = bf16[8,128,768]{2,1,0:T(8,128)(2,1)S(1)} async-done(((bf16[8,128,768]{2,1,0:T(8,128)(2,1)}), bf16[8,128,768]{2,1,0:T(8,128)(2,1)S(1)}, u32[]{:S(2)}, u32[]{:S(2)}) %all-to-all-start.2) | async-done | bytes 1572896 | tf_op jit(solution)/shard_map/all_to_all | solution.py:29
  198.9 6.5 %shard_map.225 = (bf16[416,768]{1,0:T(8,128)(2,1)}, f32[416,768]{1,0:T(8,128)}, bf16[416,8]{1,0:T(8,128)(2,1)}, f32[1,768]{1,0:T(1,128)}, bf16[1024,768]{1,0:T(8,128)(2,1)}) custom-call(bf16[1024,768]{1,0:T(8,128)(2,1)} %bitcast.86, s32[416,2]{1,0:T(8,128)} %add_select_fusion.place, s32[416,2]{1,0:T(8,128)} %bitcast.92, ...), custom_call_target="tpu_custom_call" | custom-call | flops 1048576 | bytes 1024 | tf_op jit(solution)/shard_map/pallas_call | solution.py:272
  205.4 41.0 %all_to_all.30 = bf16[8,128,768]{2,1,0:T(8,128)(2,1)} all-to-all(bf16[8,128,768]{2,1,0:T(8,128)(2,1)} %bitcast.99), channel_id=1, replica_groups=mesh['dp'=8,'tensor'=4] {'dp'}, dimensions={0} | all-to-all | bytes 3145728 | tf_op jit(solution)/shard_map/all_to_all | solution.py:29
  246.4 17.5 %shard_map.226 = (bf16[1024,3072]{1,0:T(8,128)(2,1)}, bf16[1024,768]{1,0:T(8,128)(2,1)}) custom-call(bf16[1024,768]{1,0:T(8,128)(2,1)} %bitcast.78, bf16[1024,3072]{1,0:T(8,128)(2,1)} %get-tuple-element.98.slope, bf16[768,768]{1,0:T(8,128)(2,1)} %bitcast.83, bf16[768,768]{1,0:T(8,128)(2,1)} %copy-done.16, bf16[768,768]{1,0:T(8,128)(2,1)} %copy-done.10, ...), custom_call_target="tpu_custom_call" | custom-call | flops 1048576 | bytes 1024 | tf_op jit(solution)/shard_map/pallas_call | solution.py:430
  263.9 3.8 all-to-all-start.4
  267.7 10.2 %shard_map.227 = (bf16[768,768]{1,0:T(8,128)(2,1)}, bf16[768,768]{1,0:T(8,128)(2,1)}, bf16[768,768]{1,0:T(8,128)(2,1)}, bf16[768,768]{1,0:T(8,128)(2,1)}) custom-call(bf16[1024,768]{1,0:T(8,128)(2,1)} %bitcast.79, bf16[1024,3072]{1,0:T(8,128)(2,1)} %get-tuple-element.100.cols), custom_call_target="tpu_custom_call" | custom-call | flops 1048576 | bytes 1024 | tf_op jit(solution)/shard_map/pallas_call | solution.py:430
  278.0 3.0 collective-permute-done.13
  281.1 1.6 add_convert_fusion.1
  282.8 1.6 collective-permute-start.14
  284.3 10.3 %shard_map.228 = (bf16[768,768]{1,0:T(8,128)(2,1)}, bf16[768,768]{1,0:T(8,128)(2,1)}, bf16[768,768]{1,0:T(8,128)(2,1)}, bf16[768,768]{1,0:T(8,128)(2,1)}) custom-call(bf16[1024,768]{1,0:T(8,128)(2,1)} %bitcast.81, bf16[1024,3072]{1,0:T(8,128)(2,1)} %get-tuple-element.104.cols), custom_call_target="tpu_custom_call" | custom-call | flops 1048576 | bytes 1024 | tf_op jit(solution)/shard_map/pallas_call | solution.py:430
  294.6 13.2 %collective-permute-done.14 = bf16[672,768]{1,0:T(8,128)(2,1)} collective-permute-done((bf16[672,768]{1,0:T(8,128)(2,1)S(1)}, bf16[672,768]{1,0:T(8,128)(2,1)}, u32[]{:S(2)}, u32[]{:S(2)}) %collective-permute-start.14) | collective-permute-done | bytes 1032224 | tf_op jit(solution)/shard_map/ppermute | solution.py:25
  307.8 1.1 copy-done.11
  308.9 5.1 %shard_map.229 = (f32[416,768]{1,0:T(8,128)}, bf16[416,768]{1,0:T(8,128)(2,1)}, f32[2,768]{1,0:T(2,128)}, f32[8,768]{1,0:T(8,128)}) custom-call(bf16[1024,768]{1,0:T(8,128)(2,1)} %bitcast.85, s32[416,2]{1,0:T(8,128)} %add_select_fusion.place, f32[416,768]{1,0:T(8,128)} %get-tuple-element.96.residual, f32[416,768]{1,0:T(8,128)} %get-tuple-element.110.g, ...), custom_call_target="tpu_custom_call" | custom-call | flops 1048576 | bytes 1024 | tf_op jit(solution)/shard_map/pallas_call | solution.py:272
  314.0 1.5 collective-permute-start.15
  317.2 14.7 %shard_map.230 = (bf16[2,208,768]{2,1,0:T(8,128)(2,1)}, f32[2,208,768]{2,1,0:T(8,128)}, f32[768,768]{1,0:T(8,128)}, f32[2,768]{1,0:T(2,128)}) custom-call(bf16[2,208,768]{2,1,0:T(8,128)(2,1)} %collective-permute-done.3.refs_2_.xa, bf16[2,208,768]{2,1,0:T(8,128)(2,1)} %copy-done.7, bf16[2,208,768]{2,1,0:T(8,128)(2,1)} %copy-done.29, ...), custom_call_target="tpu_custom_call" | custom-call | flops 268435456 | bytes 8388608 | tf_op jit(solution)/shard_map/pallas_call | solution.py:187
  332.1 2.1 collective-permute-done.18
  334.3 1.6 collective-permute-start.20
  337.3 14.6 %shard_map.231 = (bf16[2,208,768]{2,1,0:T(8,128)(2,1)}, f32[2,208,768]{2,1,0:T(8,128)}, bf16[8,104,768]{2,1,0:T(8,128)(2,1)}, f32[2,768]{1,0:T(2,128)}) custom-call(bf16[2,208,768]{2,1,0:T(8,128)(2,1)} %copy-done.20, bf16[2,208,768]{2,1,0:T(8,128)(2,1)} %copy-done.19, bf16[2,208,768]{2,1,0:T(8,128)(2,1)} %copy-done.24, ...), custom_call_target="tpu_custom_call" | custom-call | flops 268435456 | bytes 8388608 | tf_op jit(solution)/shard_map/pallas_call | solution.py:187
  352.2 1.1 collective-permute-done.20
  353.2 6.2 %all-to-all-start.5 = ((bf16[8,104,768]{2,1,0:T(8,128)(2,1)}), bf16[8,104,768]{2,1,0:T(8,128)(2,1)S(1)}, u32[]{:S(2)}, u32[]{:S(2)}) async-start(bf16[8,104,768]{2,1,0:T(8,128)(2,1)} %get-tuple-element.136), calls=%async_computation.5 | async-start | bytes 2555904 | tf_op jit(solution)/shard_map/all_to_all | solution.py:29
  360.0 1.7 add_convert_fusion.2
  361.7 1.6 collective-permute-start.23
  364.1 14.0 %collective-permute-done.23 = bf16[2,208,768]{2,1,0:T(8,128)(2,1)S(1)} collective-permute-done((bf16[2,208,768]{2,1,0:T(8,128)(2,1)S(1)}, bf16[2,208,768]{2,1,0:T(8,128)(2,1)S(1)}, u32[]{:S(2)}, u32[]{:S(2)}) %collective-permute-start.23) | collective-permute-done | bytes 639008 | tf_op jit(solution)/shard_map/ppermute | solution.py:25
  378.2 1.5 collective-permute-start.26
  379.7 3.1 convert_add_fusion.1
  382.8 0.8 copy-done.28
  383.7 4.3 %shard_map.232 = f32[394,768]{1,0:T(8,128)} custom-call(bf16[416,768]{1,0:T(8,128)(2,1)} %bitcast.77, f32[416,768]{1,0:T(8,128)} %bitcast.100, bf16[416,768]{1,0:T(8,128)(2,1)} %bitcast.105, bf16[416,768]{1,0:T(8,128)(2,1)} %bitcast.104, f32[4,768]{1,0:T(4,128)} %reshape.170.refs_3_.refs_7_.gains, f32[416,768]{1,0:T(8,128)} %get-tuple-element.141.grad_residual), custom_call_target="tpu_custom_call" | custom-call | flops 1048576 | bytes 1024 | tf_op jit(solution)/shard_map/pallas_call | solution.py:272
  388.0 1.6 collective-permute-done.26
  389.7 1.8 convert_add_fusion
  391.5 1.1 copy-done.13
  392.5 2.3 shard_map.233
  394.9 1.5 collective-permute-start.28
  396.8 0.9 reshape.169
  398.7 0.9 collective-permute-done.29
  (161 shorter events, 25.4 us)
Async XLA Ops:
  8.0 7.4 %copy-start.30 = (bf16[394,768]{1,0:T(8,128)(2,1)S(1)}, bf16[394,768]{1,0:T(8,128)(2,1)}, u32[]{:S(2)}) copy-start(bf16[394,768]{1,0:T(8,128)(2,1)} %param.13) | copy-start | bytes 1815556
  8.0 38.2 %all-to-all-start = ((bf16[8,98,768]{2,1,0:T(8,128)(2,1)}), bf16[8,98,768]{2,1,0:T(8,128)(2,1)}, u32[]{:S(2)}, u32[]{:S(2)}) async-start(bf16[8,98,768]{2,1,0:T(8,128)(2,1)} %shard_map.220), calls=%async_computation | async-start | bytes 2555904 | tf_op jit(solution)/shard_map/all_to_all | solution.py:29
  15.4 1.8 copy-start.9
  15.6 31.7 %copy-start.7 = (bf16[2,208,768]{2,1,0:T(8,128)(2,1)}, bf16[2,208,768]{2,1,0:T(8,128)(2,1)S(1)}, u32[]{:S(2)}) copy-start(bf16[2,208,768]{2,1,0:T(8,128)(2,1)S(1)} %pad.15.refs_0_.xb) | copy-start | bytes 1916932
  15.6 3.9 copy-start.2
  15.6 17.4 %collective-permute-start = (bf16[2,208,768]{2,1,0:T(8,128)(2,1)S(1)}, bf16[2,208,768]{2,1,0:T(8,128)(2,1)S(1)}, u32[]{:S(2)}, u32[]{:S(2)}) collective-permute-start(bf16[2,208,768]{2,1,0:T(8,128)(2,1)S(1)} %pad.15.refs_0_.xb), channel_id=1, source_target_pairs={{0,2},{1,3},{2,0},{3,1},{4,6},{5,7},{6,4},{7,5},{8,10},{9,11},{10,... | collective-permute-start | bytes 1916936 | tf_op jit(solution)/shard_map/ppermute | solution.py:25
  17.2 33.8 %collective-permute-start.3 = (bf16[2,208,768]{2,1,0:T(8,128)(2,1)S(1)}, bf16[2,208,768]{2,1,0:T(8,128)(2,1)}, u32[]{:S(2)}, u32[]{:S(2)}) collective-permute-start(bf16[2,208,768]{2,1,0:T(8,128)(2,1)S(1)} %pad.15.refs_0_.xb), channel_id=1, source_target_pairs={{0,1},{1,0},{2,3},{3,2},{4,5},{5,4},{6,7},{7,6},{8,9},{9,8},{10,11... | collective-permute-start | bytes 1916936 | tf_op jit(solution)/shard_map/ppermute | solution.py:25
  18.3 32.7 %collective-permute-start.2 = (bf16[384,768]{1,0:T(8,128)(2,1)}, bf16[384,768]{1,0:T(8,128)(2,1)}, u32[]{:S(2)}, u32[]{:S(2)}) collective-permute-start(bf16[384,768]{1,0:T(8,128)(2,1)} %get-tuple-element.199), channel_id=1, source_target_pairs={{0,2},{1,3},{2,0},{3,1},{4,6},{5,7},{6,4},{7,5},{8,10},{9,11},{10,... | collective-permute-start | bytes 1769480 | tf_op jit(solution)/shard_map/ppermute | solution.py:25
  33.0 18.0 %copy-start.19 = (bf16[2,208,768]{2,1,0:T(8,128)(2,1)}, bf16[2,208,768]{2,1,0:T(8,128)(2,1)S(1)}, u32[]{:S(2)}) copy-start(bf16[2,208,768]{2,1,0:T(8,128)(2,1)S(1)} %collective-permute-done.refs_1_.xb) | copy-start | bytes 1916932
  33.0 18.0 %collective-permute-start.1 = (bf16[2,208,768]{2,1,0:T(8,128)(2,1)S(1)}, bf16[2,208,768]{2,1,0:T(8,128)(2,1)S(1)}, u32[]{:S(2)}, u32[]{:S(2)}) collective-permute-start(bf16[2,208,768]{2,1,0:T(8,128)(2,1)S(1)} %collective-permute-done.refs_1_.xb), channel_id=1, source_target_pairs={{0,1},{1,0},{2,3},{3,2},{4,5},{5,4},{6,7},{7,6},{8,9},{9,8},{10,11... | collective-permute-start | bytes 1916936 | tf_op jit(solution)/shard_map/ppermute | solution.py:25
  62.5 2.4 collective-permute-start.5
  62.6 13.7 %collective-permute-start.4 = (bf16[2,208,768]{2,1,0:T(8,128)(2,1)}, bf16[2,208,768]{2,1,0:T(8,128)(2,1)S(1)}, u32[]{:S(2)}, u32[]{:S(2)}) collective-permute-start(bf16[2,208,768]{2,1,0:T(8,128)(2,1)} %get-tuple-element.87), channel_id=1, source_target_pairs={{0,1},{1,0},{2,3},{3,2},{4,5},{5,4},{6,7},{7,6},{8,9},{9,8},{10,11... | collective-permute-start | bytes 1916936 | tf_op jit(solution)/shard_map/ppermute | solution.py:25
  64.8 4.2 %copy-start.40 = (s32[394,2]{0,1:T(2,128)S(1)}, s32[394,2]{0,1:T(2,128)}, u32[]{:S(2)}) copy-start(s32[394,2]{0,1:T(2,128)} %param.16) | copy-start | bytes 9460
  66.3 16.5 %collective-permute-start.6 = (bf16[2,208,768]{2,1,0:T(8,128)(2,1)S(1)}, bf16[2,208,768]{2,1,0:T(8,128)(2,1)S(1)}, u32[]{:S(2)}, u32[]{:S(2)}) collective-permute-start(bf16[2,208,768]{2,1,0:T(8,128)(2,1)S(1)} %add_convert_fusion.3), channel_id=1, source_target_pairs={{0,2},{1,3},{2,0},{3,1},{4,6},{5,7},{6,4},{7,5},{8,10},{9,11},{10,... | collective-permute-start | bytes 1916936 | tf_op jit(solution)/shard_map/ppermute | solution.py:25
  69.3 94.4 %copy-start.18 = (s32[2,208,2]{2,1,0:T(8,128)}, s32[2,208,2]{2,1,0:T(8,128)S(1)}, u32[]{:S(2)}) copy-start(s32[2,208,2]{2,1,0:T(8,128)S(1)} %pad.17) | copy-start | bytes 9988
  76.3 6.5 %copy-start.25 = (bf16[2,208,768]{2,1,0:T(8,128)(2,1)}, bf16[2,208,768]{2,1,0:T(8,128)(2,1)S(1)}, u32[]{:S(2)}) copy-start(bf16[2,208,768]{2,1,0:T(8,128)(2,1)S(1)} %collective-permute-done.4) | copy-start | bytes 1916932
  88.2 5.9 %copy-start.32 = (bf16[384,768]{1,0:T(8,128)(2,1)S(1)}, bf16[384,768]{1,0:T(8,128)(2,1)}, u32[]{:S(2)}) copy-start(bf16[384,768]{1,0:T(8,128)(2,1)} %get-tuple-element.92) | copy-start | bytes 1769476
  88.2 49.1 %all-to-all-start.1 = ((bf16[8,128,768]{2,1,0:T(8,128)(2,1)}), bf16[8,128,768]{2,1,0:T(8,128)(2,1)S(1)}, u32[]{:S(2)}, u32[]{:S(2)}) async-start(bf16[8,128,768]{2,1,0:T(8,128)(2,1)} %bitcast.96), calls=%async_computation.1 | async-start | bytes 3145728 | tf_op jit(solution)/shard_map/all_to_all | solution.py:29
  92.6 40.2 %collective-permute-start.11 = (bf16[768,768]{1,0:T(8,128)(2,1)}, bf16[768,768]{1,0:T(8,128)(2,1)S(1)}, u32[]{:S(2)}, u32[]{:S(2)}) collective-permute-start(bf16[768,768]{1,0:T(8,128)(2,1)} %bitcast.87), channel_id=1, source_target_pairs={{0,2},{1,3},{2,0},{3,1},{4,6},{5,7},{6,4},{7,5},{8,10},{9,11},{10,... | collective-permute-start | bytes 3538952 | tf_op jit(solution)/shard_map/ppermute | solution.py:25
  94.2 38.4 %collective-permute-start.8 = (bf16[384,768]{1,0:T(8,128)(2,1)S(1)}, bf16[384,768]{1,0:T(8,128)(2,1)S(1)}, u32[]{:S(2)}, u32[]{:S(2)}) collective-permute-start(bf16[384,768]{1,0:T(8,128)(2,1)S(1)} %copy-done.32), channel_id=1, source_target_pairs={{0,2},{1,3},{2,0},{3,1},{4,6},{5,7},{6,4},{7,5},{8,10},{9,11},{10,... | collective-permute-start | bytes 1769480 | tf_op jit(solution)/shard_map/ppermute | solution.py:25
  94.7 38.6 %collective-permute-start.10 = (bf16[768,768]{1,0:T(8,128)(2,1)}, bf16[768,768]{1,0:T(8,128)(2,1)S(1)}, u32[]{:S(2)}, u32[]{:S(2)}) collective-permute-start(bf16[768,768]{1,0:T(8,128)(2,1)} %bitcast.88), channel_id=1, source_target_pairs={{0,1},{1,0},{2,3},{3,2},{4,5},{5,4},{6,7},{7,6},{8,9},{9,8},{10,11... | collective-permute-start | bytes 3538952 | tf_op jit(solution)/shard_map/ppermute | solution.py:25
  94.7 38.6 %collective-permute-start.7 = (bf16[768,768]{1,0:T(8,128)(2,1)S(1)}, bf16[768,768]{1,0:T(8,128)(2,1)S(1)}, u32[]{:S(2)}, u32[]{:S(2)}) collective-permute-start(bf16[768,768]{1,0:T(8,128)(2,1)S(1)} %bitcast.84), channel_id=1, source_target_pairs={{0,1},{1,0},{2,3},{3,2},{4,5},{5,4},{6,7},{7,6},{8,9},{9,8},{10,11... | collective-permute-start | bytes 3538952 | tf_op jit(solution)/shard_map/ppermute | solution.py:25
  132.6 3.6 copy-start.10
  132.6 3.6 collective-permute-start.9
  132.7 3.5 copy-start.14
  132.7 4.6 %collective-permute-start.12 = (bf16[768,768]{1,0:T(8,128)(2,1)S(1)}, bf16[768,768]{1,0:T(8,128)(2,1)}, u32[]{:S(2)}, u32[]{:S(2)}) collective-permute-start(bf16[768,768]{1,0:T(8,128)(2,1)S(1)} %collective-permute-done.11.refs_6_), channel_id=1, source_target_pairs={{0,1},{1,0},{2,3},{3,2},{4,5},{5,4},{6,7},{7,6},{8,9},{9,8},{10,11... | collective-permute-start | bytes 3538952 | tf_op jit(solution)/shard_map/ppermute | solution.py:25
  133.2 3.0 copy-start.15
  133.2 3.0 copy-start.16
  136.3 1.0 copy-start.17
  137.4 1.1 copy-start.8
  154.5 6.0 %copy-start.38 = (f32[1,2,1,208]{3,1,2,0:T(2,128)S(1)}, f32[1,2,1,208]{3,1,2,0:T(2,128)}, u32[]{:S(2)}) copy-start(f32[1,2,1,208]{3,1,2,0:T(2,128)} %get-tuple-element.194) | copy-start | bytes 4996
  154.6 6.9 %copy-start.34 = (s32[416,8]{0,1:T(8,128)S(1)}, s32[416,8]{0,1:T(8,128)}, u32[]{:S(2)}) copy-start(s32[416,8]{0,1:T(8,128)} %fusion) | copy-start | bytes 39940
  154.6 6.8 %copy-start.36 = (s32[416,2]{0,1:T(2,128)S(1)}, s32[416,2]{0,1:T(2,128)}, u32[]{:S(2)}) copy-start(s32[416,2]{0,1:T(2,128)} %copy-done.35) | copy-start | bytes 9988
  154.6 43.2 %all-to-all-start.2 = ((bf16[8,128,768]{2,1,0:T(8,128)(2,1)}), bf16[8,128,768]{2,1,0:T(8,128)(2,1)S(1)}, u32[]{:S(2)}, u32[]{:S(2)}) async-start(bf16[8,128,768]{2,1,0:T(8,128)(2,1)} %bitcast.98), calls=%async_computation.2 | async-start | bytes 3145728 | tf_op jit(solution)/shard_map/all_to_all | solution.py:29
  197.7 1.1 copy-start.12
  263.9 43.9 %all-to-all-start.4 = ((bf16[8,128,768]{2,1,0:T(8,128)(2,1)}), bf16[8,128,768]{2,1,0:T(8,128)(2,1)S(1)}, u32[]{:S(2)}, u32[]{:S(2)}) async-start(bf16[8,128,768]{2,1,0:T(8,128)(2,1)} %bitcast.97), calls=%async_computation.4 | async-start | bytes 3145728 | tf_op jit(solution)/shard_map/all_to_all | solution.py:29
  278.0 3.1 collective-permute-start.13
  282.8 25.0 %collective-permute-start.14 = (bf16[672,768]{1,0:T(8,128)(2,1)S(1)}, bf16[672,768]{1,0:T(8,128)(2,1)}, u32[]{:S(2)}, u32[]{:S(2)}) collective-permute-start(bf16[672,768]{1,0:T(8,128)(2,1)S(1)} %slice.99), channel_id=1, source_target_pairs={{0,2},{1,3},{2,0},{3,1},{4,6},{5,7},{6,4},{7,5},{8,10},{9,11},{10,... | collective-permute-start | bytes 3096584 | tf_op jit(solution)/shard_map/ppermute | solution.py:25
  307.8 1.1 copy-start.11
  307.8 24.0 %collective-permute-start.17 = (bf16[768,768]{1,0:T(8,128)(2,1)}, bf16[768,768]{1,0:T(8,128)(2,1)S(1)}, u32[]{:S(2)}, u32[]{:S(2)}) collective-permute-start(bf16[768,768]{1,0:T(8,128)(2,1)} %get-tuple-element.121), channel_id=1, source_target_pairs={{0,1},{1,0},{2,3},{3,2},{4,5},{5,4},{6,7},{7,6},{8,9},{9,8},{10,11... | collective-permute-start | bytes 3538952 | tf_op jit(solution)/shard_map/ppermute | solution.py:25
  314.0 2.3 collective-permute-start.16
  314.0 20.2 %collective-permute-start.15 = (bf16[2,208,768]{2,1,0:T(8,128)(2,1)}, bf16[2,208,768]{2,1,0:T(8,128)(2,1)}, u32[]{:S(2)}, u32[]{:S(2)}) collective-permute-start(bf16[2,208,768]{2,1,0:T(8,128)(2,1)} %bitcast.107), channel_id=1, source_target_pairs={{0,2},{1,3},{2,0},{3,1},{4,6},{5,7},{6,4},{7,5},{8,10},{9,11},{10,... | collective-permute-start | bytes 1916936 | tf_op jit(solution)/shard_map/ppermute | solution.py:25
  315.6 18.6 %collective-permute-start.18 = (bf16[96,768]{1,0:T(8,128)(2,1)S(1)}, bf16[96,768]{1,0:T(8,128)(2,1)S(1)}, u32[]{:S(2)}, u32[]{:S(2)}) collective-permute-start(bf16[96,768]{1,0:T(8,128)(2,1)S(1)} %slice.100), channel_id=1, source_target_pairs={{0,2},{1,3},{2,0},{3,1},{4,6},{5,7},{6,4},{7,5},{8,10},{9,11},{10,... | collective-permute-start | bytes 442376 | tf_op jit(solution)/shard_map/ppermute | solution.py:25
  317.2 14.7 %copy-start.21 = (bf16[768,768]{1,0:T(8,128)(2,1)S(1)}, bf16[768,768]{1,0:T(8,128)(2,1)}, u32[]{:S(2)}) copy-start(bf16[768,768]{1,0:T(8,128)(2,1)} %get-tuple-element.120) | copy-start | bytes 3538948
  334.2 2.3 collective-permute-start.19
  334.3 19.0 %collective-permute-start.20 = (bf16[480,768]{1,0:T(8,128)(2,1)S(1)}, bf16[480,768]{1,0:T(8,128)(2,1)S(1)}, u32[]{:S(2)}, u32[]{:S(2)}) collective-permute-start(bf16[480,768]{1,0:T(8,128)(2,1)S(1)} %slice.85), channel_id=1, source_target_pairs={{0,2},{1,3},{2,0},{3,1},{4,6},{5,7},{6,4},{7,5},{8,10},{9,11},{10,... | collective-permute-start | bytes 2211848 | tf_op jit(solution)/shard_map/ppermute | solution.py:25
  352.0 8.0 %collective-permute-start.22 = (bf16[2,208,768]{2,1,0:T(8,128)(2,1)}, bf16[2,208,768]{2,1,0:T(8,128)(2,1)}, u32[]{:S(2)}, u32[]{:S(2)}) collective-permute-start(bf16[2,208,768]{2,1,0:T(8,128)(2,1)} %get-tuple-element.140), channel_id=1, source_target_pairs={{0,1},{1,0},{2,3},{3,2},{4,5},{5,4},{6,7},{7,6},{8,9},{9,8},{10,11... | collective-permute-start | bytes 1916936 | tf_op jit(solution)/shard_map/ppermute | solution.py:25
  353.2 38.2 %all-to-all-start.5 = ((bf16[8,104,768]{2,1,0:T(8,128)(2,1)}), bf16[8,104,768]{2,1,0:T(8,128)(2,1)S(1)}, u32[]{:S(2)}, u32[]{:S(2)}) async-start(bf16[8,104,768]{2,1,0:T(8,128)(2,1)} %get-tuple-element.136), calls=%async_computation.5 | async-start | bytes 2555904 | tf_op jit(solution)/shard_map/all_to_all | solution.py:29
  359.4 20.3 %collective-permute-start.24 = (bf16[768,768]{1,0:T(8,128)(2,1)}, bf16[768,768]{1,0:T(8,128)(2,1)S(1)}, u32[]{:S(2)}, u32[]{:S(2)}) collective-permute-start(bf16[768,768]{1,0:T(8,128)(2,1)} %get-tuple-element.143), channel_id=1, source_target_pairs={{0,1},{1,0},{2,3},{3,2},{4,5},{5,4},{6,7},{7,6},{8,9},{9,8},{10,11... | collective-permute-start | bytes 3538952 | tf_op jit(solution)/shard_map/ppermute | solution.py:25
  359.5 28.5 %collective-permute-start.25 = (bf16[768,768]{1,0:T(8,128)(2,1)}, bf16[768,768]{1,0:T(8,128)(2,1)S(1)}, u32[]{:S(2)}, u32[]{:S(2)}) collective-permute-start(bf16[768,768]{1,0:T(8,128)(2,1)} %get-tuple-element.147), channel_id=1, source_target_pairs={{0,1},{1,0},{2,3},{3,2},{4,5},{5,4},{6,7},{7,6},{8,9},{9,8},{10,11... | collective-permute-start | bytes 3538952 | tf_op jit(solution)/shard_map/ppermute | solution.py:25
  360.0 3.3 copy-start.41
  360.0 19.7 %copy-start.23 = (bf16[768,768]{1,0:T(8,128)(2,1)S(1)}, bf16[768,768]{1,0:T(8,128)(2,1)}, u32[]{:S(2)}) copy-start(bf16[768,768]{1,0:T(8,128)(2,1)} %get-tuple-element.142) | copy-start | bytes 3538948
  361.7 16.4 %collective-permute-start.23 = (bf16[2,208,768]{2,1,0:T(8,128)(2,1)S(1)}, bf16[2,208,768]{2,1,0:T(8,128)(2,1)S(1)}, u32[]{:S(2)}, u32[]{:S(2)}) collective-permute-start(bf16[2,208,768]{2,1,0:T(8,128)(2,1)S(1)} %add_convert_fusion.2), channel_id=1, source_target_pairs={{0,2},{1,3},{2,0},{3,1},{4,6},{5,7},{6,4},{7,5},{8,10},{9,11},{10,... | collective-permute-start | bytes 1916936 | tf_op jit(solution)/shard_map/ppermute | solution.py:25
  363.3 19.5 %collective-permute-start.21 = (bf16[2,208,768]{2,1,0:T(8,128)(2,1)S(1)}, bf16[2,208,768]{2,1,0:T(8,128)(2,1)S(1)}, u32[]{:S(2)}, u32[]{:S(2)}) collective-permute-start(bf16[2,208,768]{2,1,0:T(8,128)(2,1)S(1)} %copy-done.41), channel_id=1, source_target_pairs={{0,1},{1,0},{2,3},{3,2},{4,5},{5,4},{6,7},{7,6},{8,9},{9,8},{10,11... | collective-permute-start | bytes 1916936 | tf_op jit(solution)/shard_map/ppermute | solution.py:25
  378.2 4.7 %copy-start.27 = (bf16[2,208,768]{2,1,0:T(8,128)(2,1)}, bf16[2,208,768]{2,1,0:T(8,128)(2,1)S(1)}, u32[]{:S(2)}) copy-start(bf16[2,208,768]{2,1,0:T(8,128)(2,1)S(1)} %collective-permute-done.23) | copy-start | bytes 1916932
  378.2 11.5 %collective-permute-start.26 = (bf16[288,768]{1,0:T(8,128)(2,1)}, bf16[288,768]{1,0:T(8,128)(2,1)S(1)}, u32[]{:S(2)}, u32[]{:S(2)}) collective-permute-start(bf16[288,768]{1,0:T(8,128)(2,1)} %slice.86), channel_id=1, source_target_pairs={{0,2},{1,3},{2,0},{3,1},{4,6},{5,7},{6,4},{7,5},{8,10},{9,11},{10,... | collective-permute-start | bytes 1327112 | tf_op jit(solution)/shard_map/ppermute | solution.py:25
  383.7 6.0 %copy-start.22 = (bf16[768,768]{1,0:T(8,128)(2,1)S(1)}, bf16[768,768]{1,0:T(8,128)(2,1)}, u32[]{:S(2)}) copy-start(bf16[768,768]{1,0:T(8,128)(2,1)} %get-tuple-element.146) | copy-start | bytes 3538948
  391.5 5.3 %copy-start.31 = (bf16[416,768]{1,0:T(8,128)(2,1)S(1)}, bf16[416,768]{1,0:T(8,128)(2,1)}, u32[]{:S(2)}) copy-start(bf16[416,768]{1,0:T(8,128)(2,1)} %get-tuple-element.152) | copy-start | bytes 1916932
  391.5 1.1 copy-start.13
  394.9 2.9 copy-start.33
  394.9 3.6 collective-permute-start.27
  394.9 3.9 collective-permute-start.28
  396.4 3.3 collective-permute-start.29
  396.7 2.9 copy-start.39
  (13 other events, 9.8 us)

commit v4 on v3

--- a/solution.py
+++ b/solution.py
@@ -70,6 +70,16 @@
 
 def attn_fwd_kernel(heads, n, *refs):
     xs, keeps, (w_ref, gains), outs = refs[:n], refs[n : 2 * n], refs[2 * n : 2 * n + 2], refs[2 * n + 2 :]
+    if len(w_ref.shape) == 3:
+        unpacked = outs[-1]
+
+        @pl.when(pl.program_id(0) == 0)
+        def _():
+            rows = unpacked.shape[0] // w_ref.shape[0]
+            for k in range(w_ref.shape[0]):
+                unpacked[k * rows : (k + 1) * rows] = w_ref[k, :rows]
+
+        w_ref = unpacked
     w = w_ref[...]
     gain, shift = gains[0:1], gains[1:2]
     for i in range(n):
@@ -105,12 +115,13 @@
         functools.partial(attn_fwd_kernel, heads, len(xs)),
         grid=(images,),
         in_specs=[each((rows, width)) for _ in xs] + [each((1, rows)) for _ in xs] + [whole(w.shape), whole(gains.shape)],
-        out_specs=[each(s) for s, _ in outs],
-        out_shape=[jax.ShapeDtypeStruct((images,) + s, d) for s, d in outs],
+        out_specs=[each(s) for s, _ in outs] + [whole((width, width))] * (w.ndim - 2),
+        out_shape=[jax.ShapeDtypeStruct((images,) + s, d) for s, d in outs]
+        + [jax.ShapeDtypeStruct((width, width), BF)] * (w.ndim - 2),
         compiler_params=params(ALL),
         cost_estimate=CHEAP,
     )(*xs, *keeps, w, gains)
-    return [made[4 * i : 4 * i + 4] for i in range(len(xs))]
+    return [made[4 * i : 4 * i + 4] for i in range(len(xs))] + list(made[4 * len(xs) :])
 
 
 def one_image_back(x, ga, qkv, context, lse, keep, w, gain, shift, heads):
@@ -291,36 +302,29 @@
         return copy
 
 
-def dense_kernel(parts, qkv, proj, small):
-    total = parts[0].astype(F32)
+def dense_kernel(parts, qkv, proj):
+    rows, c = proj.shape
+    total = parts[0, :rows].astype(F32)
     for k in range(1, parts.shape[0]):
-        total = total + parts[k].astype(F32)
-    rows, c = proj.shape
+        total = total + parts[k, :rows].astype(F32)
     for i in range(3):
-        qkv[:, i, :] = total[:rows, i * c : (i + 1) * c]
-    proj[...] = total[:rows, 3 * c :]
-    last = total[rows:]
-    piece = lambda i: last[:, i * rows : (i + 1) * rows]
-    small[...] = jnp.concatenate([piece(0) + piece(1), piece(2) + piece(3)], 0)
-
-
-def shard_kernel(qkv, proj, g1, s1, g2, s2, router, mask, out, block, sems):
+        qkv[:, i, :] = total[:, i * c : (i + 1) * c]
+    proj[...] = total[:, 3 * c :]
+
+
+def shard_kernel(qkv, proj, g1, s1, g2, s2, router, mask, out):
     weights = jnp.concatenate([qkv[:, i, :] for i in range(3)] + [proj[...]], 1)
     rows, width = weights.shape
     count = jnp.sum(jnp.sum(mask[...].astype(F32), 1, keepdims=True), 0, keepdims=True)
     high = jnp.floor(count / 128)
     vectors = [v[...].astype(F32) for v in (g1, s1, g2, s2)] + [high, count - 128 * high]
     vectors.append(jnp.zeros((1, width - 4 * rows - 2), F32))
-    at = [lax.broadcasted_iota(jnp.int32, (rows, rows), i) for i in (0, 1)]
-    turned = dot(router[...], jnp.where(at[0] == at[1], 1.0, 0.0).astype(BF), 0, 0)
+    turned = router[...].astype(F32)
     last = jnp.concatenate([turned[e : e + 1] for e in range(turned.shape[0])], 1)
     extra = jnp.concatenate([jnp.concatenate(vectors, 1), last], 0)
-    block[...] = jnp.concatenate([weights, extra.astype(BF)], 0)
-    copies = Copies(sems)
+    block = jnp.concatenate([weights, extra.astype(BF)], 0)
     for k in range(out.shape[0]):
-        copies.start(block, out.at[k])
-    for copy in copies.made:
-        copy.wait()
+        out[k] = block
 
 
 def gelu_parts(u):
@@ -329,88 +333,102 @@
     return u * phi, phi + u * bell * 0.3989422804014327
 
 
-def side_by_side(refs):
-    return jnp.concatenate([r[...] for r in refs], 1)
-
-
-def over_chunks(rows, step, body):
-    def one(i, carry):
-        body(pl.ds(pl.multiple_of(i * step, step), step))
-        return carry
-
-    lax.fori_loop(0, rows // step, one, 0)
-
-
-def expert_fwd_kernel(n, step, x, *refs):
-    ups, downs, (out, hidden, slope) = refs[:n], refs[n : 2 * n], refs[2 * n : 2 * n + 3]
-    wu, wd, hs, ss, os, sems = refs[2 * n + 3 :]
+class Pieces:
+    def __init__(self, lists):
+        self.arrays = [v for pieces in lists for v in pieces]
+        self.plan = []
+        for pieces in lists:
+            ends = [sum(v.shape[0] for v in pieces[: i + 1]) for i in range(len(pieces))]
+            self.plan.append([(end - v.shape[0], v.shape[0]) for end, v in zip(ends, pieces)])
+
+    def starter(self, copies, refs, target):
+        refs, made = iter(refs), []
+        for t, pieces in enumerate(self.plan):
+            made.append([(next(refs), target.at[t, slice(at, at + size)]) for at, size in pieces])
+        return lambda t: [copies.start(*pair) for pair in made[t]]
+
+
+def wait_all(copies):
+    for copy in copies:
+        copy.wait()
+
+
+def expert_fwd_kernel(ups, downs, step, x, *refs):
+    count = len(ups.arrays), len(downs.arrays)
+    (out, hidden, slope), (wu, wd, hs, ss, os, sems) = refs[-9:-6], refs[-6:]
     copies = Copies(sems)
-    f = wu.shape[2]
-    up_in = [copies.start(ups[t], wu.at[t]) for t in range(n)]
-    down_in = []
-    outgoing = []
-    for row in range(0, x.shape[0], step):
-        at = slice(row, row + step)
-        for t in range(n):
-            cols = slice(t * f, (t + 1) * f)
-            if row == 0:
-                up_in[t].wait()
-                if t == 0:
-                    down_in = [copies.start(downs[i], wd.at[i]) for i in range(n)]
-            value, der = gelu_parts(dot(x[at], wu[t], 1, 0))
-            hs[at, cols] = value.astype(BF)
-            ss[at, cols] = der.astype(BF)
-        outgoing.append(copies.start(hs.at[at], hidden.at[at]))
-        outgoing.append(copies.start(ss.at[at], slope.at[at]))
-        if row == 0:
-            for copy in down_in:
-                copy.wait()
-        os[at] = dot(hs[at], jnp.concatenate([wd[t] for t in range(n)], 1), 1, 1).astype(BF)
-        outgoing.append(copies.start(os.at[at], out.at[at]))
-    for copy in outgoing:
-        copy.wait()
-
-
-def expert_bwd_kernel(n, step, go, slope, *refs):
-    ups, downs, (grad_up, out) = refs[:n], refs[n : 2 * n], refs[2 * n : 2 * n + 2]
-    wu, wd, gs, ss, os, sems = refs[2 * n + 2 :]
-    copies = Copies(sems)
-    f = wu.shape[2]
-    rows = go.shape[0]
-    chunks = [slice(row, row + step) for row in range(0, rows, step)]
-    down_in = [copies.start(downs[0], wd.at[0])]
-    slope_in = [copies.start(slope.at[chunks[0]], ss.at[chunks[0]])]
-    up_in = []
-    outgoing = []
+    start_up = ups.starter(copies, refs[: count[0]], wu)
+    start_down = downs.starter(copies, refs[count[0] : sum(count)], wd)
+    n, f = wu.shape[0], wu.shape[2]
+    chunks = [slice(row, row + step) for row in range(0, x.shape[0], step)]
+    ready, down_in, outgoing = [start_up(t) for t in range(min(2, n))], [], []
     for i, at in enumerate(chunks):
         for t in range(n):
             cols = slice(t * f, (t + 1) * f)
             if i == 0:
-                down_in[t].wait()
-            if t == 0:
-                slope_in[i].wait()
-                if i == 0:
-                    down_in += [copies.start(downs[j], wd.at[j]) for j in range(1, n)]
-                    up_in = [copies.start(ups[j], wu.at[j]) for j in range(n)]
-                    slope_in += [copies.start(slope.at[later], ss.at[later]) for later in chunks[1:]]
+                wait_all(ready[t])
+                if t + 2 < n:
+                    ready.append(start_up(t + 2))
+            value, der = gelu_parts(dot(x[at], wu[t], 1, 0))
+            hs[at, cols] = value.astype(BF)
+            ss[at, cols] = der.astype(BF)
+        for t in range(i * n // len(chunks), (i + 1) * n // len(chunks)):
+            down_in += start_down(t)
+        outgoing.append(copies.start(hs.at[at], hidden.at[at]))
+        outgoing.append(copies.start(ss.at[at], slope.at[at]))
+    wait_all(down_in)
+    for at in chunks:
+        os[at] = dot(hs[at], jnp.concatenate([wd[t] for t in range(n)], 1), 1, 1).astype(BF)
+        outgoing.append(copies.start(os.at[at], out.at[at]))
+    wait_all(outgoing)
+
+
+def expert_bwd_kernel(ups, downs, step, go, slope, *refs):
+    count = len(ups.arrays), len(downs.arrays)
+    (grad_up, out), (wu, wd, gs, ss, os, sems) = refs[-8:-6], refs[-6:]
+    copies = Copies(sems)
+    start_up = ups.starter(copies, refs[: count[0]], wu)
+    start_down = downs.starter(copies, refs[count[0] : sum(count)], wd)
+    n, f = wu.shape[0], wu.shape[2]
+    chunks = [slice(row, row + step) for row in range(0, go.shape[0], step)]
+    def start_first(t):
+        cols = slice(t * f, (t + 1) * f)
+        return start_down(t) + [copies.start(slope.at[chunks[0], cols], ss.at[chunks[0], cols])]
+
+    ready, slope_in = [start_first(t) for t in range(min(2, n))], [None]
+    up_in, outgoing = [], []
+    for i, at in enumerate(chunks):
+        if i > 0:
+            slope_in[i].wait()
+        if 0 < i and i + 1 < len(chunks):
+            slope_in.append(copies.start(slope.at[chunks[i + 1]], ss.at[chunks[i + 1]]))
+        for t in range(n):
+            cols = slice(t * f, (t + 1) * f)
+            if i == 0:
+                wait_all(ready[t])
+                if t + 2 < n:
+                    ready.append(start_first(t + 2))
+                elif t + 2 == n and len(chunks) > 1:
+                    slope_in.append(copies.start(slope.at[chunks[1]], ss.at[chunks[1]]))
             grad_hidden = dot(go[at], wd[t], 1, 0)
             gs[at, cols] = (grad_hidden * ss[at, cols].astype(F32)).astype(BF)
+        for t in range(i * n // len(chunks), (i + 1) * n // len(chunks)):
+            up_in += start_up(t)
         outgoing.append(copies.start(gs.at[at], grad_up.at[at]))
-        if i == 0:
-            for copy in up_in:
-                copy.wait()
+    wait_all(up_in)
+    for at in chunks:
         os[at] = dot(gs[at], jnp.concatenate([wu[t] for t in range(n)], 1), 1, 1).astype(BF)
         outgoing.append(copies.start(os.at[at], out.at[at]))
-    for copy in outgoing:
-        copy.wait()
-
-
-def expert_weights_kernel(n, rows, cols, *refs):
+    wait_all(outgoing)
+
+
+def expert_weights_kernel(parts, rows, cols, *refs):
+    n = len(parts)
     outs, (rs, cs, os, sems) = refs[:n], refs[n:]
     copies = Copies(sems)
     f = os.shape[2]
     rows_in = copies.start(rows, rs)
-    cols_in = [copies.start(cols.at[:, slice(t * f, (t + 1) * f)], cs.at[t]) for t in range(n)]
+    cols_in = [copies.start(cols.at[:, slice(t * f, (t + 1) * f)], cs.at[i]) for i, t in enumerate(parts)]
     rows_in.wait()
     outgoing = []
     for t in range(n):
@@ -487,21 +505,13 @@
 
     dense_rows = proj_weight.shape[0]
     row = lambda v: v.reshape(1, dense_rows)
-    block = (dense_rows + 2, width)
-    [shards] = copying(
+    [shards] = plain(
         shard_kernel,
-        (qkv_weight, proj_weight)
-        + tuple(row(v) for v in (attn_gain, attn_shift, moe_gain, moe_shift))
-        + (router_weight, valid_mask),
-        (0,) * 8,
-        [((n_dp,) + block, BF)],
-        (1,),
-        [(block, BF)],
-        n_dp,
-        PLAIN,
+        [((n_dp, dense_rows + 2, width), BF)],
+        *(qkv_weight, proj_weight, row(attn_gain), row(attn_shift), row(moe_gain), row(moe_shift)),
+        *(router_weight.T, valid_mask),
     )
     got = to_all(shards)
-    w = got[:, :dense_rows].reshape(width, width)
     extras = got[:, dense_rows]
     gains = extras[:, : 4 * dense_rows].reshape(n_dp, 4, dense_rows).swapaxes(0, 1).reshape(4, width).astype(F32)
     counts = jnp.sum(extras[:, 4 * dense_rows : 4 * dense_rows + 2].astype(F32), 0)
@@ -509,8 +519,8 @@
     router = got[:, dense_rows + 1].reshape(n_dp, experts, dense_rows).swapaxes(0, 1).reshape(experts, width)
 
     up0, down0 = up_weight[0], down_weight[0]
-    part = lambda eighths: width * eighths // 8
-    up2 = [swap(up0[: part(4)], 2)]
+    part = lambda sixteenths: width * sixteenths // 16
+    up2 = [swap(up0[: part(9)], 2)]
 
     mask = jnp.pad(valid_mask, ((0, 0), (0, padded - length))).reshape(n_tensor, images, 1, padded)
     masks = [lax.dynamic_index_in_dim(mask, tensor_me ^ k, 0, keepdims=False) for k in range(4)]
@@ -525,19 +535,16 @@
     place = jnp.where(ids < 0, -1, ids * slots + jnp.sum(jnp.where(named, slot[:, None, :], 0), -1))
     slot = slot.T
 
-    w, up2[0] = lax.optimization_barrier((w, up2[0]))
-    (q3, c3, l3, p3), (q2, c2, l2, p2), (q1, c1, l1, p1) = attn_fwd(
+    got, up2[0] = lax.optimization_barrier((got, up2[0]))
+    w = got if dense_rows % 16 == 0 else got[:, :dense_rows].reshape(width, width)
+    (q3, c3, l3, p3), (q2, c2, l2, p2), (q1, c1, l1, p1), *unpacked = attn_fwd(
         (x3, x2, x1), (masks[3], masks[2], masks[1]), (BF, F32, BF), w, gains, heads
     )
+    w = unpacked[0] if unpacked else w
     far = (p2 + swap(p3, 1).astype(F32)).astype(BF)
     r2 = swap(far, 2)
     [(q0, c0, l0, p0)] = attn_fwd((x0,), (masks[0],), (F32,), w, gains, heads)
     r1 = swap(p1, 1)
-    up2.append(swap(after(up0[part(4) :], r2), 2))
-    up2 = jnp.concatenate(up2)
-    ups = (up0, swap(up0, 1), up2, swap(up2, 1))
-    down2 = swap(after(down0, r2), 2)
-    downs = (down0, swap(down0, 1), down2, swap(down2, 1))
     flat = lambda v: v.reshape(own, v.shape[-1])
     row_f32 = ((own, width), F32)
     row_bf = ((own, width), BF)
@@ -547,6 +554,12 @@
         [row_f32, ((own, experts), F32), all_slots],
         *(flat(x0), flat(p0), flat(r1), flat(r2), gains, router, slot),
     )
+    up2.append(swap(after(up0[part(9) :], r2), 2))
+    down2 = [swap(after(down0[: part(12)], r2), 2)]
+    down2.append(swap(after(down0[part(12) :], down2[0]), 2))
+    beside = lambda v: [swap(piece, 1) for piece in v]
+    ups = [[up0], beside([up0]), up2, beside(up2)]
+    downs = [[down0], beside([down0]), down2, beside(down2)]
 
     exchange = lambda v: to_all(v.reshape(n_dp, slots, width)).reshape(n_dp * slots, width)
     arrived = exchange(sent)
@@ -556,14 +569,16 @@
     wide = ((total, n_tensor * f), BF)
     weights_in = [((n_tensor, width, f), BF)] * 2
     chunks = total // step
+    pieces = Pieces(ups), Pieces(downs)
+    weights = pieces[0].arrays + pieces[1].arrays
     out, hidden, slope = copying(
-        functools.partial(expert_fwd_kernel, n_tensor, step),
-        (arrived, *ups, *downs),
-        (0,) + (1,) * (2 * n_tensor),
+        functools.partial(expert_fwd_kernel, *pieces, step),
+        (arrived, *weights),
+        (0,) + (1,) * len(weights),
         [all_slots, wide, wide],
         (1, 1, 1),
         weights_in + [wide, wide, all_slots],
-        2 * n_tensor + 3 * chunks,
+        len(weights) + 3 * chunks,
         ALL,
     )
     returned = exchange(out)
@@ -575,37 +590,40 @@
     )
     grad_out = exchange(grad_sent)
     grad_up, grad_arrived = copying(
-        functools.partial(expert_bwd_kernel, n_tensor, step),
-        (grad_out, slope, *ups, *downs),
-        (0, 1) + (1,) * (2 * n_tensor),
+        functools.partial(expert_bwd_kernel, *pieces, step),
+        (grad_out, slope, *weights),
+        (0, 1) + (1,) * len(weights),
         [wide, all_slots],
         (1, 1),
         weights_in + [wide, wide, all_slots],
-        2 * n_tensor + 3 * chunks,
+        len(weights) + n_tensor + 3 * chunks,
         ALL,
     )
     grad_back = exchange(grad_arrived)
 
-    def weight_parts(rows_in, cols_in):
+    def weight_parts(rows_in, cols_in, parts):
+        n = len(parts)
         return copying(
-            functools.partial(expert_weights_kernel, n_tensor),
+            functools.partial(expert_weights_kernel, parts),
             (rows_in, cols_in),
             (1, 1),
-            [((width, f), BF)] * n_tensor,
-            (1,) * n_tensor,
-            [all_slots, ((n_tensor, total, f), BF), ((n_tensor, width, f), BF)],
-            2 * n_tensor + 1,
+            [((width, f), BF)] * n,
+            (1,) * n,
+            [all_slots, ((n, total, f), BF), ((n, width, f), BF)],
+            2 * n + 1,
             ALL,
         )
 
     widened = lambda v: v.astype(F32)
-    downs_part = weight_parts(grad_out, hidden)
+    near, far = (0, 1), (2, 3)
+    downs_far = weight_parts(grad_out, hidden, far)
+    down_far = (widened(downs_far[0]) + widened(swap(downs_far[1], 1))).astype(BF)
+    down_got = swap(down_far, 2)
+    grad_out, grad_up = lax.optimization_barrier((grad_out, grad_up, downs_far))[:2]
+    downs_part = weight_parts(grad_out, hidden, near)
+    ups_part = weight_parts(arrived, grad_up, near + far)
+    grad_back, down_got, downs_part, ups_part = lax.optimization_barrier((grad_back, down_got, downs_part, ups_part))
     down_near = swap(downs_part[1], 1)
-    down_far = (widened(downs_part[2]) + widened(swap(downs_part[3], 1))).astype(BF)
-    down_got = [swap(down_far[: part(7)], 2)]
-    ups_part = weight_parts(arrived, after(grad_up, down_far))
-    grad_back, down_got[0], ups_part = lax.optimization_barrier((grad_back, down_got[0], ups_part))
-    down_got.append(swap(down_far[part(7) :], 2))
     up_near = swap(ups_part[1], 1)
     up_far = (widened(ups_part[2]) + widened(swap(ups_part[3], 1))).astype(BF)
 
@@ -623,9 +641,8 @@
     h1, h0, dw, vec_one = attn_bwd(
         *(x1, x0, g1, g0, q1, q0, c1, c0, l1, l0, masks[1], masks[0], w, gains, (), heads, None)
     )
-    g2, dw, up_far, down_got[1] = lax.optimization_barrier((g2, dw, up_far, down_got[1]))
-    down_got = jnp.concatenate(down_got)
-    up_got = [swap(up_far[: part(5)], 2)]
+    g2, dw, up_far = lax.optimization_barrier((g2, dw, up_far))
+    up_got = [swap(up_far[: part(10)], 2)]
     g3 = swap(g2, 1)
     h3, h2, sums, _ = attn_bwd(
         *(x3, x2, g3, g2, q3, q2, c3, c2, l3, l2, masks[3], masks[2], w, gains, (dw, vec_one) + others, heads, packed)
@@ -633,27 +650,30 @@
     sums, up_got[0] = lax.optimization_barrier((sums, up_got[0]))
     t1 = swap(h1, 1)
     t2 = swap((h2 + swap(h3, 1).astype(F32)).astype(BF), 2)
-    up_got.append(swap(after(up_far[part(5) :], t2), 2))
+    up_got.append(swap(after(up_far[part(10) :], t2), 2))
     up_got = jnp.concatenate(up_got)
     grad_down_w = widened(downs_part[0]) + widened(down_near) + widened(down_got)
     grad_up_w = widened(ups_part[0]) + widened(up_near) + widened(up_got)
     [grad_tokens] = plain(
         functools.partial(last_kernel, images), [((rows, width), F32)], *(flat(x0), flat(h0), flat(t1), flat(t2), gains, grad_residual)
     )
-    gathered, grad_tokens, grad_down_w, grad_up_w = lax.optimization_barrier(
-        (to_all(sums), grad_tokens, grad_down_w, grad_up_w)
-    )
-    grad_qkv_w, grad_proj_w, small = plain(
+    gathered, grad_tokens, grad_down_w, grad_up_w, result = lax.optimization_barrier(
+        (to_all(sums), grad_tokens, grad_down_w, grad_up_w, unpad(result))
+    )
+    grad_qkv_w, grad_proj_w = plain(
         dense_kernel,
-        [(qkv_weight.shape, F32), (proj_weight.shape, F32), ((2 * experts, dense_rows), F32)],
-        gathered,
-    )
+        [(qkv_weight.shape, F32), (proj_weight.shape, F32)],
+        gathered if dense_rows % 16 == 0 else gathered[:, :dense_rows],
+    )
+    last = jnp.sum(gathered[:, dense_rows:, : 4 * dense_rows].astype(F32), 0)
+    piece = lambda i: last[:, i * dense_rows : (i + 1) * dense_rows]
+    small = jnp.concatenate([piece(0) + piece(1), piece(2) + piece(3)])
     small = small + swap(small, 1) + swap(small, 2) + swap(small, 3)
     vectors = small[experts:]
     loss = vectors[4, 0] / count
     return (
         loss,
-        unpad(result),
+        result,
         grad_tokens,
         vectors[0],
         vectors[1],

time: 411 us -> 402 us (0.978)
  local copies, waits for them, and re-layouts: 33.8 us -> 25.7 us
  waiting for transfers between devices: 141 us -> 133 us
    all_to_all x5, waiting for transfers between devices: 43.4 us -> 31.5 us  [to_all(): return lax.all_to_all(v, 'dp', split_axis=0, concat_axis=0, tiled=True)]
    unnamed x90 -> x66, local copies, waits for them, and re-layouts: 18.3 us -> 10.3 us
    ppermute x30 -> x32, waiting for transfers between devices: 97.6 us -> 102 us  [swap(): return lax.ppermute(value, 'tensor', [(i, i ^ k) for i in range(n)])]
    pallas_call x5 -> x6, Pallas kernels: 22.9 us -> 25.2 us  [plain(): pl.pallas_call(kernel, grid=(1,), in_specs=[whole(v.shape) for v in args]...]
    ppermute x30 -> x32, starting transfers between devices: 19.2 us -> 19.7 us  [swap(): return lax.ppermute(value, 'tensor', [(i, i ^ k) for i in range(n)])]
  transfers between devices with their start and end apart: 35 -> 37, of which waited for: 18 -> 16; matrix products, arithmetic and copies ran while one was open for 7% -> 7% of each run, Pallas kernels for 16% -> 18%
where the time goes in v4:
time: 402 us; the launch traced here: 394 us
  waiting for transfers between devices  133 us (33%)
  Pallas kernels  127 us (32%)
  starting transfers between devices  49.6 us (12%)
  blocking collectives  41 us (10%)
  local copies, waits for them, and re-layouts  25.7 us (6%)
  other arithmetic  12.6 us (3%)
  between operations  4.53 us (1%)
    ppermute x32, waiting for transfers between devices, swap(): return lax.ppermute(value, 'tensor', [(i, i ^ k) for i in range(n)])  102 us
    pallas_call x5, Pallas kernels, copying(): pl.pallas_call(kernel, in_specs=[spec(far) for far in in_hbm], out_specs=...  56.3 us
    all_to_all x1, blocking collectives, to_all(): return lax.all_to_all(v, 'dp', split_axis=0, concat_axis=0, tiled=True)  41 us
    all_to_all x5, waiting for transfers between devices, to_all(): return lax.all_to_all(v, 'dp', split_axis=0, concat_axis=0, tiled=True)  31.5 us
    all_to_all x5, starting transfers between devices, to_all(): return lax.all_to_all(v, 'dp', split_axis=0, concat_axis=0, tiled=True)  29.8 us
    pallas_call x2, Pallas kernels, attn_bwd(): pl.pallas_call(functools.partial(attn_bwd_kernel, heads), grid=(images,),...  29.3 us
    pallas_call x6, Pallas kernels, plain(): pl.pallas_call(kernel, grid=(1,), in_specs=[whole(v.shape) for v in args]...  25.2 us
    ppermute x32, starting transfers between devices, swap(): return lax.ppermute(value, 'tensor', [(i, i ^ k) for i in range(n)])  19.7 us
  transfers between devices with their start and end apart: 37, of which 16 were waited for; matrix products, arithmetic and copies ran while one was open for 7% of the time, Pallas kernels for 18%

profile of v4, /device:TPU:0, one launch (start us, length us, event | category | flops | bytes accessed | tf_op | source)
XLA Modules:
  0.0 394.3 jit_solution(10486666816114370741)
XLA Ops:
  0.6 1.7 copy.51.qkv
  2.4 2.3 shard_map.220
  4.7 7.4 %all-to-all-start = ((bf16[8,98,768]{2,1,0:T(8,128)(2,1)}), bf16[8,98,768]{2,1,0:T(8,128)(2,1)S(1)}, u32[]{:S(2)}, u32[]{:S(2)}) async-start(bf16[8,98,768]{2,1,0:T(8,128)(2,1)} %shard_map.220), calls=%async_computation | async-start | bytes 2555904 | tf_op jit(solution)/shard_map/all_to_all | solution.py:29
  12.1 0.9 reshape.140
  13.0 1.1 pad.15.refs_0_.xb
  14.2 1.6 collective-permute-start
  15.8 0.9 slice_bitcast_fusion.1
  17.8 13.8 %collective-permute-done.refs_1_.xb = bf16[2,208,768]{2,1,0:T(8,128)(2,1)} collective-permute-done((bf16[2,208,768]{2,1,0:T(8,128)(2,1)S(1)}, bf16[2,208,768]{2,1,0:T(8,128)(2,1)}, u32[]{:S(2)}, u32[]{:S(2)}) %collective-permute-start) | collective-permute-done | bytes 639008 | tf_op jit(solution)/shard_map/ppermute | solution.py:25
  32.2 12.2 %collective-permute-done.3.refs_2_ = bf16[432,768]{1,0:T(8,128)(2,1)} collective-permute-done((bf16[432,768]{1,0:T(8,128)(2,1)}, bf16[432,768]{1,0:T(8,128)(2,1)}, u32[]{:S(2)}, u32[]{:S(2)}) %collective-permute-start.3) | collective-permute-done | bytes 663584 | tf_op jit(solution)/shard_map/ppermute | solution.py:25
  45.5 11.0 %shard_map.221 = (bf16[2,208,576]{2,1,0:T(8,128)(2,1)}, bf16[2,208,192]{2,1,0:T(8,128)(2,1)}, f32[2,208,3]{2,1,0:T(8,128)}, bf16[2,208,768]{2,1,0:T(8,128)(2,1)}...) custom-call(bf16[2,208,768]{2,1,0:T(8,128)(2,1)} %collective-permute, ...), custom_call_target="tpu_custom_call" | custom-call | flops 1048576 | bytes 1024 | tf_op jit(solution)/shard_map/pallas_call | solution.py:114
  57.1 1.8 collective-permute-done.5
  58.9 1.5 add_convert_fusion.3
  60.3 1.6 collective-permute-start.6
  64.5 5.3 %shard_map.222 = (bf16[2,208,576]{2,1,0:T(8,128)(2,1)}, bf16[2,208,192]{2,1,0:T(8,128)(2,1)}, f32[2,208,3]{2,1,0:T(8,128)}, f32[2,208,768]{2,1,0:T(8,128)}) custom-call(bf16[2,208,768]{2,1,0:T(8,128)(2,1)} %copy-done, s32[2,1,208]{2,1,0:T(1,128)} %squeeze.39.refs_1_.kb, bf16[768,768]{1,0:T(8,128)(2,1)} %get-tuple-element.90.refs_2_.w_ref, ...), custom_call_target="tpu_custom_call" | custom-call | flops 1048576 | bytes 1024 | tf_op jit(solution)/shard_map/pallas_call | solution.py:114
  69.8 7.1 %collective-permute-done.6 = bf16[2,208,768]{2,1,0:T(8,128)(2,1)S(1)} collective-permute-done((bf16[2,208,768]{2,1,0:T(8,128)(2,1)S(1)}, bf16[2,208,768]{2,1,0:T(8,128)(2,1)S(1)}, u32[]{:S(2)}, u32[]{:S(2)}) %collective-permute-start.6) | collective-permute-done | bytes 639008 | tf_op jit(solution)/shard_map/ppermute | solution.py:25
  77.7 4.6 %shard_map.223 = (f32[416,768]{1,0:T(8,128)}, f32[416,8]{1,0:T(8,128)}, bf16[1024,768]{1,0:T(8,128)(2,1)}) custom-call(bf16[416,768]{1,0:T(8,128)(2,1)} %bitcast.75, f32[416,768]{1,0:T(8,128)} %bitcast.97, bf16[416,768]{1,0:T(8,128)(2,1)} %bitcast.98, bf16[416,768]{1,0:T(8,128)(2,1)} %bitcast.99, f32[4,768]{1,0:T(4,128)} %reshape.168.refs_7_.refs_3_.gains, ...), custom_call_target="tpu_custom_call" | custom-call | flops 1048576 | bytes 1024 | tf_op jit(solution)/shard_map/pallas_call | solution.py:283
  82.3 6.3 %all-to-all-start.1 = ((bf16[8,128,768]{2,1,0:T(8,128)(2,1)}), bf16[8,128,768]{2,1,0:T(8,128)(2,1)S(1)}, u32[]{:S(2)}, u32[]{:S(2)}) async-start(bf16[8,128,768]{2,1,0:T(8,128)(2,1)} %bitcast.92), calls=%async_computation.1 | async-start | bytes 3145728 | tf_op jit(solution)/shard_map/all_to_all | solution.py:29
  88.6 1.3 slice_bitcast_fusion
  90.0 1.6 collective-permute-start.12
  92.3 20.2 %collective-permute-done.12.refs_8_ = bf16[576,768]{1,0:T(8,128)(2,1)S(1)} collective-permute-done((bf16[576,768]{1,0:T(8,128)(2,1)S(1)}, bf16[576,768]{1,0:T(8,128)(2,1)S(1)}, u32[]{:S(2)}, u32[]{:S(2)}) %collective-permute-start.12) | collective-permute-done | bytes 884768 | tf_op jit(solution)/shard_map/ppermute | solution.py:25
  113.0 1.6 collective-permute-start.13
  114.6 8.9 %collective-permute-done.8.refs_3_ = bf16[336,768]{1,0:T(8,128)(2,1)S(1)} collective-permute-done((bf16[336,768]{1,0:T(8,128)(2,1)S(1)}, bf16[336,768]{1,0:T(8,128)(2,1)S(1)}, u32[]{:S(2)}, u32[]{:S(2)}) %collective-permute-start.8) | collective-permute-done | bytes 516128 | tf_op jit(solution)/shard_map/ppermute | solution.py:25
  123.5 5.8 %collective-permute-done.13.refs_9_ = bf16[192,768]{1,0:T(8,128)(2,1)S(1)} collective-permute-done((bf16[192,768]{1,0:T(8,128)(2,1)S(1)}, bf16[192,768]{1,0:T(8,128)(2,1)S(1)}, u32[]{:S(2)}, u32[]{:S(2)}) %collective-permute-start.13) | collective-permute-done | bytes 294944 | tf_op jit(solution)/shard_map/ppermute | solution.py:25
  129.4 1.5 collective-permute-done.15.refs_11_
  131.7 1.1 copy-done.1
  132.8 16.0 %shard_map.224 = (bf16[1024,768]{1,0:T(8,128)(2,1)}, bf16[1024,3072]{1,0:T(8,128)(2,1)}, bf16[1024,3072]{1,0:T(8,128)(2,1)}) custom-call(bf16[1024,768]{1,0:T(8,128)(2,1)} %bitcast.77, bf16[768,768]{1,0:T(8,128)(2,1)} %bitcast.79, bf16[768,768]{1,0:T(8,128)(2,1)} %copy-done.8, bf16[432,768]{1,0:T(8,128)(2,1)} %collective-permute-done.3.refs_2_, ...), custom_call_target="tpu_custom_call" | custom-call | flops 1048576 | bytes 1024 | tf_op jit(solution)/shard_map/pallas_call | solution.py:448
  148.9 6.2 %all-to-all-start.2 = ((bf16[8,128,768]{2,1,0:T(8,128)(2,1)}), bf16[8,128,768]{2,1,0:T(8,128)(2,1)S(1)}, u32[]{:S(2)}, u32[]{:S(2)}) async-start(bf16[8,128,768]{2,1,0:T(8,128)(2,1)} %bitcast.94), calls=%async_computation.2 | async-start | bytes 3145728 | tf_op jit(solution)/shard_map/all_to_all | solution.py:29
  155.3 0.9 convert_element_type.106.mask
  156.2 1.2 reshape.156
  157.4 0.9 pad.18
  160.9 31.5 %all-to-all-done.2 = bf16[8,128,768]{2,1,0:T(8,128)(2,1)S(1)} async-done(((bf16[8,128,768]{2,1,0:T(8,128)(2,1)}), bf16[8,128,768]{2,1,0:T(8,128)(2,1)S(1)}, u32[]{:S(2)}, u32[]{:S(2)}) %all-to-all-start.2) | async-done | bytes 1572896 | tf_op jit(solution)/shard_map/all_to_all | solution.py:29
  193.5 6.5 %shard_map.225 = (bf16[416,768]{1,0:T(8,128)(2,1)}, f32[416,768]{1,0:T(8,128)}, bf16[416,8]{1,0:T(8,128)(2,1)}, f32[1,768]{1,0:T(1,128)}, bf16[1024,768]{1,0:T(8,128)(2,1)}) custom-call(bf16[1024,768]{1,0:T(8,128)(2,1)} %bitcast.86, s32[416,2]{1,0:T(8,128)} %add_select_fusion.place, s32[416,2]{1,0:T(8,128)} %bitcast.88, ...), custom_call_target="tpu_custom_call" | custom-call | flops 1048576 | bytes 1024 | tf_op jit(solution)/shard_map/pallas_call | solution.py:283
  200.0 41.0 %all_to_all.30 = bf16[8,128,768]{2,1,0:T(8,128)(2,1)} all-to-all(bf16[8,128,768]{2,1,0:T(8,128)(2,1)} %bitcast.95), channel_id=1, replica_groups=mesh['dp'=8,'tensor'=4] {'dp'}, dimensions={0} | all-to-all | bytes 3145728 | tf_op jit(solution)/shard_map/all_to_all | solution.py:29
  241.0 16.7 %shard_map.226 = (bf16[1024,3072]{1,0:T(8,128)(2,1)}, bf16[1024,768]{1,0:T(8,128)(2,1)}) custom-call(bf16[1024,768]{1,0:T(8,128)(2,1)} %bitcast.72, bf16[1024,3072]{1,0:T(8,128)(2,1)} %get-tuple-element.104.slope, bf16[768,768]{1,0:T(8,128)(2,1)} %bitcast.80, bf16[768,768]{1,0:T(8,128)(2,1)} %copy-done.8, bf16[432,768]{1,0:T(8,128)(2,1)} %collective-permute-done.3.refs_2_, ...), custom_call_target="tpu_custom_call" | custom-call | flops 1048576 | bytes 1024 | tf_op jit(solution)/shard_map/pallas_call | solution.py:448
  257.7 3.8 all-to-all-start.4
  261.6 6.7 %shard_map.227 = (bf16[768,768]{1,0:T(8,128)(2,1)}, bf16[768,768]{1,0:T(8,128)(2,1)}) custom-call(bf16[1024,768]{1,0:T(8,128)(2,1)} %bitcast.73, bf16[1024,3072]{1,0:T(8,128)(2,1)} %get-tuple-element.106.cols), custom_call_target="tpu_custom_call" | custom-call | flops 1048576 | bytes 1024 | tf_op jit(solution)/shard_map/pallas_call | solution.py:448
  268.3 3.0 collective-permute-done.16
  271.3 1.6 add_convert_fusion.1
  272.9 1.6 collective-permute-start.17
  274.5 6.6 %shard_map.228 = (bf16[768,768]{1,0:T(8,128)(2,1)}, bf16[768,768]{1,0:T(8,128)(2,1)}) custom-call(bf16[1024,768]{1,0:T(8,128)(2,1)} %bitcast.74, bf16[1024,3072]{1,0:T(8,128)(2,1)} %get-tuple-element.106.cols), custom_call_target="tpu_custom_call" | custom-call | flops 1048576 | bytes 1024 | tf_op jit(solution)/shard_map/pallas_call | solution.py:448
  281.1 10.3 %shard_map.229 = (bf16[768,768]{1,0:T(8,128)(2,1)}, bf16[768,768]{1,0:T(8,128)(2,1)}, bf16[768,768]{1,0:T(8,128)(2,1)}, bf16[768,768]{1,0:T(8,128)(2,1)}) custom-call(bf16[1024,768]{1,0:T(8,128)(2,1)} %bitcast.78, bf16[1024,3072]{1,0:T(8,128)(2,1)} %get-tuple-element.113.cols), custom_call_target="tpu_custom_call" | custom-call | flops 1048576 | bytes 1024 | tf_op jit(solution)/shard_map/pallas_call | solution.py:448
  291.4 9.7 %collective-permute-done.17 = bf16[768,768]{1,0:T(8,128)(2,1)} collective-permute-done((bf16[768,768]{1,0:T(8,128)(2,1)S(1)}, bf16[768,768]{1,0:T(8,128)(2,1)}, u32[]{:S(2)}, u32[]{:S(2)}) %collective-permute-start.17) | collective-permute-done | bytes 1179680 | tf_op jit(solution)/shard_map/ppermute | solution.py:25
  301.1 1.1 copy-done.4
  302.2 5.1 %shard_map.230 = (f32[416,768]{1,0:T(8,128)}, bf16[416,768]{1,0:T(8,128)(2,1)}, f32[2,768]{1,0:T(2,128)}, f32[8,768]{1,0:T(8,128)}) custom-call(bf16[1024,768]{1,0:T(8,128)(2,1)} %bitcast.85, s32[416,2]{1,0:T(8,128)} %add_select_fusion.place, f32[416,768]{1,0:T(8,128)} %get-tuple-element.102.residual, f32[416,768]{1,0:T(8,128)} %get-tuple-element.119.g, ...), custom_call_target="tpu_custom_call" | custom-call | flops 1048576 | bytes 1024 | tf_op jit(solution)/shard_map/pallas_call | solution.py:283
  307.3 1.5 collective-permute-start.18
  309.6 0.8 copy-done.25
  310.5 14.7 %shard_map.231 = (bf16[2,208,768]{2,1,0:T(8,128)(2,1)}, f32[2,208,768]{2,1,0:T(8,128)}, f32[768,768]{1,0:T(8,128)}, f32[2,768]{1,0:T(2,128)}) custom-call(bf16[2,208,768]{2,1,0:T(8,128)(2,1)} %collective-permute-done.2.refs_2_.xa, bf16[2,208,768]{2,1,0:T(8,128)(2,1)} %copy-done, bf16[2,208,768]{2,1,0:T(8,128)(2,1)} %copy-done.25, ...), custom_call_target="tpu_custom_call" | custom-call | flops 268435456 | bytes 8388608 | tf_op jit(solution)/shard_map/pallas_call | solution.py:198
  325.7 1.6 collective-permute-start.22
  327.6 0.8 copy-done.21
  328.4 14.6 %shard_map.232 = (bf16[2,208,768]{2,1,0:T(8,128)(2,1)}, f32[2,208,768]{2,1,0:T(8,128)}, bf16[8,104,768]{2,1,0:T(8,128)(2,1)}, f32[2,768]{1,0:T(2,128)}) custom-call(bf16[2,208,768]{2,1,0:T(8,128)(2,1)} %collective-permute-done.1.refs_0_.xa, bf16[2,208,768]{2,1,0:T(8,128)(2,1)} %collective-permute-done.refs_1_.xb, bf16[2,208,768]{2,1,0:T(8,128)(2,1)} %copy-done.21, ...), custom_call_target="tpu_custom_call" | custom-call | flops 268435456 | bytes 8388608 | tf_op jit(solution)/shard_map/pallas_call | solution.py:198
  343.3 1.4 collective-permute-done.22
  344.6 6.2 %all-to-all-start.5 = ((bf16[8,104,768]{2,1,0:T(8,128)(2,1)}), bf16[8,104,768]{2,1,0:T(8,128)(2,1)S(1)}, u32[]{:S(2)}, u32[]{:S(2)}) async-start(bf16[8,104,768]{2,1,0:T(8,128)(2,1)} %get-tuple-element.145), calls=%async_computation.5 | async-start | bytes 2555904 | tf_op jit(solution)/shard_map/all_to_all | solution.py:29
  351.4 1.5 add_convert_fusion.2
  352.9 1.6 collective-permute-start.25
  355.3 14.0 %collective-permute-done.25 = bf16[2,208,768]{2,1,0:T(8,128)(2,1)S(1)} collective-permute-done((bf16[2,208,768]{2,1,0:T(8,128)(2,1)S(1)}, bf16[2,208,768]{2,1,0:T(8,128)(2,1)S(1)}, u32[]{:S(2)}, u32[]{:S(2)}) %collective-permute-start.25) | collective-permute-done | bytes 639008 | tf_op jit(solution)/shard_map/ppermute | solution.py:25
  369.3 1.5 collective-permute-start.28
  370.9 0.9 reshape.167
  371.9 3.6 convert_add_fusion.1
  375.4 4.3 %shard_map.233 = f32[394,768]{1,0:T(8,128)} custom-call(bf16[416,768]{1,0:T(8,128)(2,1)} %bitcast.76, f32[416,768]{1,0:T(8,128)} %bitcast.96, bf16[416,768]{1,0:T(8,128)(2,1)} %bitcast.35.r1, bf16[416,768]{1,0:T(8,128)(2,1)} %bitcast.100, f32[4,768]{1,0:T(4,128)} %reshape.168.refs_7_.refs_3_.gains, f32[416,768]{1,0:T(8,128)} %get-tuple-element.150.grad_residual), custom_call_target="tpu_custom_call" | custom-call | flops 1048576 | bytes 1024 | tf_op jit(solution)/shard_map/pallas_call | solution.py:283
  379.8 1.1 collective-permute-done.28
  380.9 3.3 convert_add_fusion
  384.3 1.5 collective-permute-start.30
  386.4 2.3 shard_map.234
  388.8 1.8 copy.58
  (144 shorter events, 17.2 us)
Async XLA Ops:
  4.7 7.4 %copy-start.26 = (bf16[394,768]{1,0:T(8,128)(2,1)S(1)}, bf16[394,768]{1,0:T(8,128)(2,1)}, u32[]{:S(2)}) copy-start(bf16[394,768]{1,0:T(8,128)(2,1)} %param.13) | copy-start | bytes 1815556
  4.7 39.7 %all-to-all-start = ((bf16[8,98,768]{2,1,0:T(8,128)(2,1)}), bf16[8,98,768]{2,1,0:T(8,128)(2,1)S(1)}, u32[]{:S(2)}, u32[]{:S(2)}) async-start(bf16[8,98,768]{2,1,0:T(8,128)(2,1)} %shard_map.220), calls=%async_computation | async-start | bytes 2555904 | tf_op jit(solution)/shard_map/all_to_all | solution.py:29
  12.1 3.7 copy-start.2
  13.0 4.1 %copy-start.29 = (s32[8,197]{1,0:T(8,128)S(1)}, s32[8,197]{1,0:T(8,128)}, u32[]{:S(2)}) copy-start(s32[8,197]{1,0:T(8,128)} %mask.1) | copy-start | bytes 18916
  14.2 42.3 %copy-start = (bf16[2,208,768]{2,1,0:T(8,128)(2,1)}, bf16[2,208,768]{2,1,0:T(8,128)(2,1)S(1)}, u32[]{:S(2)}) copy-start(bf16[2,208,768]{2,1,0:T(8,128)(2,1)S(1)} %pad.15.refs_0_.xb) | copy-start | bytes 1916932
  14.2 17.5 %collective-permute-start = (bf16[2,208,768]{2,1,0:T(8,128)(2,1)S(1)}, bf16[2,208,768]{2,1,0:T(8,128)(2,1)}, u32[]{:S(2)}, u32[]{:S(2)}) collective-permute-start(bf16[2,208,768]{2,1,0:T(8,128)(2,1)S(1)} %pad.15.refs_0_.xb), channel_id=1, source_target_pairs={{0,2},{1,3},{2,0},{3,1},{4,6},{5,7},{6,4},{7,5},{8,10},{9,11},{10,... | collective-permute-start | bytes 1916936 | tf_op jit(solution)/shard_map/ppermute | solution.py:25
  16.7 27.8 %collective-permute-start.3 = (bf16[432,768]{1,0:T(8,128)(2,1)}, bf16[432,768]{1,0:T(8,128)(2,1)}, u32[]{:S(2)}, u32[]{:S(2)}) collective-permute-start(bf16[432,768]{1,0:T(8,128)(2,1)} %slice_bitcast_fusion.1), channel_id=1, source_target_pairs={{0,2},{1,3},{2,0},{3,1},{4,6},{5,7},{6,4},{7,5},{8,10},{9,11},{10,... | collective-permute-start | bytes 1990664 | tf_op jit(solution)/shard_map/ppermute | solution.py:25
  17.2 28.3 %collective-permute-start.2 = (bf16[2,208,768]{2,1,0:T(8,128)(2,1)S(1)}, bf16[2,208,768]{2,1,0:T(8,128)(2,1)}, u32[]{:S(2)}, u32[]{:S(2)}) collective-permute-start(bf16[2,208,768]{2,1,0:T(8,128)(2,1)S(1)} %pad.15.refs_0_.xb), channel_id=1, source_target_pairs={{0,1},{1,0},{2,3},{3,2},{4,5},{5,4},{6,7},{7,6},{8,9},{9,8},{10,11... | collective-permute-start | bytes 1916936 | tf_op jit(solution)/shard_map/ppermute | solution.py:25
  31.7 13.8 %collective-permute-start.1 = (bf16[2,208,768]{2,1,0:T(8,128)(2,1)}, bf16[2,208,768]{2,1,0:T(8,128)(2,1)}, u32[]{:S(2)}, u32[]{:S(2)}) collective-permute-start(bf16[2,208,768]{2,1,0:T(8,128)(2,1)} %collective-permute-done.refs_1_.xb), channel_id=1, source_target_pairs={{0,1},{1,0},{2,3},{3,2},{4,5},{5,4},{6,7},{7,6},{8,9},{9,8},{10,11... | collective-permute-start | bytes 1916936 | tf_op jit(solution)/shard_map/ppermute | solution.py:25
  44.4 1.0 copy-start.6
  56.5 2.4 collective-permute-start.5
  56.6 13.2 %collective-permute-start.4 = (bf16[2,208,768]{2,1,0:T(8,128)(2,1)}, bf16[2,208,768]{2,1,0:T(8,128)(2,1)S(1)}, u32[]{:S(2)}, u32[]{:S(2)}) collective-permute-start(bf16[2,208,768]{2,1,0:T(8,128)(2,1)} %get-tuple-element.92), channel_id=1, source_target_pairs={{0,1},{1,0},{2,3},{3,2},{4,5},{5,4},{6,7},{7,6},{8,9},{9,8},{10,11... | collective-permute-start | bytes 1916936 | tf_op jit(solution)/shard_map/ppermute | solution.py:25
  58.9 3.0 copy-start.30
  60.3 16.5 %collective-permute-start.6 = (bf16[2,208,768]{2,1,0:T(8,128)(2,1)S(1)}, bf16[2,208,768]{2,1,0:T(8,128)(2,1)S(1)}, u32[]{:S(2)}, u32[]{:S(2)}) collective-permute-start(bf16[2,208,768]{2,1,0:T(8,128)(2,1)S(1)} %add_convert_fusion.3), channel_id=1, source_target_pairs={{0,2},{1,3},{2,0},{3,1},{4,6},{5,7},{6,4},{7,5},{8,10},{9,11},{10,... | collective-permute-start | bytes 1916936 | tf_op jit(solution)/shard_map/ppermute | solution.py:25
  62.7 95.5 %copy-start.11 = (s32[2,208,2]{2,1,0:T(8,128)}, s32[2,208,2]{2,1,0:T(8,128)S(1)}, u32[]{:S(2)}) copy-start(s32[2,208,2]{2,1,0:T(8,128)S(1)} %pad.17) | copy-start | bytes 9988
  69.7 7.1 %copy-start.22 = (bf16[2,208,768]{2,1,0:T(8,128)(2,1)}, bf16[2,208,768]{2,1,0:T(8,128)(2,1)S(1)}, u32[]{:S(2)}) copy-start(bf16[2,208,768]{2,1,0:T(8,128)(2,1)S(1)} %collective-permute-done.4) | copy-start | bytes 1916932
  82.3 49.4 %all-to-all-start.1 = ((bf16[8,128,768]{2,1,0:T(8,128)(2,1)}), bf16[8,128,768]{2,1,0:T(8,128)(2,1)S(1)}, u32[]{:S(2)}, u32[]{:S(2)}) async-start(bf16[8,128,768]{2,1,0:T(8,128)(2,1)} %bitcast.92), calls=%async_computation.1 | async-start | bytes 3145728 | tf_op jit(solution)/shard_map/all_to_all | solution.py:29
  88.5 3.0 copy-start.3
  88.6 24.4 %collective-permute-start.7 = (bf16[768,768]{1,0:T(8,128)(2,1)S(1)}, bf16[768,768]{1,0:T(8,128)(2,1)S(1)}, u32[]{:S(2)}, u32[]{:S(2)}) collective-permute-start(bf16[768,768]{1,0:T(8,128)(2,1)S(1)} %bitcast.81), channel_id=1, source_target_pairs={{0,1},{1,0},{2,3},{3,2},{4,5},{5,4},{6,7},{7,6},{8,9},{9,8},{10,11... | collective-permute-start | bytes 3538952 | tf_op jit(solution)/shard_map/ppermute | solution.py:25
  90.0 22.5 %collective-permute-start.12 = (bf16[576,768]{1,0:T(8,128)(2,1)S(1)}, bf16[576,768]{1,0:T(8,128)(2,1)S(1)}, u32[]{:S(2)}, u32[]{:S(2)}) collective-permute-start(bf16[576,768]{1,0:T(8,128)(2,1)S(1)} %slice_bitcast_fusion), channel_id=1, source_target_pairs={{0,2},{1,3},{2,0},{3,1},{4,6},{5,7},{6,4},{7,5},{8,10},{9,11},{10,... | collective-permute-start | bytes 2654216 | tf_op jit(solution)/shard_map/ppermute | solution.py:25
  91.5 37.8 %collective-permute-start.11 = (bf16[768,768]{1,0:T(8,128)(2,1)S(1)}, bf16[768,768]{1,0:T(8,128)(2,1)S(1)}, u32[]{:S(2)}, u32[]{:S(2)}) collective-permute-start(bf16[768,768]{1,0:T(8,128)(2,1)S(1)} %bitcast.84), channel_id=1, source_target_pairs={{0,1},{1,0},{2,3},{3,2},{4,5},{5,4},{6,7},{7,6},{8,9},{9,8},{10,11... | collective-permute-start | bytes 3538952 | tf_op jit(solution)/shard_map/ppermute | solution.py:25
  91.7 31.8 %collective-permute-start.8 = (bf16[336,768]{1,0:T(8,128)(2,1)S(1)}, bf16[336,768]{1,0:T(8,128)(2,1)S(1)}, u32[]{:S(2)}, u32[]{:S(2)}) collective-permute-start(bf16[336,768]{1,0:T(8,128)(2,1)S(1)} %slice_bitcast_fusion.2), channel_id=1, source_target_pairs={{0,2},{1,3},{2,0},{3,1},{4,6},{5,7},{6,4},{7,5},{8,10},{9,11},{10,... | collective-permute-start | bytes 1548296 | tf_op jit(solution)/shard_map/ppermute | solution.py:25
  112.5 18.5 %copy-start.10 = (bf16[576,768]{1,0:T(8,128)(2,1)}, bf16[576,768]{1,0:T(8,128)(2,1)S(1)}, u32[]{:S(2)}) copy-start(bf16[576,768]{1,0:T(8,128)(2,1)S(1)} %collective-permute-done.12.refs_8_) | copy-start | bytes 2654212
  112.5 19.2 %collective-permute-start.14 = (bf16[576,768]{1,0:T(8,128)(2,1)S(1)}, bf16[576,768]{1,0:T(8,128)(2,1)}, u32[]{:S(2)}, u32[]{:S(2)}) collective-permute-start(bf16[576,768]{1,0:T(8,128)(2,1)S(1)} %collective-permute-done.12.refs_8_), channel_id=1, source_target_pairs={{0,1},{1,0},{2,3},{3,2},{4,5},{5,4},{6,7},{7,6},{8,9},{9,8},{10,11... | collective-permute-start | bytes 2654216 | tf_op jit(solution)/shard_map/ppermute | solution.py:25
  112.5 16.9 %collective-permute-start.9 = (bf16[432,768]{1,0:T(8,128)(2,1)}, bf16[432,768]{1,0:T(8,128)(2,1)S(1)}, u32[]{:S(2)}, u32[]{:S(2)}) collective-permute-start(bf16[432,768]{1,0:T(8,128)(2,1)} %collective-permute-done.3.refs_2_), channel_id=1, source_target_pairs={{0,1},{1,0},{2,3},{3,2},{4,5},{5,4},{6,7},{7,6},{8,9},{9,8},{10,11... | collective-permute-start | bytes 1990664 | tf_op jit(solution)/shard_map/ppermute | solution.py:25
  113.0 18.0 %copy-start.8 = (bf16[768,768]{1,0:T(8,128)(2,1)}, bf16[768,768]{1,0:T(8,128)(2,1)S(1)}, u32[]{:S(2)}) copy-start(bf16[768,768]{1,0:T(8,128)(2,1)S(1)} %collective-permute-done.7.refs_1_) | copy-start | bytes 3538948
  113.0 16.4 %collective-permute-start.13 = (bf16[192,768]{1,0:T(8,128)(2,1)S(1)}, bf16[192,768]{1,0:T(8,128)(2,1)S(1)}, u32[]{:S(2)}, u32[]{:S(2)}) collective-permute-start(bf16[192,768]{1,0:T(8,128)(2,1)S(1)} %slice_bitcast_fusion.3), channel_id=1, source_target_pairs={{0,2},{1,3},{2,0},{3,1},{4,6},{5,7},{6,4},{7,5},{8,10},{9,11},{10,... | collective-permute-start | bytes 884744 | tf_op jit(solution)/shard_map/ppermute | solution.py:25
  123.5 8.2 %copy-start.13 = (bf16[336,768]{1,0:T(8,128)(2,1)}, bf16[336,768]{1,0:T(8,128)(2,1)S(1)}, u32[]{:S(2)}) copy-start(bf16[336,768]{1,0:T(8,128)(2,1)S(1)} %collective-permute-done.8.refs_3_) | copy-start | bytes 1548292
  123.5 5.9 %collective-permute-start.10 = (bf16[336,768]{1,0:T(8,128)(2,1)S(1)}, bf16[336,768]{1,0:T(8,128)(2,1)S(1)}, u32[]{:S(2)}, u32[]{:S(2)}) collective-permute-start(bf16[336,768]{1,0:T(8,128)(2,1)S(1)} %collective-permute-done.8.refs_3_), channel_id=1, source_target_pairs={{0,1},{1,0},{2,3},{3,2},{4,5},{5,4},{6,7},{7,6},{8,9},{9,8},{10,11... | collective-permute-start | bytes 1548296 | tf_op jit(solution)/shard_map/ppermute | solution.py:25
  129.4 2.3 copy-start.18
  129.4 1.6 collective-permute-start.15
  129.4 1.6 copy-start.9
  129.4 1.6 copy-start.12
  129.4 2.3 copy-start.14
  131.7 1.1 copy-start.1
  148.8 6.2 %copy-start.28 = (s32[416,8]{0,1:T(8,128)S(1)}, s32[416,8]{0,1:T(8,128)}, u32[]{:S(2)}) copy-start(s32[416,8]{0,1:T(8,128)} %fusion) | copy-start | bytes 39940
  148.9 43.5 %all-to-all-start.2 = ((bf16[8,128,768]{2,1,0:T(8,128)(2,1)}), bf16[8,128,768]{2,1,0:T(8,128)(2,1)S(1)}, u32[]{:S(2)}, u32[]{:S(2)}) async-start(bf16[8,128,768]{2,1,0:T(8,128)(2,1)} %bitcast.94), calls=%async_computation.2 | async-start | bytes 3145728 | tf_op jit(solution)/shard_map/all_to_all | solution.py:29
  192.4 1.1 copy-start.5
  257.7 43.3 %all-to-all-start.4 = ((bf16[8,128,768]{2,1,0:T(8,128)(2,1)}), bf16[8,128,768]{2,1,0:T(8,128)(2,1)S(1)}, u32[]{:S(2)}, u32[]{:S(2)}) async-start(bf16[8,128,768]{2,1,0:T(8,128)(2,1)} %bitcast.93), calls=%async_computation.4 | async-start | bytes 3145728 | tf_op jit(solution)/shard_map/all_to_all | solution.py:29
  268.2 3.1 collective-permute-start.16
  272.9 28.2 %collective-permute-start.17 = (bf16[768,768]{1,0:T(8,128)(2,1)S(1)}, bf16[768,768]{1,0:T(8,128)(2,1)}, u32[]{:S(2)}, u32[]{:S(2)}) collective-permute-start(bf16[768,768]{1,0:T(8,128)(2,1)S(1)} %add_convert_fusion.1), channel_id=1, source_target_pairs={{0,2},{1,3},{2,0},{3,1},{4,6},{5,7},{6,4},{7,5},{8,10},{9,11},{10,... | collective-permute-start | bytes 3538952 | tf_op jit(solution)/shard_map/ppermute | solution.py:25
  301.1 1.1 copy-start.4
  301.1 24.0 %collective-permute-start.20 = (bf16[768,768]{1,0:T(8,128)(2,1)}, bf16[768,768]{1,0:T(8,128)(2,1)S(1)}, u32[]{:S(2)}, u32[]{:S(2)}) collective-permute-start(bf16[768,768]{1,0:T(8,128)(2,1)} %get-tuple-element.130), channel_id=1, source_target_pairs={{0,1},{1,0},{2,3},{3,2},{4,5},{5,4},{6,7},{7,6},{8,9},{9,8},{10,11... | collective-permute-start | bytes 3538952 | tf_op jit(solution)/shard_map/ppermute | solution.py:25
  307.3 2.3 collective-permute-start.19
  307.3 18.1 %collective-permute-start.18 = (bf16[2,208,768]{2,1,0:T(8,128)(2,1)}, bf16[2,208,768]{2,1,0:T(8,128)(2,1)S(1)}, u32[]{:S(2)}, u32[]{:S(2)}) collective-permute-start(bf16[2,208,768]{2,1,0:T(8,128)(2,1)} %bitcast.102), channel_id=1, source_target_pairs={{0,2},{1,3},{2,0},{3,1},{4,6},{5,7},{6,4},{7,5},{8,10},{9,11},{10,... | collective-permute-start | bytes 1916936 | tf_op jit(solution)/shard_map/ppermute | solution.py:25
  310.5 14.7 %copy-start.15 = (bf16[768,768]{1,0:T(8,128)(2,1)S(1)}, bf16[768,768]{1,0:T(8,128)(2,1)}, u32[]{:S(2)}) copy-start(bf16[768,768]{1,0:T(8,128)(2,1)} %get-tuple-element.129) | copy-start | bytes 3538948
  325.4 2.2 copy-start.20
  325.5 2.1 collective-permute-start.21
  325.7 18.9 %collective-permute-start.22 = (bf16[480,768]{1,0:T(8,128)(2,1)S(1)}, bf16[480,768]{1,0:T(8,128)(2,1)}, u32[]{:S(2)}, u32[]{:S(2)}) collective-permute-start(bf16[480,768]{1,0:T(8,128)(2,1)S(1)} %slice.104), channel_id=1, source_target_pairs={{0,2},{1,3},{2,0},{3,1},{4,6},{5,7},{6,4},{7,5},{8,10},{9,11},{10,... | collective-permute-start | bytes 2211848 | tf_op jit(solution)/shard_map/ppermute | solution.py:25
  343.1 8.3 %collective-permute-start.24 = (bf16[2,208,768]{2,1,0:T(8,128)(2,1)}, bf16[2,208,768]{2,1,0:T(8,128)(2,1)S(1)}, u32[]{:S(2)}, u32[]{:S(2)}) collective-permute-start(bf16[2,208,768]{2,1,0:T(8,128)(2,1)} %get-tuple-element.149), channel_id=1, source_target_pairs={{0,1},{1,0},{2,3},{3,2},{4,5},{5,4},{6,7},{7,6},{8,9},{9,8},{10,11... | collective-permute-start | bytes 1916936 | tf_op jit(solution)/shard_map/ppermute | solution.py:25
  344.6 39.5 %all-to-all-start.5 = ((bf16[8,104,768]{2,1,0:T(8,128)(2,1)}), bf16[8,104,768]{2,1,0:T(8,128)(2,1)S(1)}, u32[]{:S(2)}, u32[]{:S(2)}) async-start(bf16[8,104,768]{2,1,0:T(8,128)(2,1)} %get-tuple-element.145), calls=%async_computation.5 | async-start | bytes 2555904 | tf_op jit(solution)/shard_map/all_to_all | solution.py:29
  350.8 21.0 %collective-permute-start.26 = (bf16[768,768]{1,0:T(8,128)(2,1)}, bf16[768,768]{1,0:T(8,128)(2,1)}, u32[]{:S(2)}, u32[]{:S(2)}) collective-permute-start(bf16[768,768]{1,0:T(8,128)(2,1)} %get-tuple-element.152), channel_id=1, source_target_pairs={{0,1},{1,0},{2,3},{3,2},{4,5},{5,4},{6,7},{7,6},{8,9},{9,8},{10,11... | collective-permute-start | bytes 3538952 | tf_op jit(solution)/shard_map/ppermute | solution.py:25
  350.9 28.9 %collective-permute-start.27 = (bf16[768,768]{1,0:T(8,128)(2,1)}, bf16[768,768]{1,0:T(8,128)(2,1)}, u32[]{:S(2)}, u32[]{:S(2)}) collective-permute-start(bf16[768,768]{1,0:T(8,128)(2,1)} %get-tuple-element.155), channel_id=1, source_target_pairs={{0,1},{1,0},{2,3},{3,2},{4,5},{5,4},{6,7},{7,6},{8,9},{9,8},{10,11... | collective-permute-start | bytes 3538952 | tf_op jit(solution)/shard_map/ppermute | solution.py:25
  351.4 19.5 %copy-start.27 = (bf16[416,768]{1,0:T(8,128)(2,1)S(1)}, bf16[416,768]{1,0:T(8,128)(2,1)}, u32[]{:S(2)}) copy-start(bf16[416,768]{1,0:T(8,128)(2,1)} %get-tuple-element.158) | copy-start | bytes 1916932
  352.9 16.4 %collective-permute-start.25 = (bf16[2,208,768]{2,1,0:T(8,128)(2,1)S(1)}, bf16[2,208,768]{2,1,0:T(8,128)(2,1)S(1)}, u32[]{:S(2)}, u32[]{:S(2)}) collective-permute-start(bf16[2,208,768]{2,1,0:T(8,128)(2,1)S(1)} %add_convert_fusion.2), channel_id=1, source_target_pairs={{0,2},{1,3},{2,0},{3,1},{4,6},{5,7},{6,4},{7,5},{8,10},{9,11},{10,... | collective-permute-start | bytes 1916936 | tf_op jit(solution)/shard_map/ppermute | solution.py:25
  354.5 20.9 %collective-permute-start.23 = (bf16[2,208,768]{2,1,0:T(8,128)(2,1)}, bf16[2,208,768]{2,1,0:T(8,128)(2,1)}, u32[]{:S(2)}, u32[]{:S(2)}) collective-permute-start(bf16[2,208,768]{2,1,0:T(8,128)(2,1)} %get-tuple-element.147), channel_id=1, source_target_pairs={{0,1},{1,0},{2,3},{3,2},{4,5},{5,4},{6,7},{7,6},{8,9},{9,8},{10,11... | collective-permute-start | bytes 1916936 | tf_op jit(solution)/shard_map/ppermute | solution.py:25
  355.3 16.6 %copy-start.17 = (bf16[768,768]{1,0:T(8,128)(2,1)S(1)}, bf16[768,768]{1,0:T(8,128)(2,1)}, u32[]{:S(2)}) copy-start(bf16[768,768]{1,0:T(8,128)(2,1)} %get-tuple-element.151) | copy-start | bytes 3538948
  369.3 1.5 copy-start.24
  369.3 11.5 %collective-permute-start.28 = (bf16[288,768]{1,0:T(8,128)(2,1)}, bf16[288,768]{1,0:T(8,128)(2,1)S(1)}, u32[]{:S(2)}, u32[]{:S(2)}) collective-permute-start(bf16[288,768]{1,0:T(8,128)(2,1)} %slice.105), channel_id=1, source_target_pairs={{0,2},{1,3},{2,0},{3,1},{4,6},{5,7},{6,4},{7,5},{8,10},{9,11},{10,... | collective-permute-start | bytes 1327112 | tf_op jit(solution)/shard_map/ppermute | solution.py:25
  375.4 5.4 %copy-start.16 = (bf16[768,768]{1,0:T(8,128)(2,1)S(1)}, bf16[768,768]{1,0:T(8,128)(2,1)}, u32[]{:S(2)}) copy-start(bf16[768,768]{1,0:T(8,128)(2,1)} %get-tuple-element.154) | copy-start | bytes 3538948
  384.2 2.3 copy-start.7
  384.3 6.3 %collective-permute-start.30 = (f32[16,96]{1,0:T(8,128)S(1)}, f32[16,96]{1,0:T(8,128)S(1)}, u32[]{:S(2)}, u32[]{:S(2)}) collective-permute-start(f32[16,96]{1,0:T(8,128)S(1)} %pad_maximum_fusion), channel_id=1, source_target_pairs={{0,2},{1,3},{2,0},{3,1},{4,6},{5,7},{6,4},{7,5},{8,10},{9,11},{10,... | collective-permute-start | bytes 18440 | tf_op jit(solution)/shard_map/ppermute | solution.py:25
  385.8 4.7 %collective-permute-start.31 = (f32[16,96]{1,0:T(8,128)S(1)}, f32[16,96]{1,0:T(8,128)S(1)}, u32[]{:S(2)}, u32[]{:S(2)}) collective-permute-start(f32[16,96]{1,0:T(8,128)S(1)} %pad_maximum_fusion), channel_id=1, source_target_pairs={{0,3},{1,2},{2,1},{3,0},{4,7},{5,6},{6,5},{7,4},{8,11},{9,10},{10,... | collective-permute-start | bytes 18440 | tf_op jit(solution)/shard_map/ppermute | solution.py:25
  385.8 4.7 %collective-permute-start.29 = (f32[16,96]{1,0:T(8,128)S(1)}, f32[16,96]{1,0:T(8,128)S(1)}, u32[]{:S(2)}, u32[]{:S(2)}) collective-permute-start(f32[16,96]{1,0:T(8,128)S(1)} %pad_maximum_fusion), channel_id=1, source_target_pairs={{0,1},{1,0},{2,3},{3,2},{4,5},{5,4},{6,7},{7,6},{8,9},{9,8},{10,11... | collective-permute-start | bytes 18440 | tf_op jit(solution)/shard_map/ppermute | solution.py:25
  (4 other events, 3.2 us)
